TPU v7x, 32 devices: a whole 2x2x4 slice. The times are simulated.
32 devices in a mesh: dom: 16 (over z, y, core), col: 2 (over x).
Axes of the slice: x: 2, y: 2, z: 4, core: 2. Of those that a mesh axis runs over, the one named last changes fastest.
Arguments:
- tmat: bfloat16 [65536, 1024], P('dom', 'col'), may hold values from -6 to 6
- stored_mass_blocks: bfloat16 [4096, 128, 128], P('dom'), may hold values from -0.0009765625 to 0.0009765625
- block_index: int32 [4096, 2], P('dom'), may hold values from 0 to 35, as said below
- live_block_count: int32 [16], P('dom'), may hold values from 36 to 256, as said below
- send_rows: int32 [32, 256], P('dom'), may hold values from 0 to 4095, as said below
Outputs:
- reduced: float32 [512, 1024], P('dom', 'col')
Inputs may be any that keep to these rules, and one draw needn't show every extreme that they name: `block_index`: row entries lie in 0 to 31 and column entries in 0 to 35. In each partition's list slot k < 32 is block (k, k), and slot 32 + m for m < 4 has block column 32 + m. `live_block_count`: some partition uses all 256 slots in every draw. `send_rows`: the 256 rows in each list are distinct local row numbers of the sending partition.
All inputs are finite; a program needn't handle non-finite values.
Results may differ from a plain program's by a relative error of at most 0.0029.
Values may be sent and summed in bfloat16 or wider, within the bound.
No kernel may reach another device: no remote copies, remote signals or barrier semaphores. Data moves between devices by JAX's collectives and lax.ppermute only.
A program may use at most 128 MiB of HBM per device.

v0:
```python
import jax
import jax.numpy as jnp
from jax import lax
from jax.sharding import PartitionSpec as P


def passed_along(block, axis, distance):
    devices = range(lax.axis_size(axis))
    route = [(i - distance, i) for i in devices if i - distance in devices]
    return lax.ppermute(block, axis, route)


def broadcast(block, axis, holder):
    block = jnp.where(lax.axis_index(axis) == holder, block, jnp.zeros_like(block))
    return lax.psum(block, axis)


def contract(left, right):
    return lax.dot_general(
        left, right, (((0,), (0,)), ((), ())), preferred_element_type=jnp.float32
    )


def mass_product(panel, stored_mass_blocks, block_index, live_block_count, send_rows):
    rows_dev, width = panel.shape
    bsize = stored_mass_blocks.shape[1]
    nrows_blk = rows_dev // bsize
    slot_number = stored_mass_blocks.shape[0]
    to_lower = jnp.take(panel, send_rows[0], axis=0)
    to_upper = jnp.take(panel, send_rows[1], axis=0)
    from_lower = passed_along(to_upper, "dom", 1)
    from_upper = passed_along(to_lower, "dom", -1)
    extended = jnp.concatenate([panel, from_lower, from_upper], 0).reshape(-1, bsize, width)
    live_flags = (jnp.arange(slot_number) < live_block_count[0]).astype(jnp.float32)
    partition_groups = 4
    partition_group_width = slot_number // partition_groups

    def step(acc, group):
        begin = group * partition_group_width
        blocks = lax.dynamic_slice_in_dim(stored_mass_blocks, begin, partition_group_width, 0)
        columns = lax.dynamic_slice_in_dim(block_index[:, 1], begin, partition_group_width, 0)
        targets = lax.dynamic_slice_in_dim(block_index[:, 0], begin, partition_group_width, 0)
        weights = lax.dynamic_slice_in_dim(live_flags, begin, partition_group_width, 0)
        selected = jnp.take(extended, columns, axis=0)
        prod = jnp.einsum("kab,kbw->kaw", blocks, selected, preferred_element_type=jnp.float32)
        acc = acc.at[targets].add(prod * weights[:, None, None])
        return (acc, None)

    start_acc = jnp.zeros((nrows_blk, bsize, width), jnp.float32)
    summed, _ = lax.scan(step, start_acc, jnp.arange(partition_groups))
    return summed.reshape(rows_dev, width).astype(jnp.bfloat16)


def body(tmat, stored_mass_blocks, block_index, live_block_count, send_rows):
    n_col = lax.axis_size("col")
    n_dom = lax.axis_size("dom")
    panel_width = tmat.shape[1]
    panel = broadcast(tmat, "col", n_col - 1)
    interface_mass_panel = mass_product(
        panel, stored_mass_blocks, block_index, live_block_count, send_rows
    )
    share = panel_width // n_dom
    total = lax.psum(contract(interface_mass_panel, tmat), "dom")
    return lax.dynamic_slice_in_dim(total, lax.axis_index("dom") * share, share, 0)


def solution(mesh):
    return jax.shard_map(
        body,
        mesh=mesh,
        in_specs=(P("dom", "col"), P("dom", None, None), P("dom", None), P("dom"), P("dom", None)),
        out_specs=P("dom", "col"),
        check_vma=False,
    )
```

profile of v0, /device:TPU:0, one launch (start us, length us, event | category | flops | bytes accessed | tf_op | source)
XLA Modules:
  0.0 492.2 jit_solution(12430480679996038683)
XLA Ops:
  6.5 2.2 broadcast_select_fusion
  9.0 112.8 %all-reduce.3.cloned.1.call-done = bf16[4096,512]{1,0:T(8,128)(2,1)} async-done(((bf16[4096,512]{1,0:T(8,128)(2,1)}), bf16[4096,512]{1,0:T(8,128)(2,1)}) %all-reduce.3.cloned.1.call-update) | async-done | bytes 4194320 | tf_op jit(solution)/shard_map/psum | solution.py:15
  121.7 3.9 gather_fusion.1
  125.7 0.1 broadcast_select_fusion.2
  125.8 1.8 collective-permute-start
  127.5 3.9 gather_fusion.2
  131.6 1.3 collective-permute-start.1
  133.6 2.7 collective-permute-done.1
  136.3 4.0 pad_maximum_fusion
  140.3 4.3 broadcast_in_dim.27
  144.6 232.7 %while.10 = (s32[]{:T(128)}, f32[32,128,512]{2,1,0:T(8,128)}, s32[256,2]{0,1:T(2,128)S(1)}, s32[4]{0:T(128)S(1)}, bf16[256,128,128]{2,1,0:T(8,128)(2,1)}, /*inde...) while((s32[]{:T(128)}, f32[32,128,512]{2,1,0:T(8,128)}, ...), condition=%wide.region_3.5_spmd, body=%wide.region_1.0_spmd.sunk | while | flops 1086326400 | bytes 94382912 | solution.py:50
  144.6 0.7 dynamic_slice.38
  146.2 7.9 %gather_fusion = bf16[64,128,512]{2,1,0:T(8,128)(2,1)} fusion(bf16[36,128,512]{2,1,0:T(8,128)(2,1)} %get-tuple-element.142, s32[1024]{0:T(1024)S(1)} %pad_clamp_fusion.4), kind=kCustom, calls=%fused_computation.1.clone.1 | custom fusion | bytes 16777472 | tf_op jit(solution)/shard_map/while/body/eval_jaxpr/jit(_take)/gather | solution.py:44
  154.0 12.2 %convolution_multiply_fusion.2 = f32[64,128,512]{2,1,0:T(8,128)} fusion(f32[64]{0:T(128)S(1)} %dynamic_slice.39, bf16[64,128,512]{2,1,0:T(8,128)(2,1)} %gather_fusion, pred[64]{0:T(512)(128)(4,1)S(1)} %get-tuple-element.114, bf16[256,128,128]{2,1,0:T(8,128)(2,1)} %get-tuple-element.141, s32[]{:T(128)S(6)} %select_n.70), kind=kOutput, calls=%fused_computation.4.clone.1 | convolution fusion | flops 1082130432 | bytes 27263300 | tf_op jit(solution)/shard_map/while/body/eval_jaxpr/kab,kbw->kaw/dot_general | solution.py:45
  166.2 36.7 %scatter_fusion = f32[32,128,512]{2,1,0:T(8,128)} fusion(f32[32,128,512]{2,1,0:T(8,128)} %get-tuple-element.127, s32[64]{0:T(128)S(1)} %fusion.19, f32[64,128,512]{2,1,0:T(8,128)} %convolution_multiply_fusion.2), kind=kCustom, calls=%fused_computation.3.clone.1 | custom fusion | flops 4194304 | bytes 50331904 | tf_op jit(solution)/shard_map/while/body/eval_jaxpr/scatter-add | solution.py:46
  202.9 0.7 dynamic_slice.38
  204.5 7.9 %gather_fusion = bf16[64,128,512]{2,1,0:T(8,128)(2,1)} fusion(bf16[36,128,512]{2,1,0:T(8,128)(2,1)} %get-tuple-element.142, s32[1024]{0:T(1024)S(1)} %pad_clamp_fusion.4), kind=kCustom, calls=%fused_computation.1.clone.1 | custom fusion | bytes 16777472 | tf_op jit(solution)/shard_map/while/body/eval_jaxpr/jit(_take)/gather | solution.py:44
  212.4 12.2 %convolution_multiply_fusion.2 = f32[64,128,512]{2,1,0:T(8,128)} fusion(f32[64]{0:T(128)S(1)} %dynamic_slice.39, bf16[64,128,512]{2,1,0:T(8,128)(2,1)} %gather_fusion, pred[64]{0:T(512)(128)(4,1)S(1)} %get-tuple-element.114, bf16[256,128,128]{2,1,0:T(8,128)(2,1)} %get-tuple-element.141, s32[]{:T(128)S(6)} %select_n.70), kind=kOutput, calls=%fused_computation.4.clone.1 | convolution fusion | flops 1082130432 | bytes 27263300 | tf_op jit(solution)/shard_map/while/body/eval_jaxpr/kab,kbw->kaw/dot_general | solution.py:45
  224.5 36.4 %scatter_fusion = f32[32,128,512]{2,1,0:T(8,128)} fusion(f32[32,128,512]{2,1,0:T(8,128)} %get-tuple-element.127, s32[64]{0:T(128)S(1)} %fusion.19, f32[64,128,512]{2,1,0:T(8,128)} %convolution_multiply_fusion.2), kind=kCustom, calls=%fused_computation.3.clone.1 | custom fusion | flops 4194304 | bytes 50331904 | tf_op jit(solution)/shard_map/while/body/eval_jaxpr/scatter-add | solution.py:46
  261.0 0.7 dynamic_slice.38
  262.6 7.9 %gather_fusion = bf16[64,128,512]{2,1,0:T(8,128)(2,1)} fusion(bf16[36,128,512]{2,1,0:T(8,128)(2,1)} %get-tuple-element.142, s32[1024]{0:T(1024)S(1)} %pad_clamp_fusion.4), kind=kCustom, calls=%fused_computation.1.clone.1 | custom fusion | bytes 16777472 | tf_op jit(solution)/shard_map/while/body/eval_jaxpr/jit(_take)/gather | solution.py:44
  270.4 12.2 %convolution_multiply_fusion.2 = f32[64,128,512]{2,1,0:T(8,128)} fusion(f32[64]{0:T(128)S(1)} %dynamic_slice.39, bf16[64,128,512]{2,1,0:T(8,128)(2,1)} %gather_fusion, pred[64]{0:T(512)(128)(4,1)S(1)} %get-tuple-element.114, bf16[256,128,128]{2,1,0:T(8,128)(2,1)} %get-tuple-element.141, s32[]{:T(128)S(6)} %select_n.70), kind=kOutput, calls=%fused_computation.4.clone.1 | convolution fusion | flops 1082130432 | bytes 27263300 | tf_op jit(solution)/shard_map/while/body/eval_jaxpr/kab,kbw->kaw/dot_general | solution.py:45
  282.6 36.7 %scatter_fusion = f32[32,128,512]{2,1,0:T(8,128)} fusion(f32[32,128,512]{2,1,0:T(8,128)} %get-tuple-element.127, s32[64]{0:T(128)S(1)} %fusion.19, f32[64,128,512]{2,1,0:T(8,128)} %convolution_multiply_fusion.2), kind=kCustom, calls=%fused_computation.3.clone.1 | custom fusion | flops 4194304 | bytes 50331904 | tf_op jit(solution)/shard_map/while/body/eval_jaxpr/scatter-add | solution.py:46
  319.2 0.7 dynamic_slice.38
  320.8 7.9 %gather_fusion = bf16[64,128,512]{2,1,0:T(8,128)(2,1)} fusion(bf16[36,128,512]{2,1,0:T(8,128)(2,1)} %get-tuple-element.142, s32[1024]{0:T(1024)S(1)} %pad_clamp_fusion.4), kind=kCustom, calls=%fused_computation.1.clone.1 | custom fusion | bytes 16777472 | tf_op jit(solution)/shard_map/while/body/eval_jaxpr/jit(_take)/gather | solution.py:44
  328.7 12.2 %convolution_multiply_fusion.2 = f32[64,128,512]{2,1,0:T(8,128)} fusion(f32[64]{0:T(128)S(1)} %dynamic_slice.39, bf16[64,128,512]{2,1,0:T(8,128)(2,1)} %gather_fusion, pred[64]{0:T(512)(128)(4,1)S(1)} %get-tuple-element.114, bf16[256,128,128]{2,1,0:T(8,128)(2,1)} %get-tuple-element.141, s32[]{:T(128)S(6)} %select_n.70), kind=kOutput, calls=%fused_computation.4.clone.1 | convolution fusion | flops 1082130432 | bytes 27263300 | tf_op jit(solution)/shard_map/while/body/eval_jaxpr/kab,kbw->kaw/dot_general | solution.py:45
  340.9 36.4 %scatter_fusion = f32[32,128,512]{2,1,0:T(8,128)} fusion(f32[32,128,512]{2,1,0:T(8,128)} %get-tuple-element.127, s32[64]{0:T(128)S(1)} %fusion.19, f32[64,128,512]{2,1,0:T(8,128)} %convolution_multiply_fusion.2), kind=kCustom, calls=%fused_computation.3.clone.1 | custom fusion | flops 4194304 | bytes 50331904 | tf_op jit(solution)/shard_map/while/body/eval_jaxpr/scatter-add | solution.py:46
  377.3 4.2 convert_element_type.10
  381.5 0.4 copy-done
  381.9 3.4 fusion.9
  385.3 98.6 %all-reduce.5.cloned.1.call-done = f32[512,512]{1,0:T(8,128)} async-done(((f32[512,512]{1,0:T(8,128)}), f32[512,512]{1,0:T(8,128)}) %all-reduce.5.cloned.1.call-update) | async-done | bytes 1048592 | tf_op jit(solution)/shard_map/psum | solution.py:63
  483.9 1.5 constant_dynamic-slice_fusion.2
  (40 shorter events, 1.2 us)
Async XLA Ops:
  6.5 2.3 copy-start.2
  6.5 115.2 %all-reduce.3.cloned.1.call-start = ((), (), s32[]{:S(2)}) async-start(), calls=%async_computation | async-start | bytes 8388608 | tf_op jit(solution)/shard_map/psum | solution.py:15
  8.8 475.1 %all-reduce.5.cloned.1.call-start = ((), (), s32[]{:S(2)}) async-start(), calls=%async_computation.1 | async-start | bytes 2097152 | tf_op jit(solution)/shard_map/psum | solution.py:63
  125.8 7.8 %collective-permute-start = (bf16[256,512]{1,0:T(8,128)(2,1)S(1)}, bf16[256,512]{1,0:T(8,128)(2,1)S(1)}, u32[]{:S(2)}, u32[]{:S(2)}) collective-permute-start(bf16[256,512]{1,0:T(8,128)(2,1)S(1)} %broadcast_select_fusion.2), channel_id=1, source_target_pairs={{0,2},{2,4},{4,6},{6,8},{8,10},{10,12},{12,14},{14,16},{16,18},{18... | collective-permute-start | bytes 786440 | tf_op jit(solution)/shard_map/ppermute | solution.py:10
  131.6 4.7 collective-permute-start.1
  133.5 11.0 %copy-start.1 = (s32[256,2]{0,1:T(2,128)S(1)}, s32[256,2]{0,1:T(2,128)}, u32[]{:S(2)}) copy-start(s32[256,2]{0,1:T(2,128)} %param.11) | copy-start | bytes 6148
  377.3 4.6 copy-start
Sparse Core Ops, SparseCore 0:
  9.8 111.8 all-reduce.2
  385.4 98.4 all-reduce.4
where the time goes:
time: 493 us; the launch traced here: 492 us
  waiting for transfers between devices  214 us (43%)
  other arithmetic  157 us (32%)
  matrix products  52 us (11%)
  local copies, waits for them, and re-layouts  48.5 us (10%)
  between operations  14.2 us (3%)
    scatter-add x4, other arithmetic, step(): acc = acc.at[targets].add(prod * weights[:, None, None])  146 us
    psum x1, waiting for transfers between devices, broadcast(): return lax.psum(block, axis)  113 us
    psum x1, waiting for transfers between devices, body(): total = lax.psum(contract(interface_mass_panel, tmat), 'dom')  98.6 us
    dot_general x4, matrix products, step(): jnp.einsum('kab,kbw->kaw', blocks, selected, preferred_element_type=jnp.f...  48.6 us
    gather x4, local copies, waits for them, and re-layouts, step(): selected = jnp.take(extended, columns, axis=0)  31.5 us
  transfers between devices with their start and end apart: 4, of which 3 were waited for; matrix products, arithmetic and copies ran while one was open for 1% of the time, Pallas kernels for 0%

commit v1 on v0

v1 whole, which is shorter than its diff:
```python
import functools

import jax
import jax.numpy as jnp
from jax import lax
from jax.experimental import pallas as pl
from jax.experimental.pallas import tpu as pltpu
from jax.sharding import PartitionSpec as P

GROUP = 4
UNROLL = 8
CHUNKS = 2


def contract(left, right):
    return lax.dot_general(
        left, right, (((0,), (0,)), ((), ())), preferred_element_type=jnp.float32
    )


def slot_list(block_index, live, nrows_blk, shift):
    slots = block_index.shape[0]
    rows, cols = block_index[:, 0], block_index[:, 1]
    k = jnp.arange(slots)
    alive = k < live
    earlier = (rows[:, None] == rows[None, :]) & alive[None, :] & (k[None, :] < k[:, None])
    rank = jnp.sum(earlier.astype(jnp.int32), 1)
    r = jnp.arange(nrows_blk)
    count = jnp.sum(((rows[None, :] == r[:, None]) & alive[None, :]).astype(jnp.int32), 1)
    groups = (count + GROUP - 1) // GROUP
    bounds = jnp.arange(nrows_blk + 1)
    first = jnp.sum(jnp.where(r[None, :] < bounds[:, None], groups[None, :], 0), 1)
    begin = jnp.sum(jnp.where(rows[:, None] == r[None, :], first[None, :nrows_blk], 0), 1)
    place = begin * GROUP + rank
    total = slots // GROUP + nrows_blk
    g = jnp.arange(total)
    owner_row = jnp.sum((first[None, 1:nrows_blk] <= g[:, None]).astype(jnp.int32), 1)
    hit = (place[None, :] == jnp.arange(total * GROUP)[:, None]) & alive[None, :]
    value = ((k + 1) << shift) + cols
    return first, owner_row, jnp.sum(jnp.where(hit, value[None, :], 0), 1)


def spmm_kernel(row0, nrows, col0, width, shift, first, owner_row, entries, blocks, panel, low, up, after, out, ext, acc, sem):
    bsize = blocks.shape[1]
    rows_dev, halo = panel.shape[0], low.shape[0]
    cols = pl.ds(col0, width)
    copies = [
        pltpu.make_async_copy(panel.at[:, cols], ext.at[pl.ds(0, rows_dev)], sem.at[0]),
        pltpu.make_async_copy(low.at[:, cols], ext.at[pl.ds(rows_dev, halo)], sem.at[1]),
        pltpu.make_async_copy(up.at[:, cols], ext.at[pl.ds(rows_dev + halo, halo)], sem.at[2]),
    ]
    for copy in copies:
        copy.start()
    acc[...] = jnp.zeros_like(acc)
    for copy in copies:
        copy.wait()
    begin, end = first[row0], first[row0 + nrows]

    @pl.loop(0, (end - begin + UNROLL - 1) // UNROLL)
    def _(step):
        rows, prods = [], []
        for u in range(UNROLL):
            g = begin + step * UNROLL + u
            inside = g < end
            g = jnp.minimum(g, end - 1)
            rows.append(jnp.where(inside, owner_row[g] - row0, 0))
            left, right = [], []
            for j in range(GROUP):
                entry = jnp.where(inside, entries[g * GROUP + j], 0)
                block = blocks[jnp.maximum((entry >> shift) - 1, 0)]
                column = entry & ((1 << shift) - 1)
                left.append(jnp.where(entry > 0, block, jnp.zeros_like(block)))
                right.append(ext[pl.ds(pl.multiple_of(column * bsize, bsize), bsize), :])
            prods.append(
                jnp.dot(jnp.concatenate(left, 1), jnp.concatenate(right, 0), preferred_element_type=jnp.float32)
            )
        for row, prod in zip(rows, prods):
            acc[pl.ds(pl.multiple_of(row * bsize, bsize), bsize), :] += prod

    @pl.loop(0, nrows)
    def _(i):
        rows = pl.ds(pl.multiple_of(i * bsize, bsize), bsize)
        out[rows, :] = acc[rows, :].astype(out.dtype)


def spmm(lists, blocks, panel, low, up, after, shift, row0, nrows, col0, width):
    nblk, bsize, _ = blocks.shape
    ext_rows = panel.shape[0] + 2 * low.shape[0]
    near = pl.BlockSpec(memory_space=pltpu.VMEM)
    scalar = pl.BlockSpec(memory_space=pltpu.SMEM)
    blocks, panel, low, up = (pltpu.with_memory_space_constraint(a, pltpu.VMEM) for a in (blocks, panel, low, up))
    return pl.pallas_call(
        functools.partial(spmm_kernel, row0, nrows, col0, width, shift),
        out_shape=jax.ShapeDtypeStruct((nrows * bsize, width), jnp.bfloat16),
        in_specs=[scalar] * 3 + [near] * 4 + [pl.BlockSpec(memory_space=pl.ANY)],
        out_specs=near,
        scratch_shapes=[
            pltpu.VMEM((ext_rows, width), panel.dtype),
            pltpu.VMEM((nrows * bsize, width), jnp.float32),
            pltpu.SemaphoreType.DMA((3,)),
        ],
        compiler_params=pltpu.CompilerParams(vmem_limit_bytes=32 << 20),
        cost_estimate=pl.CostEstimate(
            flops=2 * nrows * 8 * bsize * bsize * width,
            bytes_accessed=2 * (ext_rows * width + nrows * bsize * width),
            transcendentals=0,
        ),
    )(*lists, blocks, panel, low, up, after)


def scatter(x):
    n_dom = lax.axis_size("dom")
    bits = n_dom.bit_length() - 1
    x = x.reshape((2,) * bits + x.shape[1:])
    for b in range(bits):
        bit = 1 << b
        mine = (lax.axis_index("dom") // bit) % 2
        keep = lax.dynamic_index_in_dim(x, mine, bits - 1 - b, keepdims=False)
        send = lax.dynamic_index_in_dim(x, 1 - mine, bits - 1 - b, keepdims=False)
        x = keep + lax.ppermute(send, "dom", [(i, i ^ bit) for i in range(n_dom)])
    return x


def halo_rows(panel, send_rows, order, owner):
    n_dom, n_col = lax.axis_size("dom"), lax.axis_size("col")
    sides, halo = send_rows.shape
    picks = send_rows.reshape(sides * halo, 1) == jnp.arange(panel.shape[0])[None, :]
    rows = jnp.dot(picks.astype(panel.dtype), panel, preferred_element_type=jnp.float32).astype(panel.dtype)
    if order is not None:
        rows = jnp.dot(rows, order, preferred_element_type=jnp.float32).astype(panel.dtype)
    up = [(i * n_col + owner, (i + 1) * n_col + owner) for i in range(n_dom - 1)]
    from_lower = lax.ppermute(rows[halo:], ("dom", "col"), up)
    from_upper = lax.ppermute(rows[:halo], ("dom", "col"), [(b, a) for a, b in up])
    return from_lower, from_upper


def body(tmat, stored_mass_blocks, block_index, live_block_count, send_rows):
    n_col, n_dom = lax.axis_size("col"), lax.axis_size("dom")
    owner = n_col - 1
    col = lax.axis_index("col")
    rows_dev, width = tmat.shape
    bsize = stored_mass_blocks.shape[1]
    nrows_blk = rows_dev // bsize
    share = width // n_dom
    shift = (nrows_blk + 2 * send_rows.shape[1] // bsize).bit_length()
    live = jnp.where(col == owner, live_block_count[0], 0)
    lists = slot_list(block_index, live, nrows_blk, shift)

    if n_col != 2 or n_dom & (n_dom - 1) or share % CHUNKS:
        low, up = halo_rows(tmat, send_rows, None, owner)
        mass = spmm(lists, stored_mass_blocks, tmat, low, up, low, shift, 0, nrows_blk, 0, width)
        total = lax.psum(contract(lax.psum(mass, "col"), tmat), "dom")
        return lax.dynamic_slice_in_dim(total, lax.axis_index("dom") * share, share, 0)

    sub, part = share // CHUNKS, width // CHUNKS
    new = jnp.arange(width)
    old = (new // sub % n_dom) * share + (new // part) * sub + new % sub
    order = (jnp.arange(width)[:, None] == old[None, :]).astype(tmat.dtype)

    na = (nrows_blk * 7) // 16
    cut = rows_dev - na * bsize
    early = cut - na * bsize
    t_b, t_a = tmat[:cut], tmat[cut:]
    ahead = [lax.ppermute(tmat[:early, h * part : (h + 1) * part], "col", [(0, 1)]) for h in range(CHUNKS)]

    low, up = halo_rows(tmat, send_rows, order, owner)
    panel = jnp.dot(tmat, order, preferred_element_type=jnp.float32).astype(tmat.dtype)

    def mass(after, row0, nrows, col0, cols):
        return spmm(lists, stored_mass_blocks, panel, low, up, after, shift, row0, nrows, col0, cols)

    mass_a, got = [], []
    for h in range(CHUNKS):
        mass_a.append(mass(ahead[h], nrows_blk - na, na, h * part, part))
        piece = jnp.where(col == owner, mass_a[h], tmat[early:cut, h * part : (h + 1) * part])
        got.append(lax.ppermute(piece, "col", [(0, 1), (1, 0)]))
    mass_b = mass(low, 0, nrows_blk - na, 0, width)

    own = jnp.concatenate([contract(m, t_a) for m in mass_a], 0) + contract(mass_b, t_b)
    own = own.reshape(CHUNKS, n_dom, sub, width).transpose(1, 0, 2, 3).reshape(n_dom, share, width)

    def in_panel_column(ahead, got):
        x = contract(mass_b, jnp.concatenate([ahead, got], 0))
        return x.reshape(CHUNKS, n_dom, sub, part).transpose(1, 2, 0, 3).reshape(n_dom, sub, width)

    def in_other_column(ahead, got):
        return contract(got, t_a).reshape(n_dom, sub, width)

    sums, back = [], []
    for h in range(CHUNKS):
        x = lax.cond(col == owner, in_panel_column, in_other_column, ahead[h], got[h])
        if h == 0:
            x = jnp.concatenate([x, own], 1)
        x = scatter(x)
        if h == 0:
            own = x[sub:]
        sums.append(x[:sub])
        back.append(lax.ppermute(x[:sub], "col", [(1, 0)]))
    back = jnp.stack(back).reshape(CHUNKS, sub, CHUNKS, part).transpose(2, 1, 0, 3)
    other = jnp.concatenate(sums, 0) + back.reshape(share, width)
    return jnp.where(col == owner, own, other)


def solution(mesh):
    return jax.shard_map(
        body,
        mesh=mesh,
        in_specs=(P("dom", "col"), P("dom", None, None), P("dom", None), P("dom"), P("dom", None)),
        out_specs=P("dom", "col"),
        check_vma=False,
    )
```

time: 493 us -> 123 us (0.25)
  waiting for transfers between devices: 214 us -> 51.4 us
  other arithmetic: 157 us -> 5.09 us
  local copies, waits for them, and re-layouts: 48.5 us -> 12.3 us
  matrix products: 52 us -> 17.4 us
  starting transfers between devices: 3.09 us -> 31.5 us
  between operations: 14.2 us -> 1.06 us
    psum x2 -> x0, waiting for transfers between devices: 211 us -> none  [the longest x1 113 us: broadcast(): return lax.psum(block, axis)]
    scatter-add x4 -> x0, other arithmetic: 146 us -> none  [step(): acc = acc.at[targets].add(prod * weights[:, None, None])]
    ppermute x2 -> x16, waiting for transfers between devices: 2.7 us -> 51.4 us  [the longest x2 31.6 us: body(): got.append(lax.ppermute(piece, 'col', [(0, 1), (1, 0)]))]
    gather x6 -> x0, local copies, waits for them, and re-layouts: 39.3 us -> none  [the longest x4 31.5 us: step(): selected = jnp.take(extended, columns, axis=0)]
    dot_general x4 -> x2, matrix products: 48.6 us -> 11.4 us  [the longest x1 6.53 us: body(): jnp.dot(tmat, order, preferred_element_type=jnp.float32).astype(tmat.dtype)]
    ppermute x2 -> x16, starting transfers between devices: 3.05 us -> 31.5 us  [the longest x8 16.3 us: scatter(): x = keep + lax.ppermute(send, 'dom', [(i, i ^ bit) for i in range(n_dom)])]
    unnamed x6 -> x12, local copies, waits for them, and re-layouts: 0.41 us -> 7.4 us
  transfers between devices with their start and end apart: 4 -> 16, of which waited for: 3 -> 9; matrix products, arithmetic and copies ran while one was open for 1% -> 17% of each run, Pallas kernels for 0% -> 2%
where the time goes in v1:
time: 123 us
  waiting for transfers between devices  51.4 us (42%)
  starting transfers between devices  31.5 us (26%)
  matrix products  17.4 us (14%)
  local copies, waits for them, and re-layouts  12.3 us (10%)
  other arithmetic  5.09 us (4%)
  Pallas kernels  3.61 us (3%)
    ppermute x2, waiting for transfers between devices, body(): got.append(lax.ppermute(piece, 'col', [(0, 1), (1, 0)]))  31.6 us
    ppermute x8, starting transfers between devices, scatter(): x = keep + lax.ppermute(send, 'dom', [(i, i ^ bit) for i in range(n_dom)])  16.3 us
    ppermute x8, waiting for transfers between devices, scatter(): x = keep + lax.ppermute(send, 'dom', [(i, i ^ bit) for i in range(n_dom)])  13.4 us
    ppermute x2, starting transfers between devices, body(): lax.ppermute(tmat[:early, h * part:(h + 1) * part], 'col', [(0, 1)])  9.24 us
    unnamed x12, local copies, waits for them, and re-layouts  7.4 us
    dot_general x1, matrix products, body(): jnp.dot(tmat, order, preferred_element_type=jnp.float32).astype(tmat.dtype)  6.53 us
    ppermute x2, waiting for transfers between devices, body(): back.append(lax.ppermute(x[:sub], 'col', [(1, 0)]))  6.33 us
    dot_general x5, matrix products, contract(): lax.dot_general(left, right, (((0,), (0,)), ((), ())), preferred_element_...  5.98 us
  transfers between devices with their start and end apart: 16, of which 9 were waited for; matrix products, arithmetic and copies ran while one was open for 17% of the time, Pallas kernels for 2%

profile of v1, /device:TPU:0, one launch (start us, length us, event | category | flops | bytes accessed | tf_op | source)
XLA Modules:
  0.0 122.5 jit_solution(6200533429799787283)
XLA Ops:
  0.7 4.9 %convolution_convert_fusion.1 = bf16[512,512]{1,0:T(8,128)(2,1)S(1)} fusion(bf16[4096,512]{1,0:T(8,128)(2,1)} %param.9, s32[512]{0:T(512)S(1)} %bitcast.91, s32[512]{0:T(512)S(1)} %fusion.31), kind=kOutput, calls=%fused_computation.21 | convolution fusion | flops 2418802688 | bytes 4722688 | tf_op jit(solution)/shard_map/dot_general | solution.py:130
  7.0 1.8 %fusion.41 = (bf16[512,256]{1,0:T(8,128)(2,1)S(1)}, bf16[512,256]{1,0:T(8,128)(2,1)}) fusion(bf16[4096,512]{1,0:T(8,128)(2,1)} %param.9), kind=kLoop, calls=%fused_computation.102 | loop fusion | bytes 1048576 | tf_op jit(solution)/shard_map/slice | solution.py:164
  8.8 7.2 %collective-permute-start.4 = (bf16[512,256]{1,0:T(8,128)(2,1)}, bf16[512,256]{1,0:T(8,128)(2,1)}, u32[]{:S(2)}, u32[]{:S(2)}) collective-permute-start(bf16[512,256]{1,0:T(8,128)(2,1)} %get-tuple-element.46), channel_id=1, source_target_pairs={{0,1},{2,3},{4,5},{6,7},{8,9},{10,11},{12,13},{14,15},{16,17},{18,... | collective-permute-start | bytes 786440 | tf_op jit(solution)/shard_map/ppermute | solution.py:164
  16.0 2.0 %collective-permute-start.2 = (bf16[512,256]{1,0:T(8,128)(2,1)S(1)}, bf16[512,256]{1,0:T(8,128)(2,1)}, u32[]{:S(2)}, u32[]{:S(2)}) collective-permute-start(bf16[512,256]{1,0:T(8,128)(2,1)S(1)} %get-tuple-element.45), channel_id=1, source_target_pairs={{0,1},{2,3},{4,5},{6,7},{8,9},{10,11},{12,13},{14,15},{16,17},{18,... | collective-permute-start | bytes 786440 | tf_op jit(solution)/shard_map/ppermute | solution.py:164
  19.0 6.5 %fusion.9.panel = bf16[4096,512]{1,0:T(8,128)(2,1)} fusion(bf16[4096,512]{1,0:T(8,128)(2,1)} %param.9, s32[512]{0:T(512)S(1)} %fusion.31), kind=kOutput, calls=%fused_computation.13 | convolution fusion | flops 2149842944 | bytes 8390656 | tf_op jit(solution)/shard_map/dot_general | solution.py:167
  25.8 1.6 %slice.51 = bf16[1792,512]{1,0:T(8,128)(2,1)S(1)} slice(bf16[4096,512]{1,0:T(8,128)(2,1)} %param.9), slice={[2304:4096], [0:512]} | slice | bytes 3670016 | tf_op jit(solution)/shard_map/slice | solution.py:163
  27.7 3.4 %copy-done = bf16[256,128,128]{2,1,0:T(8,128)(2,1)S(1)} copy-done((bf16[256,128,128]{2,1,0:T(8,128)(2,1)S(1)}, bf16[256,128,128]{2,1,0:T(8,128)(2,1)}, u32[]{:S(2)}) %copy-start) | copy-done | bytes 8388632
  31.1 2.2 %copy-done.1 = bf16[4096,512]{1,0:T(8,128)(2,1)S(1)} copy-done((bf16[4096,512]{1,0:T(8,128)(2,1)S(1)}, bf16[4096,512]{1,0:T(8,128)(2,1)}, u32[]{:S(2)}) %copy-start.1) | copy-done | bytes 4194328
  37.2 1.2 slice_select_fusion
  38.4 2.0 %collective-permute-start.9 = (bf16[1792,256]{1,0:T(8,128)(2,1)}, bf16[1792,256]{1,0:T(8,128)(2,1)}, u32[]{:S(2)}, u32[]{:S(2)}) collective-permute-start(bf16[1792,256]{1,0:T(8,128)(2,1)} %get-tuple-element.43), channel_id=1, source_target_pairs={{0,1},{1,0},{2,3},{3,2},{4,5},{5,4},{6,7},{7,6},{8,9},{9,8},{10,11... | collective-permute-start | bytes 2752520 | tf_op jit(solution)/shard_map/ppermute | solution.py:176
  41.1 1.5 %shard_map.56 = bf16[2304,512]{1,0:T(8,128)(2,1)S(1)} custom-call(s32[33]{0:T(128)S(1)} %select_reduce_fusion.2.first, s32[96]{0:T(128)S(1)} %convert_reduce_fusion.2.owner_row, s32[384]{0:T(512)S(1)} %select_reduce_fusion.entries, bf16[256,128,128]{2,1,0:T(8,128)(2,1)S(1)} %copy-done, bf16[4096,512]{1,0:T(8,128)(2,1)S(1)} %copy-done.1, ...), custom_call_target="tpu_custom_call" | custom-call | flops 2415919104 | bytes 7077888 | tf_op jit(solution)/shard_map/pallas_call | solution.py:92
  42.6 1.4 %maximum_add_fusion = f32[512,512]{1,0:T(8,128)S(1)} fusion(f32[256,512]{1,0:T(8,128)S(1)} %fusion.37, f32[256,512]{1,0:T(8,128)S(1)} %fusion.39, bf16[2304,512]{1,0:T(8,128)(2,1)S(1)} %shard_map.56, bf16[4096,512]{1,0:T(8,128)(2,1)S(1)} %copy-done.2), kind=kOutput, calls=%fused_computation.23 | convolution fusion | flops 1208483840 | bytes 6815744 | tf_op jit(solution)/shard_map/dot_general | solution.py:16
  44.1 16.3 %collective-permute-done.3 = bf16[1792,256]{1,0:T(8,128)(2,1)S(1)} collective-permute-done((bf16[1792,256]{1,0:T(8,128)(2,1)S(1)}, bf16[1792,256]{1,0:T(8,128)(2,1)S(1)}, u32[]{:S(2)}, u32[]{:S(2)}) %collective-permute-start.3) | collective-permute-done | bytes 917536 | tf_op jit(solution)/shard_map/ppermute | solution.py:176
  62.2 2.6 %collective-permute-start.5 = (f32[2,2,2,48,512]{4,3,2,1,0:T(8,128)}, f32[2,2,2,48,512]{4,3,2,1,0:T(8,128)}, u32[]{:S(2)}, u32[]{:S(2)}) collective-permute-start(f32[2,2,2,48,512]{4,3,2,1,0:T(8,128)} %fusion.15), channel_id=1, source_target_pairs={{0,2},{2,0},{4,6},{6,4},{8,10},{10,8},{12,14},{14,12},{16,18},{18,... | collective-permute-start | bytes 2359304 | tf_op jit(solution)/shard_map/ppermute | solution.py:120
  64.8 15.3 %collective-permute-done.9 = bf16[1792,256]{1,0:T(8,128)(2,1)} collective-permute-done((bf16[1792,256]{1,0:T(8,128)(2,1)}, bf16[1792,256]{1,0:T(8,128)(2,1)}, u32[]{:S(2)}, u32[]{:S(2)}) %collective-permute-start.9) | collective-permute-done | bytes 917536 | tf_op jit(solution)/shard_map/ppermute | solution.py:176
  80.2 2.6 %conditional.3 = (f32[2,2,2,2,16,512]{5,4,3,2,1,0:T(8,128)}) conditional(s32[]{:T(128)} %convert_element_type.26, (bf16[1792,256]{1,0:T(8,128)(2,1)}, bf16[1792,512]{1,0:T(8,128)(2,1)S(1)}) %tuple.23, (bf16[512,256]{1,0:T(8,128)(2,1)}, bf16[1792,256]{1,0:T(8,128)(2,1)}, bf16[2304,512]{1,0:T(8,128)(2,1)}) %tuple.35), branch_computations={%region_8.9_spmd, %region_9.10_spmd} | conditional | flops 606339072 | bytes 7208968 | solution.py:191
  80.2 2.6 %fusion.45 = f32[256,512]{1,0:T(8,128)} fusion(bf16[1792,256]{1,0:T(8,128)(2,1)} %get-tuple-element.38, bf16[1792,512]{1,0:T(8,128)(2,1)S(1)} %get-tuple-element.39), kind=kOutput, calls=%fused_computation.106 | convolution fusion | flops 469762048 | bytes 3276800 | tf_op jit(solution)/shard_map/cond/branch_0_fun/dot_general | solution.py:16
  85.0 1.2 collective-permute-done.10
  86.2 3.3 %collective-permute-start.11 = (f32[2,2,16,512]{3,2,1,0:T(8,128)S(1)}, f32[2,2,16,512]{3,2,1,0:T(8,128)S(1)}, u32[]{:S(2)}, u32[]{:S(2)}) collective-permute-start(f32[2,2,16,512]{3,2,1,0:T(8,128)S(1)} %dynamic-slice_bitcast_fusion.2), channel_id=1, source_target_pairs={{0,4},{2,6},{4,0},{6,2},{8,12},{10,14},{12,8},{14,10},{16,20},{18,... | collective-permute-start | bytes 393224 | tf_op jit(solution)/shard_map/ppermute | solution.py:120
  89.5 1.3 %fusion.18 = f32[2,2,2,48,512]{4,3,2,1,0:T(8,128)S(1)} fusion(f32[2,2,2,48,512]{4,3,2,1,0:T(8,128)} %collective-permute-done.5, s32[]{:T(128)S(6)} %select_n.182, f32[2,2,2,2,32,512]{5,4,3,2,1,0:T(8,128)S(1)} %bitcast.77, f32[2,2,2,2,16,512]{5,4,3,2,1,0:T(8,128)S(1)} %get-tuple-element.55), kind=kLoop, calls=%fused_computation.31 | loop fusion | flops 393216 | bytes 3145732 | tf_op jit(solution)/shard_map/add | solution.py:120
  91.0 2.4 %collective-permute-done.11 = f32[2,2,16,512]{3,2,1,0:T(8,128)S(1)} collective-permute-done((f32[2,2,16,512]{3,2,1,0:T(8,128)S(1)}, f32[2,2,16,512]{3,2,1,0:T(8,128)S(1)}, u32[]{:S(2)}, u32[]{:S(2)}) %collective-permute-start.11) | collective-permute-done | bytes 131104 | tf_op jit(solution)/shard_map/ppermute | solution.py:120
  93.4 1.9 %collective-permute-start.12 = (f32[2,16,512]{2,1,0:T(8,128)S(1)}, f32[2,16,512]{2,1,0:T(8,128)S(1)}, u32[]{:S(2)}, u32[]{:S(2)}) collective-permute-start(f32[2,16,512]{2,1,0:T(8,128)S(1)} %dynamic-slice_bitcast_fusion.4), channel_id=1, source_target_pairs={{0,8},{2,10},{4,12},{6,14},{8,0},{10,2},{12,4},{14,6},{16,24},{18,... | collective-permute-start | bytes 196616 | tf_op jit(solution)/shard_map/ppermute | solution.py:120
  95.3 6.4 %collective-permute-done.6 = f32[2,2,48,512]{3,2,1,0:T(8,128)S(1)} collective-permute-done((f32[2,2,48,512]{3,2,1,0:T(8,128)S(1)}, f32[2,2,48,512]{3,2,1,0:T(8,128)S(1)}, u32[]{:S(2)}, u32[]{:S(2)}) %collective-permute-start.6) | collective-permute-done | bytes 393248 | tf_op jit(solution)/shard_map/ppermute | solution.py:120
  101.9 1.8 %collective-permute-start.7 = (f32[2,48,512]{2,1,0:T(8,128)S(1)}, f32[2,48,512]{2,1,0:T(8,128)S(1)}, u32[]{:S(2)}, u32[]{:S(2)}) collective-permute-start(f32[2,48,512]{2,1,0:T(8,128)S(1)} %dynamic-slice_bitcast_fusion.1), channel_id=1, source_target_pairs={{0,8},{2,10},{4,12},{6,14},{8,0},{10,2},{12,4},{14,6},{16,24},{18,... | collective-permute-start | bytes 589832 | tf_op jit(solution)/shard_map/ppermute | solution.py:120
  103.7 2.6 %collective-permute-start.13 = (f32[16,512]{1,0:T(8,128)S(1)}, f32[16,512]{1,0:T(8,128)S(1)}, u32[]{:S(2)}, u32[]{:S(2)}) collective-permute-start(f32[16,512]{1,0:T(8,128)S(1)} %dynamic-slice_bitcast_fusion.5), channel_id=1, source_target_pairs={{0,16},{2,18},{4,20},{6,22},{8,24},{10,26},{12,28},{14,30},{16,0},... | collective-permute-start | bytes 98312 | tf_op jit(solution)/shard_map/ppermute | solution.py:120
  106.4 1.9 %collective-permute-done.7 = f32[2,48,512]{2,1,0:T(8,128)S(1)} collective-permute-done((f32[2,48,512]{2,1,0:T(8,128)S(1)}, f32[2,48,512]{2,1,0:T(8,128)S(1)}, u32[]{:S(2)}, u32[]{:S(2)}) %collective-permute-start.7) | collective-permute-done | bytes 196640 | tf_op jit(solution)/shard_map/ppermute | solution.py:120
  108.3 2.8 %collective-permute-start.8 = (f32[48,512]{1,0:T(8,128)S(1)}, f32[48,512]{1,0:T(8,128)S(1)}, u32[]{:S(2)}, u32[]{:S(2)}) collective-permute-start(f32[48,512]{1,0:T(8,128)S(1)} %dynamic-slice_bitcast_fusion.3), channel_id=1, source_target_pairs={{0,16},{2,18},{4,20},{6,22},{8,24},{10,26},{12,28},{14,30},{16,0},... | collective-permute-start | bytes 294920 | tf_op jit(solution)/shard_map/ppermute | solution.py:120
  111.2 1.3 %collective-permute-start.15 = (f32[16,512]{1,0:T(8,128)S(1)}, f32[16,512]{1,0:T(8,128)S(1)}, u32[]{:S(2)}, u32[]{:S(2)}) collective-permute-start(f32[16,512]{1,0:T(8,128)S(1)} %bitcast_add_fusion.6), channel_id=1, source_target_pairs={{1,0},{3,2},{5,4},{7,6},{9,8},{11,10},{13,12},{15,14},{17,16},{19,... | collective-permute-start | bytes 98312 | tf_op jit(solution)/shard_map/ppermute | solution.py:198
  112.5 1.5 %collective-permute-done.8 = f32[48,512]{1,0:T(8,128)S(1)} collective-permute-done((f32[48,512]{1,0:T(8,128)S(1)}, f32[48,512]{1,0:T(8,128)S(1)}, u32[]{:S(2)}, u32[]{:S(2)}) %collective-permute-start.8) | collective-permute-done | bytes 98336 | tf_op jit(solution)/shard_map/ppermute | solution.py:120
  114.0 1.3 %collective-permute-start.14 = (f32[16,512]{1,0:T(8,128)S(1)}, f32[16,512]{1,0:T(8,128)S(1)}, u32[]{:S(2)}, u32[]{:S(2)}) collective-permute-start(f32[16,512]{1,0:T(8,128)S(1)} %slice.60), channel_id=1, source_target_pairs={{1,0},{3,2},{5,4},{7,6},{9,8},{11,10},{13,12},{15,14},{17,16},{19,... | collective-permute-start | bytes 98312 | tf_op jit(solution)/shard_map/ppermute | solution.py:198
  115.3 2.1 %collective-permute-done.15 = f32[16,512]{1,0:T(8,128)S(1)} collective-permute-done((f32[16,512]{1,0:T(8,128)S(1)}, f32[16,512]{1,0:T(8,128)S(1)}, u32[]{:S(2)}, u32[]{:S(2)}) %collective-permute-start.15) | collective-permute-done | bytes 32800 | tf_op jit(solution)/shard_map/ppermute | solution.py:198
  117.5 4.2 %collective-permute-done.14 = f32[16,512]{1,0:T(8,128)S(1)} collective-permute-done((f32[16,512]{1,0:T(8,128)S(1)}, f32[16,512]{1,0:T(8,128)S(1)}, u32[]{:S(2)}, u32[]{:S(2)}) %collective-permute-start.14) | collective-permute-done | bytes 32800 | tf_op jit(solution)/shard_map/ppermute | solution.py:198
  (65 shorter events, 13.4 us)
Async XLA Ops:
  0.7 17.3 %copy-start.4 = (s32[256,2]{0,1:T(2,128)S(1)}, s32[256,2]{0,1:T(2,128)}, u32[]{:S(2)}) copy-start(s32[256,2]{0,1:T(2,128)} %param.11) | copy-start | bytes 6148
  5.6 22.1 %collective-permute-start = (bf16[256,512]{1,0:T(8,128)(2,1)S(1)}, bf16[256,512]{1,0:T(8,128)(2,1)S(1)}, u32[]{:S(2)}, u32[]{:S(2)}) collective-permute-start(bf16[256,512]{1,0:T(8,128)(2,1)S(1)} %get-tuple-element.50), channel_id=1, source_target_pairs={{1,3},{3,5},{5,7},{7,9},{9,11},{11,13},{13,15},{15,17},{17,19},{19... | collective-permute-start | bytes 786440 | tf_op jit(solution)/shard_map/ppermute | solution.py:132
  6.3 21.4 %collective-permute-start.1 = (bf16[256,512]{1,0:T(8,128)(2,1)S(1)}, bf16[256,512]{1,0:T(8,128)(2,1)S(1)}, u32[]{:S(2)}, u32[]{:S(2)}) collective-permute-start(bf16[256,512]{1,0:T(8,128)(2,1)S(1)} %get-tuple-element.49), channel_id=1, source_target_pairs={{3,1},{5,3},{7,5},{9,7},{11,9},{13,11},{15,13},{17,15},{19,17},{21... | collective-permute-start | bytes 786440 | tf_op jit(solution)/shard_map/ppermute | solution.py:133
  8.8 18.9 %collective-permute-start.4 = (bf16[512,256]{1,0:T(8,128)(2,1)}, bf16[512,256]{1,0:T(8,128)(2,1)}, u32[]{:S(2)}, u32[]{:S(2)}) collective-permute-start(bf16[512,256]{1,0:T(8,128)(2,1)} %get-tuple-element.46), channel_id=1, source_target_pairs={{0,1},{2,3},{4,5},{6,7},{8,9},{10,11},{12,13},{14,15},{16,17},{18,... | collective-permute-start | bytes 786440 | tf_op jit(solution)/shard_map/ppermute | solution.py:164
  16.0 20.1 %collective-permute-start.2 = (bf16[512,256]{1,0:T(8,128)(2,1)S(1)}, bf16[512,256]{1,0:T(8,128)(2,1)}, u32[]{:S(2)}, u32[]{:S(2)}) collective-permute-start(bf16[512,256]{1,0:T(8,128)(2,1)S(1)} %get-tuple-element.45), channel_id=1, source_target_pairs={{0,1},{2,3},{4,5},{6,7},{8,9},{10,11},{12,13},{14,15},{16,17},{18,... | collective-permute-start | bytes 786440 | tf_op jit(solution)/shard_map/ppermute | solution.py:164
  27.7 3.4 %copy-start = (bf16[256,128,128]{2,1,0:T(8,128)(2,1)S(1)}, bf16[256,128,128]{2,1,0:T(8,128)(2,1)}, u32[]{:S(2)}) copy-start(bf16[256,128,128]{2,1,0:T(8,128)(2,1)} %blocks.5) | copy-start | bytes 25165828
  31.1 2.2 %copy-start.1 = (bf16[4096,512]{1,0:T(8,128)(2,1)S(1)}, bf16[4096,512]{1,0:T(8,128)(2,1)}, u32[]{:S(2)}) copy-start(bf16[4096,512]{1,0:T(8,128)(2,1)} %fusion.9.panel) | copy-start | bytes 12582916
  33.3 2.2 %copy-start.2 = (bf16[4096,512]{1,0:T(8,128)(2,1)S(1)}, bf16[4096,512]{1,0:T(8,128)(2,1)}, u32[]{:S(2)}) copy-start(bf16[4096,512]{1,0:T(8,128)(2,1)} %param.9) | copy-start | bytes 12582916
  38.4 22.0 %collective-permute-start.3 = (bf16[1792,256]{1,0:T(8,128)(2,1)S(1)}, bf16[1792,256]{1,0:T(8,128)(2,1)S(1)}, u32[]{:S(2)}, u32[]{:S(2)}) collective-permute-start(bf16[1792,256]{1,0:T(8,128)(2,1)S(1)} %get-tuple-element.44), channel_id=1, source_target_pairs={{0,1},{1,0},{2,3},{3,2},{4,5},{5,4},{6,7},{7,6},{8,9},{9,8},{10,11... | collective-permute-start | bytes 2752520 | tf_op jit(solution)/shard_map/ppermute | solution.py:176
  38.4 41.8 %collective-permute-start.9 = (bf16[1792,256]{1,0:T(8,128)(2,1)}, bf16[1792,256]{1,0:T(8,128)(2,1)}, u32[]{:S(2)}, u32[]{:S(2)}) collective-permute-start(bf16[1792,256]{1,0:T(8,128)(2,1)} %get-tuple-element.43), channel_id=1, source_target_pairs={{0,1},{1,0},{2,3},{3,2},{4,5},{5,4},{6,7},{7,6},{8,9},{9,8},{10,11... | collective-permute-start | bytes 2752520 | tf_op jit(solution)/shard_map/ppermute | solution.py:176
  42.6 17.8 %copy-start.3 = (bf16[2304,512]{1,0:T(8,128)(2,1)}, bf16[2304,512]{1,0:T(8,128)(2,1)S(1)}, u32[]{:S(2)}) copy-start(bf16[2304,512]{1,0:T(8,128)(2,1)S(1)} %shard_map.56) | copy-start | bytes 7077892
  62.2 27.3 %collective-permute-start.5 = (f32[2,2,2,48,512]{4,3,2,1,0:T(8,128)}, f32[2,2,2,48,512]{4,3,2,1,0:T(8,128)}, u32[]{:S(2)}, u32[]{:S(2)}) collective-permute-start(f32[2,2,2,48,512]{4,3,2,1,0:T(8,128)} %fusion.15), channel_id=1, source_target_pairs={{0,2},{2,0},{4,6},{6,4},{8,10},{10,8},{12,14},{14,12},{16,18},{18,... | collective-permute-start | bytes 2359304 | tf_op jit(solution)/shard_map/ppermute | solution.py:120
  83.9 2.2 %collective-permute-start.10 = (f32[2,2,2,16,512]{4,3,1,0,2:T(8,128)S(1)}, f32[2,2,2,16,512]{4,3,1,0,2:T(8,128)S(1)}, u32[]{:S(2)}, u32[]{:S(2)}) collective-permute-start(f32[2,2,2,16,512]{4,3,1,0,2:T(8,128)S(1)} %bitcast.83), channel_id=1, source_target_pairs={{0,2},{2,0},{4,6},{6,4},{8,10},{10,8},{12,14},{14,12},{16,18},{18,... | collective-permute-start | bytes 786440 | tf_op jit(solution)/shard_map/ppermute | solution.py:120
  86.2 7.2 %collective-permute-start.11 = (f32[2,2,16,512]{3,2,1,0:T(8,128)S(1)}, f32[2,2,16,512]{3,2,1,0:T(8,128)S(1)}, u32[]{:S(2)}, u32[]{:S(2)}) collective-permute-start(f32[2,2,16,512]{3,2,1,0:T(8,128)S(1)} %dynamic-slice_bitcast_fusion.2), channel_id=1, source_target_pairs={{0,4},{2,6},{4,0},{6,2},{8,12},{10,14},{12,8},{14,10},{16,20},{18,... | collective-permute-start | bytes 393224 | tf_op jit(solution)/shard_map/ppermute | solution.py:120
  90.8 10.9 %collective-permute-start.6 = (f32[2,2,48,512]{3,2,1,0:T(8,128)S(1)}, f32[2,2,48,512]{3,2,1,0:T(8,128)S(1)}, u32[]{:S(2)}, u32[]{:S(2)}) collective-permute-start(f32[2,2,48,512]{3,2,1,0:T(8,128)S(1)} %dynamic-slice_bitcast_fusion), channel_id=1, source_target_pairs={{0,4},{2,6},{4,0},{6,2},{8,12},{10,14},{12,8},{14,10},{16,20},{18,... | collective-permute-start | bytes 1179656 | tf_op jit(solution)/shard_map/ppermute | solution.py:120
  93.4 10.3 %collective-permute-start.12 = (f32[2,16,512]{2,1,0:T(8,128)S(1)}, f32[2,16,512]{2,1,0:T(8,128)S(1)}, u32[]{:S(2)}, u32[]{:S(2)}) collective-permute-start(f32[2,16,512]{2,1,0:T(8,128)S(1)} %dynamic-slice_bitcast_fusion.4), channel_id=1, source_target_pairs={{0,8},{2,10},{4,12},{6,14},{8,0},{10,2},{12,4},{14,6},{16,24},{18,... | collective-permute-start | bytes 196616 | tf_op jit(solution)/shard_map/ppermute | solution.py:120
  101.9 6.4 %collective-permute-start.7 = (f32[2,48,512]{2,1,0:T(8,128)S(1)}, f32[2,48,512]{2,1,0:T(8,128)S(1)}, u32[]{:S(2)}, u32[]{:S(2)}) collective-permute-start(f32[2,48,512]{2,1,0:T(8,128)S(1)} %dynamic-slice_bitcast_fusion.1), channel_id=1, source_target_pairs={{0,8},{2,10},{4,12},{6,14},{8,0},{10,2},{12,4},{14,6},{16,24},{18,... | collective-permute-start | bytes 589832 | tf_op jit(solution)/shard_map/ppermute | solution.py:120
  103.7 7.4 %collective-permute-start.13 = (f32[16,512]{1,0:T(8,128)S(1)}, f32[16,512]{1,0:T(8,128)S(1)}, u32[]{:S(2)}, u32[]{:S(2)}) collective-permute-start(f32[16,512]{1,0:T(8,128)S(1)} %dynamic-slice_bitcast_fusion.5), channel_id=1, source_target_pairs={{0,16},{2,18},{4,20},{6,22},{8,24},{10,26},{12,28},{14,30},{16,0},... | collective-permute-start | bytes 98312 | tf_op jit(solution)/shard_map/ppermute | solution.py:120
  108.3 5.7 %collective-permute-start.8 = (f32[48,512]{1,0:T(8,128)S(1)}, f32[48,512]{1,0:T(8,128)S(1)}, u32[]{:S(2)}, u32[]{:S(2)}) collective-permute-start(f32[48,512]{1,0:T(8,128)S(1)} %dynamic-slice_bitcast_fusion.3), channel_id=1, source_target_pairs={{0,16},{2,18},{4,20},{6,22},{8,24},{10,26},{12,28},{14,30},{16,0},... | collective-permute-start | bytes 294920 | tf_op jit(solution)/shard_map/ppermute | solution.py:120
  111.2 6.3 %collective-permute-start.15 = (f32[16,512]{1,0:T(8,128)S(1)}, f32[16,512]{1,0:T(8,128)S(1)}, u32[]{:S(2)}, u32[]{:S(2)}) collective-permute-start(f32[16,512]{1,0:T(8,128)S(1)} %bitcast_add_fusion.6), channel_id=1, source_target_pairs={{1,0},{3,2},{5,4},{7,6},{9,8},{11,10},{13,12},{15,14},{17,16},{19,... | collective-permute-start | bytes 98312 | tf_op jit(solution)/shard_map/ppermute | solution.py:198
  114.0 7.7 %collective-permute-start.14 = (f32[16,512]{1,0:T(8,128)S(1)}, f32[16,512]{1,0:T(8,128)S(1)}, u32[]{:S(2)}, u32[]{:S(2)}) collective-permute-start(f32[16,512]{1,0:T(8,128)S(1)} %slice.60), channel_id=1, source_target_pairs={{1,0},{3,2},{5,4},{7,6},{9,8},{11,10},{13,12},{15,14},{17,16},{19,... | collective-permute-start | bytes 98312 | tf_op jit(solution)/shard_map/ppermute | solution.py:198

commit v2 on v0

v2 whole, which is shorter than its diff:
```python
import functools

import jax
import jax.numpy as jnp
from jax import lax
from jax.experimental import pallas as pl
from jax.experimental.pallas import tpu as pltpu
from jax.sharding import PartitionSpec as P

GROUP = 4
UNROLL = 8
VMEM_LIMIT = 32 << 20

ANYWHERE = pl.BlockSpec(memory_space=pl.ANY)
FAR = pl.BlockSpec(memory_space=pltpu.HBM)
NEAR = pl.BlockSpec(memory_space=pltpu.VMEM)
SCALAR = pl.BlockSpec(memory_space=pltpu.SMEM)


def contract(left, right):
    return lax.dot_general(
        left, right, (((0,), (0,)), ((), ())), preferred_element_type=jnp.float32
    )


def far(*arrays):
    return [pltpu.with_memory_space_constraint(a, pltpu.HBM) for a in arrays]


def near_nothing():
    return pl.CostEstimate(flops=1, bytes_accessed=1, transcendentals=0)


def slot_list(block_index, live, nrows_blk, shift):
    slots = block_index.shape[0]
    rows, cols = block_index[:, 0], block_index[:, 1]
    shared = cols >= nrows_blk
    keys = rows + jnp.where(shared, nrows_blk, 0)
    nkeys = 2 * nrows_blk
    k = jnp.arange(slots)
    alive = k < live
    earlier = (keys[:, None] == keys[None, :]) & alive[None, :] & (k[None, :] < k[:, None])
    rank = jnp.sum(earlier.astype(jnp.int32), 1)
    r = jnp.arange(nkeys)
    count = jnp.sum(((keys[None, :] == r[:, None]) & alive[None, :]).astype(jnp.int32), 1)
    groups = (count + GROUP - 1) // GROUP
    bounds = jnp.arange(nkeys + 1)
    first = jnp.sum(jnp.where(r[None, :] < bounds[:, None], groups[None, :], 0), 1)
    begin = jnp.sum(jnp.where(keys[:, None] == r[None, :], first[None, :nkeys], 0), 1)
    place = begin * GROUP + rank
    total = slots // GROUP + nkeys
    g = jnp.arange(total)
    owner_row = jnp.sum((first[None, 1:nkeys] <= g[:, None]).astype(jnp.int32), 1) % nrows_blk
    hit = (place[None, :] == jnp.arange(total * GROUP)[:, None]) & alive[None, :]
    value = ((k + 1) << shift) + cols - jnp.where(shared, nrows_blk, 0)
    return first, owner_row, jnp.sum(jnp.where(hit, value[None, :], 0), 1)


def products(lists, begin, end, row0, shift, block_of, source, acc, bsize):
    _, owner_row, entries = lists

    @pl.loop(0, (end - begin + UNROLL - 1) // UNROLL)
    def _(step):
        rows, prods = [], []
        for u in range(UNROLL):
            g = begin + step * UNROLL + u
            inside = g < end
            g = jnp.minimum(g, end - 1)
            rows.append(jnp.where(inside, owner_row[g] - row0, 0))
            left, right = [], []
            for j in range(GROUP):
                entry = jnp.where(inside, entries[g * GROUP + j], 0)
                block = block_of(g, j, entry)
                column = entry & ((1 << shift) - 1)
                left.append(jnp.where(entry > 0, block, jnp.zeros_like(block)))
                right.append(source[pl.ds(pl.multiple_of(column * bsize, bsize), bsize), :])
            prods.append(
                jnp.dot(jnp.concatenate(left, 1), jnp.concatenate(right, 0), preferred_element_type=jnp.float32)
            )
        for row, prod in zip(rows, prods):
            acc[pl.ds(pl.multiple_of(row * bsize, bsize), bsize), :] += prod


def stored(blocks, shift):
    return lambda g, j, entry: blocks[jnp.maximum((entry >> shift) - 1, 0)]


def shared_range(first, row0, nrows):
    nkeys = (first.shape[0] - 1) // 2
    return first[nkeys + row0], first[nkeys + row0 + nrows]


def begin_kernel(row0, nrows, shift, bsize, first, owner_row, entries, send_rows, blocks, tmat, first_rows, second_rows, own, ahead, panel, near_blocks, picked, acc, staged, sem):
    lists = (first, owner_row, entries)
    depth = picked.shape[0]
    steps = panel.shape[0] // depth
    copy_blocks = pltpu.make_async_copy(blocks, near_blocks, sem.at[steps])

    def part(step):
        chunk = pl.ds(pl.multiple_of(step * depth, depth), depth)
        return pltpu.make_async_copy(tmat.at[chunk], panel.at[chunk], sem.at[step])

    for step in range(steps):
        part(step).start()
    copy_blocks.start()
    picked[...] = jnp.zeros_like(picked)
    acc[...] = jnp.zeros_like(acc)

    @pl.loop(0, steps)
    def _(step):
        part(step).wait()
        begin = pl.multiple_of(step * depth, depth)
        numbers = lax.broadcasted_iota(jnp.int32, (depth, depth), 1) + begin
        picks = jnp.where(send_rows[...] == numbers, 1.0, 0.0).astype(panel.dtype)
        picked[...] += jnp.dot(picks, panel[pl.ds(begin, depth), :], preferred_element_type=jnp.float32)

    half = depth // 2
    odd = lax.axis_index("dom") % 2
    first_rows[...] = picked[pl.ds(pl.multiple_of((1 - odd) * half, half), half), :].astype(first_rows.dtype)
    second_rows[...] = picked[pl.ds(pl.multiple_of(odd * half, half), half), :].astype(second_rows.dtype)
    copy_blocks.wait()
    begin, end = shared_range(first, row0, nrows)

    @pl.loop(begin, end)
    def _(g):
        for j in range(GROUP):
            staged[(g - begin) * GROUP + j] = stored(near_blocks, shift)(g, j, entries[g * GROUP + j])

    batch = UNROLL * GROUP
    batches = (end - begin + UNROLL - 1) // UNROLL

    def out_blocks(step):
        some = pl.ds(step * batch, batch)
        return pltpu.make_async_copy(staged.at[some], ahead.at[some], sem.at[0])

    @pl.loop(0, batches)
    def _(step):
        out_blocks(step).start()

    products(lists, first[row0], first[row0 + nrows], row0, shift, stored(near_blocks, shift), panel, acc, bsize)
    out_own = pltpu.make_async_copy(acc, own, sem.at[1])
    out_own.start()

    @pl.loop(0, batches)
    def _(step):
        out_blocks(step).wait()

    out_own.wait()


def begin_work(lists, send_rows, blocks, tmat, shift, row0, nrows):
    bsize, width, picked = blocks.shape[1], tmat.shape[1], send_rows.size
    batch = UNROLL * GROUP
    room = -(-(blocks.shape[0] + nrows * GROUP) // batch) * batch
    tmat, blocks = far(tmat, blocks)
    return pl.pallas_call(
        functools.partial(begin_kernel, row0, nrows, shift, bsize),
        out_shape=[
            jax.ShapeDtypeStruct((picked // 2, width), tmat.dtype),
            jax.ShapeDtypeStruct((picked // 2, width), tmat.dtype),
            pltpu.HBM((nrows * bsize, width), jnp.float32),
            pltpu.HBM((room, bsize, bsize), blocks.dtype),
        ],
        in_specs=[SCALAR] * 3 + [NEAR] + [FAR] * 2,
        out_specs=[NEAR] * 2 + [FAR] * 2,
        scratch_shapes=[
            pltpu.VMEM(tmat.shape, tmat.dtype),
            pltpu.VMEM(blocks.shape, blocks.dtype),
            pltpu.VMEM((picked, width), jnp.float32),
            pltpu.VMEM((nrows * bsize, width), jnp.float32),
            pltpu.VMEM((room, bsize, bsize), blocks.dtype),
            pltpu.SemaphoreType.DMA((tmat.shape[0] // picked + 1,)),
        ],
        compiler_params=pltpu.CompilerParams(vmem_limit_bytes=VMEM_LIMIT),
        cost_estimate=near_nothing(),
    )(*lists, send_rows.reshape(picked, 1), blocks, tmat)


def place_halo(even, odd, halo):
    sides = even.shape[0]
    odd_partition = lax.axis_index("dom") % 2
    halo[pl.ds(pl.multiple_of((1 - odd_partition) * sides, sides), sides), :] = even[...]
    halo[pl.ds(pl.multiple_of(odd_partition * sides, sides), sides), :] = odd[...]


def pieces_kernel(row0, nrows, shift, bsize, other0, n_col, first, owner_row, entries, blocks, even, odd, own, tmat, after, *refs):
    *outs, near_blocks, halo, acc, sem, block_sem = refs
    panel_column = lax.axis_index("col") == n_col - 1
    size, part = outs[0].shape
    batch = UNROLL * GROUP

    @pl.when(panel_column)
    def _():
        begin, end = shared_range(first, row0, nrows)
        steps = (end - begin + UNROLL - 1) // UNROLL

        def in_blocks(step):
            return pltpu.make_async_copy(blocks.at[pl.ds(step * batch, batch)], near_blocks.at[pl.ds(step * batch, batch)], block_sem)

        in_own = pltpu.make_async_copy(own, acc, sem.at[0])

        @pl.loop(0, steps)
        def _(step):
            in_blocks(step).start()

        in_own.start()
        place_halo(even, odd, halo)

        @pl.loop(0, steps)
        def _(step):
            in_blocks(step).wait()

        in_own.wait()
        block_of = lambda g, j, entry: near_blocks[(g - begin) * GROUP + j]
        products((first, owner_row, entries), begin, end, row0, shift, block_of, halo, acc, bsize)
        for h, out in enumerate(outs):
            out[...] = acc[:, pl.ds(h * part, part)].astype(out.dtype)

    @pl.when(jnp.logical_not(panel_column))
    def _():
        copies = [
            pltpu.make_async_copy(tmat.at[pl.ds(other0, size), pl.ds(h * part, part)], out, sem.at[h])
            for h, out in enumerate(outs)
        ]
        for copy in copies:
            copy.start()
        for copy in copies:
            copy.wait()


def pieces(lists, blocks, even, odd, own, tmat, after, shift, row0, nrows, other0, chunks, n_col):
    bsize, width = blocks.shape[1], tmat.shape[1]
    size, part = nrows * bsize, width // chunks
    return pl.pallas_call(
        functools.partial(pieces_kernel, row0, nrows, shift, bsize, other0, n_col),
        out_shape=[jax.ShapeDtypeStruct((size, part), tmat.dtype)] * chunks,
        in_specs=[SCALAR] * 3 + [FAR] + [NEAR] * 2 + [FAR] * 2 + [ANYWHERE],
        out_specs=[NEAR] * chunks,
        scratch_shapes=[
            pltpu.VMEM(blocks.shape, blocks.dtype),
            pltpu.VMEM((2 * even.shape[0], width), tmat.dtype),
            pltpu.VMEM((size, width), jnp.float32),
            pltpu.SemaphoreType.DMA((chunks,)),
            pltpu.SemaphoreType.DMA,
        ],
        compiler_params=pltpu.CompilerParams(vmem_limit_bytes=VMEM_LIMIT),
        cost_estimate=near_nothing(),
    )(*lists, *far(blocks), even, odd, *far(own, tmat), after)


def mass_kernel(row0, nrows, shift, bsize, first, owner_row, entries, blocks, tmat, even, odd, after, out, panel, near_blocks, halo, acc, sem):
    lists = (first, owner_row, entries)
    copies = [pltpu.make_async_copy(tmat, panel, sem.at[0]), pltpu.make_async_copy(blocks, near_blocks, sem.at[1])]
    for copy in copies:
        copy.start()
    acc[...] = jnp.zeros_like(acc)
    place_halo(even, odd, halo)
    for copy in copies:
        copy.wait()
    block_of = stored(near_blocks, shift)
    products(lists, first[row0], first[row0 + nrows], row0, shift, block_of, panel, acc, bsize)
    products(lists, *shared_range(first, row0, nrows), row0, shift, block_of, halo, acc, bsize)
    out[...] = acc[...].astype(out.dtype)


def known_kernel(left, right, out):
    out[...] = contract(left[...], right[...])


def known_product(left, right):
    rows = right.shape[0]
    width = left.shape[1]
    return pl.pallas_call(
        known_kernel,
        grid=(1,),
        out_shape=jax.ShapeDtypeStruct((width, right.shape[1]), jnp.float32),
        in_specs=[pl.BlockSpec((rows, width), lambda i: (0, 0)), pl.BlockSpec(right.shape, lambda i: (0, 0))],
        out_specs=pl.BlockSpec((width, right.shape[1]), lambda i: (0, 0)),
        compiler_params=pltpu.CompilerParams(vmem_limit_bytes=VMEM_LIMIT),
        cost_estimate=near_nothing(),
    )(left, right)


def mass_rows(lists, blocks, tmat, even, odd, after, shift, row0, nrows):
    bsize, width = blocks.shape[1], tmat.shape[1]
    return pl.pallas_call(
        functools.partial(mass_kernel, row0, nrows, shift, bsize),
        out_shape=jax.ShapeDtypeStruct((nrows * bsize, width), tmat.dtype),
        in_specs=[SCALAR] * 3 + [FAR] * 2 + [NEAR] * 2 + [ANYWHERE],
        out_specs=NEAR,
        scratch_shapes=[
            pltpu.VMEM(tmat.shape, tmat.dtype),
            pltpu.VMEM(blocks.shape, blocks.dtype),
            pltpu.VMEM((2 * even.shape[0], width), tmat.dtype),
            pltpu.VMEM((nrows * bsize, width), jnp.float32),
            pltpu.SemaphoreType.DMA((2,)),
        ],
        compiler_params=pltpu.CompilerParams(vmem_limit_bytes=VMEM_LIMIT),
        cost_estimate=near_nothing(),
    )(*lists, *far(blocks, tmat), even, odd, after)


def halving(x, bit, axis, route):
    mine = (lax.axis_index("dom") // bit) % 2
    keep = lax.dynamic_index_in_dim(x, mine, axis, keepdims=False)
    send = lax.dynamic_index_in_dim(x, 1 - mine, axis, keepdims=False)
    return keep + lax.ppermute(send, *route(bit))


def body(tmat, stored_mass_blocks, block_index, live_block_count, send_rows):
    n_col, n_dom = lax.axis_size("col"), lax.axis_size("dom")
    owner = n_col - 1
    col, dom = lax.axis_index("col"), lax.axis_index("dom")
    rows_dev, width = tmat.shape
    bsize = stored_mass_blocks.shape[1]
    nrows_blk = rows_dev // bsize
    share = width // n_dom
    shift = nrows_blk.bit_length()
    live = jnp.where(col == owner, live_block_count[0], 0)
    lists = slot_list(block_index, live, nrows_blk, shift)

    blocks = stored_mass_blocks

    def exchange(block, begin):
        pairs = [(i * n_col + owner, (i + 1) * n_col + owner) for i in range(begin, n_dom - 1, 2)]
        return lax.ppermute(block, ("dom", "col"), pairs + [(b, a) for a, b in pairs])

    na = (nrows_blk * 13) // 32
    nb = nrows_blk - na
    *rows, own_a, blocks_a = begin_work(lists, send_rows, blocks, tmat, shift, nb, na)
    even, odd = exchange(rows[0], 0), exchange(rows[1], 1)

    if n_col != 2 or n_dom < 4 or n_dom & (n_dom - 1):
        mass = mass_rows(lists, blocks, tmat, even, odd, even, shift, 0, nrows_blk)
        total = lax.psum(contract(lax.psum(mass, "col"), tmat), "dom")
        return lax.dynamic_slice_in_dim(total, dom * share, share, 0)

    half = n_dom // 2
    cut = nb * bsize
    early = cut - na * bsize
    ahead = lax.ppermute(tmat[:early], "col", [(0, 1)])

    (sent,) = pieces(lists, blocks_a, even, odd, own_a, tmat, ahead, shift, nb, na, early, 1, n_col)
    got = lax.ppermute(sent, "col", [(0, 1), (1, 0)])
    mass_b = mass_rows(lists, blocks, tmat, even, odd, sent, shift, 0, nb)
    known = known_product(mass_b, ahead)
    own = contract(sent, tmat[cut:]) + contract(mass_b, tmat[:cut])

    def both(bit):
        return "dom", [(i, i ^ bit) for i in range(n_dom)]

    def panel_column(bit):
        return ("dom", "col"), [(i * n_col + owner, (i ^ bit) * n_col + owner) for i in range(n_dom)]

    bits = half.bit_length() - 1
    own = own.reshape((2,) * (bits + 1) + (share, width))
    for b in range(bits + 1):
        if b == bits - 1:
            got, own = lax.optimization_barrier((got, own))
        own = halving(own, 1 << b, bits - b, panel_column)

    def in_panel_column(got, known):
        x = (known + contract(mass_b[early:], got)).reshape(2, half, share, width)
        return jnp.concatenate([x[0], x[1]], 2)

    def in_other_column(got, known):
        x = contract(got, tmat[cut:]).reshape(2, half, share, width)
        return jnp.concatenate([x[0], x[1]], 2)

    x = lax.cond(col == owner, in_panel_column, in_other_column, got, known)
    x = x.reshape((2,) * bits + (share, 2 * width))
    for b in range(bits):
        x = halving(x, 1 << b, bits - 1 - b, both)
    x = jnp.stack([x[:, :width], x[:, width:]])
    x = halving(x, half, 0, both)
    other = x + lax.ppermute(x, "col", [(1, 0)])
    return jnp.where(col == owner, own, other)


def solution(mesh):
    return jax.shard_map(
        body,
        mesh=mesh,
        in_specs=(P("dom", "col"), P("dom", None, None), P("dom", None), P("dom"), P("dom", None)),
        out_specs=P("dom", "col"),
        check_vma=False,
    )
```

time: 493 us -> 103 us (0.21)
  waiting for transfers between devices: 214 us -> 41 us
  other arithmetic: 157 us -> 3.65 us
  matrix products: 52 us -> 5.79 us
  local copies, waits for them, and re-layouts: 48.5 us -> 2.44 us
  starting transfers between devices: 3.09 us -> 31 us
  Pallas kernels: 0 us -> 17.9 us
  between operations: 14.2 us -> 0.99 us
    psum x2 -> x0, waiting for transfers between devices: 211 us -> none  [the longest x1 113 us: broadcast(): return lax.psum(block, axis)]
    scatter-add x4 -> x0, other arithmetic: 146 us -> none  [step(): acc = acc.at[targets].add(prod * weights[:, None, None])]
    dot_general x4 -> x0, matrix products: 48.6 us -> none  [step(): jnp.einsum('kab,kbw->kaw', blocks, selected, preferred_element_type=jnp.f...]
    gather x6 -> x0, local copies, waits for them, and re-layouts: 39.3 us -> none  [the longest x4 31.5 us: step(): selected = jnp.take(extended, columns, axis=0)]
    ppermute x2 -> x13, waiting for transfers between devices: 2.7 us -> 41 us  [the longest x1 19 us: body(): got = lax.ppermute(sent, 'col', [(0, 1), (1, 0)])]
    ppermute x2 -> x13, starting transfers between devices: 3.05 us -> 31 us  [the longest x8 19.2 us: halving(): return keep + lax.ppermute(send, *route(bit))]
    pallas_call x0 -> x4, Pallas kernels: none -> 17.9 us  [the longest x1 7.6 us: begin_work(): pl.pallas_call(functools.partial(begin_kernel, row0, nrows, shift, bsize)...]
  transfers between devices with their start and end apart: 4 -> 13, of which waited for: 3 -> 7; matrix products, arithmetic and copies ran while one was open for 1% -> 6% of each run, Pallas kernels for 0% -> 15%
where the time goes in v2:
time: 103 us
  waiting for transfers between devices  41 us (40%)
  starting transfers between devices  31 us (30%)
  Pallas kernels  17.9 us (17%)
  matrix products  5.79 us (6%)
  other arithmetic  3.65 us (4%)
  local copies, waits for them, and re-layouts  2.44 us (2%)
    ppermute x8, starting transfers between devices, halving(): return keep + lax.ppermute(send, *route(bit))  19.2 us
    ppermute x1, waiting for transfers between devices, body(): got = lax.ppermute(sent, 'col', [(0, 1), (1, 0)])  19 us
    ppermute x8, waiting for transfers between devices, halving(): return keep + lax.ppermute(send, *route(bit))  12.7 us
    pallas_call x1, Pallas kernels, begin_work(): pl.pallas_call(functools.partial(begin_kernel, row0, nrows, shift, bsize)...  7.6 us
    dot_general x3, matrix products, contract(): lax.dot_general(left, right, (((0,), (0,)), ((), ())), preferred_element_...  5.79 us
    pallas_call x1, Pallas kernels, mass_rows(): pl.pallas_call(functools.partial(mass_kernel, row0, nrows, shift, bsize),...  5.49 us
    ppermute x1, starting transfers between devices, body(): ahead = lax.ppermute(tmat[:early], 'col', [(0, 1)])  4.89 us
    ppermute x1, waiting for transfers between devices, body(): other = x + lax.ppermute(x, 'col', [(1, 0)])  4.85 us
  transfers between devices with their start and end apart: 13, of which 7 were waited for; matrix products, arithmetic and copies ran while one was open for 6% of the time, Pallas kernels for 15%

profile of v2, /device:TPU:0, one launch (start us, length us, event | category | flops | bytes accessed | tf_op | source)
XLA Modules:
  0.0 102.8 jit_solution(15688715303015705585)
XLA Ops:
  0.0 1.2 %slice.53 = bf16[768,512]{1,0:T(8,128)(2,1)S(1)} slice(bf16[4096,512]{1,0:T(8,128)(2,1)} %tmat.5), slice={[0:768], [0:512]} | slice | bytes 1572864 | tf_op jit(solution)/shard_map/slice | solution.py:341
  1.2 4.9 %collective-permute-start.2 = (bf16[768,512]{1,0:T(8,128)(2,1)S(1)}, bf16[768,512]{1,0:T(8,128)(2,1)S(1)}, u32[]{:S(2)}, u32[]{:S(2)}) collective-permute-start(bf16[768,512]{1,0:T(8,128)(2,1)S(1)} %slice.53), channel_id=1, source_target_pairs={{0,1},{2,3},{4,5},{6,7},{8,9},{10,11},{12,13},{14,15},{16,17},{18,... | collective-permute-start | bytes 2359304 | tf_op jit(solution)/shard_map/ppermute | solution.py:341
  6.1 0.8 fusion.23
  8.2 0.7 copy.12
  9.3 7.6 %shard_map.55 = (bf16[256,512]{1,0:T(8,128)(2,1)S(1)}, bf16[256,512]{1,0:T(8,128)(2,1)S(1)}, f32[1664,512]{1,0:T(8,128)}, bf16[320,128,128]{2,1,0:T(8,128)(2,1)}) custom-call(s32[65]{0:T(128)S(1)} %select_reduce_fusion.2.first, s32[128]{0:T(128)S(1)} %and_select_fusion.owner_row, s32[512]{0:T(512)S(1)} %select_reduce_fusion.entries, s32[512,1]{1,0:T(8,128)S(1)} %bitcast.60, ...), custom_call_target="tpu_custom_call" | custom-call | flops 1 | bytes 1 | tf_op jit(solution)/shard_map/pallas_call | solution.py:156
  16.9 0.7 collective-permute-start
  17.6 0.7 collective-permute-start.1
  18.3 4.5 %collective-permute-done.2.after.right = bf16[768,512]{1,0:T(8,128)(2,1)S(1)} collective-permute-done((bf16[768,512]{1,0:T(8,128)(2,1)S(1)}, bf16[768,512]{1,0:T(8,128)(2,1)S(1)}, u32[]{:S(2)}, u32[]{:S(2)}) %collective-permute-start.2) | collective-permute-done | bytes 786464 | tf_op jit(solution)/shard_map/ppermute | solution.py:341
  22.8 2.1 %shard_map.56.after = bf16[1664,512]{1,0:T(8,128)(2,1)S(1)} custom-call(s32[65]{0:T(128)S(1)} %select_reduce_fusion.2.first, s32[128]{0:T(128)S(1)} %and_select_fusion.owner_row, s32[512]{0:T(512)S(1)} %select_reduce_fusion.entries, bf16[320,128,128]{2,1,0:T(8,128)(2,1)} %get-tuple-element.30.blocks, bf16[256,512]{1,0:T(8,128)(2,1)S(1)} %collective-permute-done.even, ...), custom_call_target="tpu_custom_call" | custom-call | flops 1 | bytes 1 | tf_op jit(solution)/shard_map/pallas_call | solution.py:234
  24.9 4.3 %collective-permute-start.3 = (bf16[1664,512]{1,0:T(8,128)(2,1)S(1)}, bf16[1664,512]{1,0:T(8,128)(2,1)}, u32[]{:S(2)}, u32[]{:S(2)}) collective-permute-start(bf16[1664,512]{1,0:T(8,128)(2,1)S(1)} %shard_map.56.after), channel_id=1, source_target_pairs={{0,1},{1,0},{2,3},{3,2},{4,5},{5,4},{6,7},{7,6},{8,9},{9,8},{10,11... | collective-permute-start | bytes 5111816 | tf_op jit(solution)/shard_map/ppermute | solution.py:344
  29.2 5.5 %shard_map.57.left = bf16[2432,512]{1,0:T(8,128)(2,1)S(1)} custom-call(s32[65]{0:T(128)S(1)} %select_reduce_fusion.2.first, s32[128]{0:T(128)S(1)} %and_select_fusion.owner_row, s32[512]{0:T(512)S(1)} %select_reduce_fusion.entries, bf16[256,128,128]{2,1,0:T(8,128)(2,1)} %blocks.3, bf16[4096,512]{1,0:T(8,128)(2,1)} %tmat.5, ...), custom_call_target="tpu_custom_call" | custom-call | flops 1 | bytes 1 | tf_op jit(solution)/shard_map/pallas_call | solution.py:286
  34.7 1.5 %fusion.7 = f32[512,512]{1,0:T(8,128)S(1)} fusion(bf16[2432,512]{1,0:T(8,128)(2,1)S(1)} %shard_map.57.left, bf16[4096,512]{1,0:T(8,128)(2,1)S(1)} %copy-done), kind=kOutput, calls=%fused_computation.7 | convolution fusion | flops 1275068416 | bytes 6029312 | tf_op jit(solution)/shard_map/dot_general | solution.py:21
  36.3 1.2 %fusion.11 = f32[512,512]{1,0:T(8,128)S(1)} fusion(f32[512,512]{1,0:T(8,128)S(1)} %fusion.7, bf16[1664,512]{1,0:T(8,128)(2,1)S(1)} %shard_map.56.after, bf16[4096,512]{1,0:T(8,128)(2,1)S(1)} %copy-done), kind=kOutput, calls=%fused_computation.11 | convolution fusion | flops 872677376 | bytes 5505024 | tf_op jit(solution)/shard_map/dot_general | solution.py:21
  37.6 1.5 %collective-permute-start.4 = (f32[2,2,2,32,512]{4,3,1,0,2:T(8,128)S(1)}, f32[2,2,2,32,512]{4,3,1,0,2:T(8,128)}, u32[]{:S(2)}, u32[]{:S(2)}) collective-permute-start(f32[2,2,2,32,512]{4,3,1,0,2:T(8,128)S(1)} %bitcast.67), channel_id=1, source_target_pairs={{1,3},{3,1},{5,7},{7,5},{9,11},{11,9},{13,15},{15,13},{17,19},{19,... | collective-permute-start | bytes 1572872 | tf_op jit(solution)/shard_map/ppermute | solution.py:307
  39.0 1.1 %bitcast_add_fusion.1 = f32[2,2,2,32,512]{4,3,1,0,2:T(8,128)S(1)} fusion(f32[2,2,2,32,512]{4,3,1,0,2:T(8,128)} %collective-permute-done.4, f32[2,2,2,1,32,512]{5,4,3,2,1,0:T(8,128)S(1)} %get-tuple-element.40), kind=kLoop, calls=%fused_computation.13 | loop fusion | flops 131072 | bytes 1572864 | tf_op jit(solution)/shard_map/add | solution.py:307
  40.2 0.7 collective-permute-start.5
  40.9 2.7 %shard_map.58 = f32[512,512]{1,0:T(8,128)} custom-call(bf16[2432,512]{1,0:T(8,128)(2,1)} %copy-done.1, bf16[768,512]{1,0:T(8,128)(2,1)S(1)} %collective-permute-done.2.after.right), custom_call_target="tpu_custom_call" | custom-call | flops 1 | bytes 1 | tf_op jit(solution)/shard_map/pallas_call | solution.py:273
  43.6 19.0 %collective-permute-done.3 = bf16[1664,512]{1,0:T(8,128)(2,1)} collective-permute-done((bf16[1664,512]{1,0:T(8,128)(2,1)S(1)}, bf16[1664,512]{1,0:T(8,128)(2,1)}, u32[]{:S(2)}, u32[]{:S(2)}) %collective-permute-start.3) | collective-permute-done | bytes 1703968 | tf_op jit(solution)/shard_map/ppermute | solution.py:344
  62.6 3.3 %conditional.1 = (f32[2,2,2,32,1024]{4,3,2,1,0:T(8,128)S(1)}) conditional(s32[]{:T(128)} %convert_element_type.15, (bf16[4096,512]{1,0:T(8,128)(2,1)}, bf16[1664,512]{1,0:T(8,128)(2,1)}) %tuple.15, (bf16[2432,512]{1,0:T(8,128)(2,1)}, bf16[1664,512]{1,0:T(8,128)(2,1)}, f32[512,512]{1,0:T(8,128)}) %tuple.26), branch_computations={%region_6.7_spmd, %region_7.8_spmd} | conditional | flops 872939520 | bytes 9699336 | solution.py:370
  62.6 3.1 %fusion = f32[512,512]{1,0:T(8,128)S(1)} fusion(bf16[1664,512]{1,0:T(8,128)(2,1)} %get-tuple-element.19, bf16[4096,512]{1,0:T(8,128)(2,1)} %get-tuple-element.20), kind=kOutput, calls=%fused_computation | convolution fusion | flops 872415232 | bytes 4456448 | tf_op jit(solution)/shard_map/cond/branch_0_fun/dot_general | solution.py:21
  66.0 4.6 %collective-permute-start.8 = (f32[2,2,32,1024]{3,2,1,0:T(8,128)S(1)}, f32[2,2,32,1024]{3,2,1,0:T(8,128)S(1)}, u32[]{:S(2)}, u32[]{:S(2)}) collective-permute-start(f32[2,2,32,1024]{3,2,1,0:T(8,128)S(1)} %dynamic-slice_bitcast_fusion), channel_id=1, source_target_pairs={{0,2},{2,0},{4,6},{6,4},{8,10},{10,8},{12,14},{14,12},{16,18},{18,... | collective-permute-start | bytes 1572872 | tf_op jit(solution)/shard_map/ppermute | solution.py:307
  70.6 1.5 %collective-permute-done.8 = f32[2,2,32,1024]{3,2,1,0:T(8,128)S(1)} collective-permute-done((f32[2,2,32,1024]{3,2,1,0:T(8,128)S(1)}, f32[2,2,32,1024]{3,2,1,0:T(8,128)S(1)}, u32[]{:S(2)}, u32[]{:S(2)}) %collective-permute-start.8) | collective-permute-done | bytes 524320 | tf_op jit(solution)/shard_map/ppermute | solution.py:307
  72.2 5.8 %collective-permute-start.9 = (f32[2,32,1024]{2,1,0:T(8,128)S(1)}, f32[2,32,1024]{2,1,0:T(8,128)S(1)}, u32[]{:S(2)}, u32[]{:S(2)}) collective-permute-start(f32[2,32,1024]{2,1,0:T(8,128)S(1)} %dynamic-slice_bitcast_fusion.1), channel_id=1, source_target_pairs={{0,4},{2,6},{4,0},{6,2},{8,12},{10,14},{12,8},{14,10},{16,20},{18,... | collective-permute-start | bytes 786440 | tf_op jit(solution)/shard_map/ppermute | solution.py:307
  78.1 0.7 collective-permute-start.6
  78.8 5.9 %collective-permute-done.9 = f32[2,32,1024]{2,1,0:T(8,128)S(1)} collective-permute-done((f32[2,32,1024]{2,1,0:T(8,128)S(1)}, f32[2,32,1024]{2,1,0:T(8,128)S(1)}, u32[]{:S(2)}, u32[]{:S(2)}) %collective-permute-start.9) | collective-permute-done | bytes 262176 | tf_op jit(solution)/shard_map/ppermute | solution.py:307
  84.7 2.8 %collective-permute-start.10 = (f32[32,1024]{1,0:T(8,128)S(1)}, f32[32,1024]{1,0:T(8,128)S(1)}, u32[]{:S(2)}, u32[]{:S(2)}) collective-permute-start(f32[32,1024]{1,0:T(8,128)S(1)} %dynamic-slice_bitcast_fusion.3), channel_id=1, source_target_pairs={{0,8},{2,10},{4,12},{6,14},{8,0},{10,2},{12,4},{14,6},{16,24},{18,... | collective-permute-start | bytes 393224 | tf_op jit(solution)/shard_map/ppermute | solution.py:307
  87.5 3.1 %collective-permute-done.10 = f32[32,1024]{1,0:T(8,128)S(1)} collective-permute-done((f32[32,1024]{1,0:T(8,128)S(1)}, f32[32,1024]{1,0:T(8,128)S(1)}, u32[]{:S(2)}, u32[]{:S(2)}) %collective-permute-start.10) | collective-permute-done | bytes 131104 | tf_op jit(solution)/shard_map/ppermute | solution.py:307
  90.8 2.5 %collective-permute-start.11 = (f32[32,512]{1,0:T(8,128)S(1)}, f32[32,512]{1,0:T(8,128)S(1)}, u32[]{:S(2)}, u32[]{:S(2)}) collective-permute-start(f32[32,512]{1,0:T(8,128)S(1)} %fusion.17), channel_id=1, source_target_pairs={{0,16},{2,18},{4,20},{6,22},{8,24},{10,26},{12,28},{14,30},{16,0},... | collective-permute-start | bytes 196616 | tf_op jit(solution)/shard_map/ppermute | solution.py:307
  93.3 0.7 collective-permute-start.7
  93.9 2.1 %collective-permute-done.11 = f32[32,512]{1,0:T(8,128)S(1)} collective-permute-done((f32[32,512]{1,0:T(8,128)S(1)}, f32[32,512]{1,0:T(8,128)S(1)}, u32[]{:S(2)}, u32[]{:S(2)}) %collective-permute-start.11) | collective-permute-done | bytes 65568 | tf_op jit(solution)/shard_map/ppermute | solution.py:307
  96.0 1.3 %collective-permute-start.12 = (f32[32,512]{1,0:T(8,128)S(1)}, f32[32,512]{1,0:T(8,128)S(1)}, u32[]{:S(2)}, u32[]{:S(2)}) collective-permute-start(f32[32,512]{1,0:T(8,128)S(1)} %fusion.20), channel_id=1, source_target_pairs={{1,0},{3,2},{5,4},{7,6},{9,8},{11,10},{13,12},{15,14},{17,16},{19,... | collective-permute-start | bytes 196616 | tf_op jit(solution)/shard_map/ppermute | solution.py:376
  97.3 4.8 %collective-permute-done.12 = f32[32,512]{1,0:T(8,128)S(1)} collective-permute-done((f32[32,512]{1,0:T(8,128)S(1)}, f32[32,512]{1,0:T(8,128)S(1)}, u32[]{:S(2)}, u32[]{:S(2)}) %collective-permute-start.12) | collective-permute-done | bytes 65568 | tf_op jit(solution)/shard_map/ppermute | solution.py:376
  (42 shorter events, 2.3 us)
Async XLA Ops:
  1.2 21.6 %collective-permute-start.2 = (bf16[768,512]{1,0:T(8,128)(2,1)S(1)}, bf16[768,512]{1,0:T(8,128)(2,1)S(1)}, u32[]{:S(2)}, u32[]{:S(2)}) collective-permute-start(bf16[768,512]{1,0:T(8,128)(2,1)S(1)} %slice.53), channel_id=1, source_target_pairs={{0,1},{2,3},{4,5},{6,7},{8,9},{10,11},{12,13},{14,15},{16,17},{18,... | collective-permute-start | bytes 2359304 | tf_op jit(solution)/shard_map/ppermute | solution.py:341
  16.9 1.4 %collective-permute-start = (bf16[256,512]{1,0:T(8,128)(2,1)S(1)}, bf16[256,512]{1,0:T(8,128)(2,1)S(1)}, u32[]{:S(2)}, u32[]{:S(2)}) collective-permute-start(bf16[256,512]{1,0:T(8,128)(2,1)S(1)} %get-tuple-element.31), channel_id=1, source_target_pairs={{1,3},{5,7},{9,11},{13,15},{17,19},{21,23},{25,27},{29,31},{3,1},{... | collective-permute-start | bytes 786440 | tf_op jit(solution)/shard_map/ppermute | solution.py:326
  17.6 0.7 collective-permute-start.1
  24.9 9.8 %copy-start = (bf16[4096,512]{1,0:T(8,128)(2,1)S(1)}, bf16[4096,512]{1,0:T(8,128)(2,1)}, u32[]{:S(2)}) copy-start(bf16[4096,512]{1,0:T(8,128)(2,1)} %tmat.5) | copy-start | bytes 12582916
  24.9 37.7 %collective-permute-start.3 = (bf16[1664,512]{1,0:T(8,128)(2,1)S(1)}, bf16[1664,512]{1,0:T(8,128)(2,1)}, u32[]{:S(2)}, u32[]{:S(2)}) collective-permute-start(bf16[1664,512]{1,0:T(8,128)(2,1)S(1)} %shard_map.56.after), channel_id=1, source_target_pairs={{0,1},{1,0},{2,3},{3,2},{4,5},{5,4},{6,7},{7,6},{8,9},{9,8},{10,11... | collective-permute-start | bytes 5111816 | tf_op jit(solution)/shard_map/ppermute | solution.py:344
  34.7 1.6 %copy-start.1 = (bf16[2432,512]{1,0:T(8,128)(2,1)}, bf16[2432,512]{1,0:T(8,128)(2,1)S(1)}, u32[]{:S(2)}) copy-start(bf16[2432,512]{1,0:T(8,128)(2,1)S(1)} %shard_map.57.left) | copy-start | bytes 7471108
  37.6 1.5 %collective-permute-start.4 = (f32[2,2,2,32,512]{4,3,1,0,2:T(8,128)S(1)}, f32[2,2,2,32,512]{4,3,1,0,2:T(8,128)}, u32[]{:S(2)}, u32[]{:S(2)}) collective-permute-start(f32[2,2,2,32,512]{4,3,1,0,2:T(8,128)S(1)} %bitcast.67), channel_id=1, source_target_pairs={{1,3},{3,1},{5,7},{7,5},{9,11},{11,9},{13,15},{15,13},{17,19},{19,... | collective-permute-start | bytes 1572872 | tf_op jit(solution)/shard_map/ppermute | solution.py:307
  40.2 3.4 %collective-permute-start.5 = (f32[2,2,32,512]{3,2,1,0:T(8,128)S(1)}, f32[2,2,32,512]{3,2,1,0:T(8,128)S(1)}, u32[]{:S(2)}, u32[]{:S(2)}) collective-permute-start(f32[2,2,32,512]{3,2,1,0:T(8,128)S(1)} %dynamic-slice_bitcast_fusion.2), channel_id=1, source_target_pairs={{1,5},{3,7},{5,1},{7,3},{9,13},{11,15},{13,9},{15,11},{17,21},{19,... | collective-permute-start | bytes 786440 | tf_op jit(solution)/shard_map/ppermute | solution.py:307
  66.0 6.1 %collective-permute-start.8 = (f32[2,2,32,1024]{3,2,1,0:T(8,128)S(1)}, f32[2,2,32,1024]{3,2,1,0:T(8,128)S(1)}, u32[]{:S(2)}, u32[]{:S(2)}) collective-permute-start(f32[2,2,32,1024]{3,2,1,0:T(8,128)S(1)} %dynamic-slice_bitcast_fusion), channel_id=1, source_target_pairs={{0,2},{2,0},{4,6},{6,4},{8,10},{10,8},{12,14},{14,12},{16,18},{18,... | collective-permute-start | bytes 1572872 | tf_op jit(solution)/shard_map/ppermute | solution.py:307
  72.2 12.4 %collective-permute-start.9 = (f32[2,32,1024]{2,1,0:T(8,128)S(1)}, f32[2,32,1024]{2,1,0:T(8,128)S(1)}, u32[]{:S(2)}, u32[]{:S(2)}) collective-permute-start(f32[2,32,1024]{2,1,0:T(8,128)S(1)} %dynamic-slice_bitcast_fusion.1), channel_id=1, source_target_pairs={{0,4},{2,6},{4,0},{6,2},{8,12},{10,14},{12,8},{14,10},{16,20},{18,... | collective-permute-start | bytes 786440 | tf_op jit(solution)/shard_map/ppermute | solution.py:307
  78.1 9.4 %collective-permute-start.6 = (f32[2,32,512]{2,1,0:T(8,128)S(1)}, f32[2,32,512]{2,1,0:T(8,128)S(1)}, u32[]{:S(2)}, u32[]{:S(2)}) collective-permute-start(f32[2,32,512]{2,1,0:T(8,128)S(1)} %dynamic-slice_bitcast_fusion.4), channel_id=1, source_target_pairs={{1,9},{3,11},{5,13},{7,15},{9,1},{11,3},{13,5},{15,7},{17,25},{19,... | collective-permute-start | bytes 393224 | tf_op jit(solution)/shard_map/ppermute | solution.py:307
  84.7 6.0 %collective-permute-start.10 = (f32[32,1024]{1,0:T(8,128)S(1)}, f32[32,1024]{1,0:T(8,128)S(1)}, u32[]{:S(2)}, u32[]{:S(2)}) collective-permute-start(f32[32,1024]{1,0:T(8,128)S(1)} %dynamic-slice_bitcast_fusion.3), channel_id=1, source_target_pairs={{0,8},{2,10},{4,12},{6,14},{8,0},{10,2},{12,4},{14,6},{16,24},{18,... | collective-permute-start | bytes 393224 | tf_op jit(solution)/shard_map/ppermute | solution.py:307
  90.8 5.2 %collective-permute-start.11 = (f32[32,512]{1,0:T(8,128)S(1)}, f32[32,512]{1,0:T(8,128)S(1)}, u32[]{:S(2)}, u32[]{:S(2)}) collective-permute-start(f32[32,512]{1,0:T(8,128)S(1)} %fusion.17), channel_id=1, source_target_pairs={{0,16},{2,18},{4,20},{6,22},{8,24},{10,26},{12,28},{14,30},{16,0},... | collective-permute-start | bytes 196616 | tf_op jit(solution)/shard_map/ppermute | solution.py:307
  93.3 4.0 %collective-permute-start.7 = (f32[32,512]{1,0:T(8,128)S(1)}, f32[32,512]{1,0:T(8,128)S(1)}, u32[]{:S(2)}, u32[]{:S(2)}) collective-permute-start(f32[32,512]{1,0:T(8,128)S(1)} %dynamic-slice_bitcast_fusion.5), channel_id=1, source_target_pairs={{1,17},{3,19},{5,21},{7,23},{9,25},{11,27},{13,29},{15,31},{17,1},... | collective-permute-start | bytes 196616 | tf_op jit(solution)/shard_map/ppermute | solution.py:307
  96.0 6.2 %collective-permute-start.12 = (f32[32,512]{1,0:T(8,128)S(1)}, f32[32,512]{1,0:T(8,128)S(1)}, u32[]{:S(2)}, u32[]{:S(2)}) collective-permute-start(f32[32,512]{1,0:T(8,128)S(1)} %fusion.20), channel_id=1, source_target_pairs={{1,0},{3,2},{5,4},{7,6},{9,8},{11,10},{13,12},{15,14},{17,16},{19,... | collective-permute-start | bytes 196616 | tf_op jit(solution)/shard_map/ppermute | solution.py:376

commit v3 on v2

v3 whole, which is shorter than its diff:
```python
import functools

import jax
import jax.numpy as jnp
from jax import lax
from jax.experimental import pallas as pl
from jax.experimental.pallas import tpu as pltpu
from jax.sharding import PartitionSpec as P

GROUP = 4
UNROLL = 8

ANYWHERE = pl.BlockSpec(memory_space=pl.ANY)
FAR = pl.BlockSpec(memory_space=pltpu.HBM)
NEAR = pl.BlockSpec(memory_space=pltpu.VMEM)
SCALAR = pl.BlockSpec(memory_space=pltpu.SMEM)


def contract(left, right):
    return lax.dot_general(
        left, right, (((0,), (0,)), ((), ())), preferred_element_type=jnp.float32
    )


def far(*arrays):
    return [pltpu.with_memory_space_constraint(a, pltpu.HBM) for a in arrays]


def room_for(*sizes):
    return pltpu.CompilerParams(vmem_limit_bytes=(6 << 20) + sum(sizes))


def nbytes(array):
    return array.size * array.dtype.itemsize


def near_nothing():
    return pl.CostEstimate(flops=1, bytes_accessed=1, transcendentals=0)


def columns_of(rows):
    count, width = rows.shape
    return jnp.concatenate([rows, jnp.zeros((8 - count, width), rows.dtype)], 0).T


def slot_kernel(nrows_blk, shift, n_col, live_count, index, first, owner_row, entries):
    slots = index.shape[1]
    nkeys = 2 * nrows_blk
    live = jnp.where(lax.axis_index("col") == n_col - 1, live_count[0], 0)

    def count_up(shape, axis):
        return lax.broadcasted_iota(jnp.int32, shape, axis)

    def keys_of(rows, cols):
        return rows + jnp.where(cols >= nrows_blk, nrows_blk, 0)

    def groups_of(hits, axis):
        return (jnp.sum(hits.astype(jnp.int32), axis, keepdims=True) + (GROUP - 1)) // GROUP

    across = index[...]
    down = columns_of(across)
    row_a, col_a = across[0:1], across[1:2]
    row_d, col_d = down[:, 0:1], down[:, 1:2]
    key_a, key_d = keys_of(row_a, col_a), keys_of(row_d, col_d)
    k_a, k_d = count_up((1, slots), 1), count_up((slots, 1), 0)
    alive_a, alive_d = k_a < live, k_d < live
    rank = jnp.sum(((key_a == key_d) & alive_a & (k_a < k_d)).astype(jnp.int32), 1, keepdims=True)
    groups_d = groups_of((key_a == count_up((nkeys, 1), 0)) & alive_a, 1)
    groups_a = groups_of((key_d == count_up((1, nkeys), 1)) & alive_d, 0)
    room = first.shape[1]
    first_a = jnp.sum(jnp.where(count_up((nkeys, room), 0) < count_up((nkeys, room), 1), groups_d, 0), 0, keepdims=True)
    first_d = jnp.sum(jnp.where(count_up((nkeys, nkeys), 1) < count_up((nkeys, nkeys), 0), groups_a, 0), 1, keepdims=True)
    first[...] = first_a
    started = (first_d <= count_up((nkeys, owner_row.shape[1]), 1)).astype(jnp.int32)
    key = jnp.sum(started, 0, keepdims=True) - 1
    owner_row[...] = jnp.where(key >= nrows_blk, key - nrows_blk, key)
    begin = jnp.sum(jnp.where(key_d == count_up((slots, room), 1), first_a, 0), 1, keepdims=True)
    place = begin * GROUP + rank
    value = ((k_d + 1) << shift) + col_d - jnp.where(col_d >= nrows_blk, nrows_blk, 0)
    hit = (place == count_up((slots, entries.shape[1]), 1)) & alive_d
    entries[...] = jnp.sum(jnp.where(hit, value, 0), 0, keepdims=True)


def slot_list(block_index, live_block_count, nrows_blk, shift, n_col):
    slots = block_index.shape[0]
    total = slots // GROUP + 2 * nrows_blk

    def lanes(n):
        return jax.ShapeDtypeStruct((1, -(-n // 128) * 128), jnp.int32)

    return pl.pallas_call(
        functools.partial(slot_kernel, nrows_blk, shift, n_col),
        out_shape=[lanes(2 * nrows_blk + 1), lanes(total), lanes(total * GROUP)],
        in_specs=[SCALAR, NEAR],
        out_specs=[NEAR] * 3,
        compiler_params=room_for(),
        cost_estimate=near_nothing(),
    )(live_block_count, block_index.T)


def products(lists, begin, end, row0, shift, block_of, source, acc, bsize):
    _, owner_row, entries = lists

    @pl.loop(0, (end - begin + UNROLL - 1) // UNROLL)
    def _(step):
        rows, prods = [], []
        for u in range(UNROLL):
            g = begin + step * UNROLL + u
            inside = g < end
            g = jnp.minimum(g, end - 1)
            rows.append(jnp.where(inside, owner_row[0, g] - row0, 0))
            left, right = [], []
            for j in range(GROUP):
                entry = jnp.where(inside, entries[0, g * GROUP + j], 0)
                block = block_of(g, j, entry)
                column = entry & ((1 << shift) - 1)
                left.append(jnp.where(entry > 0, block, jnp.zeros_like(block)))
                right.append(source[pl.ds(pl.multiple_of(column * bsize, bsize), bsize), :])
            prods.append(
                jnp.dot(jnp.concatenate(left, 1), jnp.concatenate(right, 0), preferred_element_type=jnp.float32)
            )
        for row, prod in zip(rows, prods):
            acc[pl.ds(pl.multiple_of(row * bsize, bsize), bsize), :] += prod


def stored(blocks, shift):
    return lambda g, j, entry: blocks[jnp.maximum((entry >> shift) - 1, 0)]


def shared_range(first, nrows_blk, row0, nrows):
    return first[0, nrows_blk + row0], first[0, nrows_blk + row0 + nrows]


def gather_kernel(send_rows, tmat, blocks, first_rows, second_rows, panel, near_blocks, picked, sem):
    depth = picked.shape[0]
    steps = panel.shape[0] // depth
    copy_blocks = pltpu.make_async_copy(blocks, near_blocks, sem.at[steps])

    def part(step):
        chunk = pl.ds(pl.multiple_of(step * depth, depth), depth)
        return pltpu.make_async_copy(tmat.at[chunk], panel.at[chunk], sem.at[step])

    for step in range(steps):
        part(step).start()
    copy_blocks.start()
    picked[...] = jnp.zeros_like(picked)
    lists = columns_of(send_rows[...])
    wanted = jnp.concatenate([lists[:, 0:1], lists[:, 1:2]], 0)

    @pl.loop(0, steps)
    def _(step):
        part(step).wait()
        begin = pl.multiple_of(step * depth, depth)
        numbers = lax.broadcasted_iota(jnp.int32, (depth, depth), 1) + begin
        picks = jnp.where(wanted == numbers, 1.0, 0.0).astype(panel.dtype)
        picked[...] += jnp.dot(picks, panel[pl.ds(begin, depth), :], preferred_element_type=jnp.float32)

    half = depth // 2
    odd = lax.axis_index("dom") % 2
    first_rows[...] = picked[pl.ds(pl.multiple_of((1 - odd) * half, half), half), :].astype(first_rows.dtype)
    second_rows[...] = picked[pl.ds(pl.multiple_of(odd * half, half), half), :].astype(second_rows.dtype)
    copy_blocks.wait()


def gather_rows(send_rows, tmat, blocks):
    width, picked = tmat.shape[1], send_rows.size
    return pl.pallas_call(
        gather_kernel,
        out_shape=[jax.ShapeDtypeStruct((picked // 2, width), tmat.dtype)] * 2
        + [jax.ShapeDtypeStruct(a.shape, a.dtype) for a in (tmat, blocks)],
        in_specs=[NEAR] + [FAR] * 2,
        out_specs=[NEAR] * 4,
        scratch_shapes=[
            pltpu.VMEM((picked, width), jnp.float32),
            pltpu.SemaphoreType.DMA((tmat.shape[0] // picked + 1,)),
        ],
        compiler_params=room_for(nbytes(tmat), nbytes(blocks), 6 * picked * width),
        cost_estimate=near_nothing(),
    )(send_rows, *far(tmat, blocks))


def own_kernel(row0, nrows, shift, bsize, first, owner_row, entries, blocks, panel, acc):
    acc[...] = jnp.zeros_like(acc)
    lists = (first, owner_row, entries)
    products(lists, first[0, row0], first[0, row0 + nrows], row0, shift, stored(blocks, shift), panel, acc, bsize)


def own_products(lists, blocks, panel, shift, row0, nrows):
    bsize, width = blocks.shape[1], panel.shape[1]
    return pl.pallas_call(
        functools.partial(own_kernel, row0, nrows, shift, bsize),
        out_shape=jax.ShapeDtypeStruct((nrows * bsize, width), jnp.float32),
        in_specs=[SCALAR] * 3 + [NEAR] * 2,
        out_specs=NEAR,
        compiler_params=room_for(4 * nrows * bsize * width),
        cost_estimate=near_nothing(),
    )(*lists, blocks, panel)


def place_halo(even, odd, halo):
    sides = even.shape[0]
    odd_partition = lax.axis_index("dom") % 2
    halo[pl.ds(pl.multiple_of((1 - odd_partition) * sides, sides), sides), :] = even[...]
    halo[pl.ds(pl.multiple_of(odd_partition * sides, sides), sides), :] = odd[...]


def pieces_kernel(nrows_blk, row0, nrows, shift, bsize, other0, n_col, first, owner_row, entries, blocks, even, odd, own, tmat, after, out, halo, acc, sem):
    panel_column = lax.axis_index("col") == n_col - 1

    @pl.when(panel_column)
    def _():
        acc[...] = own[...]
        place_halo(even, odd, halo)
        lists = (first, owner_row, entries)
        products(lists, *shared_range(first, nrows_blk, row0, nrows), row0, shift, stored(blocks, shift), halo, acc, bsize)
        out[...] = acc[...].astype(out.dtype)

    @pl.when(jnp.logical_not(panel_column))
    def _():
        copy = pltpu.make_async_copy(tmat.at[pl.ds(other0, out.shape[0])], out, sem)
        copy.start()
        copy.wait()


def piece(lists, blocks, even, odd, own, tmat, after, shift, row0, nrows, other0, n_col):
    bsize, width = blocks.shape[1], tmat.shape[1]
    size = nrows * bsize
    return pl.pallas_call(
        functools.partial(pieces_kernel, tmat.shape[0] // bsize, row0, nrows, shift, bsize, other0, n_col),
        out_shape=jax.ShapeDtypeStruct((size, width), tmat.dtype),
        in_specs=[SCALAR] * 3 + [NEAR] * 4 + [FAR, ANYWHERE],
        out_specs=NEAR,
        scratch_shapes=[
            pltpu.VMEM((2 * even.shape[0], width), tmat.dtype),
            pltpu.VMEM((size, width), jnp.float32),
            pltpu.SemaphoreType.DMA,
        ],
        compiler_params=room_for(2 * nbytes(even), 6 * size * width),
        cost_estimate=near_nothing(),
    )(*lists, blocks, even, odd, own, *far(tmat), after)


def mass_kernel(nrows_blk, row0, nrows, shift, bsize, first, owner_row, entries, blocks, panel, even, odd, after, out, halo, acc):
    lists = (first, owner_row, entries)
    acc[...] = jnp.zeros_like(acc)
    place_halo(even, odd, halo)
    block_of = stored(blocks, shift)
    products(lists, first[0, row0], first[0, row0 + nrows], row0, shift, block_of, panel, acc, bsize)
    products(lists, *shared_range(first, nrows_blk, row0, nrows), row0, shift, block_of, halo, acc, bsize)
    out[...] = acc[...].astype(out.dtype)


def known_kernel(left, right, out):
    out[...] = contract(left[...], right[...])


def known_product(left, right):
    rows, width = right.shape[0], left.shape[1]
    return pl.pallas_call(
        known_kernel,
        grid=(1,),
        out_shape=jax.ShapeDtypeStruct((width, right.shape[1]), jnp.float32),
        in_specs=[pl.BlockSpec((rows, width), lambda i: (0, 0)), pl.BlockSpec(right.shape, lambda i: (0, 0))],
        out_specs=pl.BlockSpec((width, right.shape[1]), lambda i: (0, 0)),
        compiler_params=room_for(4 * nbytes(right), 8 * width * width),
        cost_estimate=near_nothing(),
    )(left, right)


def mass_rows(lists, blocks, panel, even, odd, after, shift, row0, nrows):
    bsize, width = blocks.shape[1], panel.shape[1]
    return pl.pallas_call(
        functools.partial(mass_kernel, panel.shape[0] // bsize, row0, nrows, shift, bsize),
        out_shape=jax.ShapeDtypeStruct((nrows * bsize, width), panel.dtype),
        in_specs=[SCALAR] * 3 + [NEAR] * 4 + [ANYWHERE],
        out_specs=NEAR,
        scratch_shapes=[
            pltpu.VMEM((2 * even.shape[0], width), panel.dtype),
            pltpu.VMEM((nrows * bsize, width), jnp.float32),
        ],
        compiler_params=room_for(4 * nbytes(even), 6 * nrows * bsize * width),
        cost_estimate=near_nothing(),
    )(*lists, blocks, panel, even, odd, after)


def fold_kernel(bit, terms, *refs):
    parts, (keep, send) = refs[:terms], refs[terms:]
    mine = (lax.axis_index("dom") // bit) % 2
    for o in range(keep.shape[0]):
        for out, side in ((keep, mine), (send, 1 - mine)):
            total = parts[0][o, side]
            for part in parts[1:]:
                total += part[o, side]
            out[o] = total


def fold(bit, *parts):
    outer, _, rows, width = parts[0].shape
    half = jax.ShapeDtypeStruct((outer, rows, width), jnp.float32)
    return pl.pallas_call(
        functools.partial(fold_kernel, bit, len(parts)),
        out_shape=[half] * 2,
        in_specs=[NEAR] * len(parts),
        out_specs=[NEAR] * 2,
        compiler_params=pltpu.CompilerParams(vmem_limit_bytes=12 << 20),
        cost_estimate=near_nothing(),
    )(*parts)


def scatter(x, bits, route, beside=()):
    targets, rows, width = x.shape
    parts = (x,)
    for bit in reversed(bits):
        targets //= 2
        keep, send = fold(bit, *(p.reshape(targets, 2, rows, width) for p in parts))
        got = lax.ppermute(send, *route(bit))
        if beside and bit == bits[-2]:
            got, *beside = lax.optimization_barrier((got, *beside))
        parts = (keep, got)
    return (parts[0] + parts[1]).reshape(rows, width), *beside


def body(tmat, stored_mass_blocks, block_index, live_block_count, send_rows):
    n_col, n_dom = lax.axis_size("col"), lax.axis_size("dom")
    owner = n_col - 1
    col, dom = lax.axis_index("col"), lax.axis_index("dom")
    rows_dev, width = tmat.shape
    bsize = stored_mass_blocks.shape[1]
    nrows_blk = rows_dev // bsize
    share = width // n_dom
    shift = nrows_blk.bit_length()
    lists = slot_list(block_index, live_block_count, nrows_blk, shift, n_col)


    def exchange(block, begin):
        pairs = [(i * n_col + owner, (i + 1) * n_col + owner) for i in range(begin, n_dom - 1, 2)]
        return lax.ppermute(block, ("dom", "col"), pairs + [(b, a) for a, b in pairs])

    na = (nrows_blk * 13) // 32
    nb = nrows_blk - na
    *rows, panel, blocks = gather_rows(send_rows, tmat, stored_mass_blocks)
    even, odd = exchange(rows[0], 0), exchange(rows[1], 1)

    if n_col != 2 or n_dom < 4 or n_dom & (n_dom - 1):
        mass = mass_rows(lists, blocks, panel, even, odd, even, shift, 0, nrows_blk)
        total = lax.psum(contract(lax.psum(mass, "col"), tmat), "dom")
        return lax.dynamic_slice_in_dim(total, dom * share, share, 0)

    cut = nb * bsize
    early = cut - na * bsize
    ahead = lax.ppermute(tmat[:early], "col", [(0, 1)])

    own_a = own_products(lists, blocks, panel, shift, nb, na)
    sent = piece(lists, blocks, even, odd, own_a, tmat, ahead, shift, nb, na, early, n_col)
    got = lax.ppermute(sent, "col", [(0, 1), (1, 0)])
    mass_b = mass_rows(lists, blocks, panel, even, odd, sent, shift, 0, nb)
    own = contract(sent, tmat[cut:]) + contract(mass_b, tmat[:cut])
    known = known_product(mass_b, ahead)

    def both(bit):
        return "dom", [(i, i ^ bit) for i in range(n_dom)]

    def panel_column(bit):
        return ("dom", "col"), [(i * n_col + owner, (i ^ bit) * n_col + owner) for i in range(n_dom)]

    bits = [n_dom >> (b + 1) for b in range(n_dom.bit_length() - 1)]
    own, known = scatter(own.reshape(n_dom, share, width), bits, panel_column, (known,))
    got, own = lax.optimization_barrier((got, own))

    x = contract(jnp.where(col == owner, mass_b[early:], got), jnp.where(col == owner, got, tmat[cut:])) + known
    (x,) = scatter(x.reshape(n_dom, share, width), bits, both)
    other = x + lax.ppermute(x, "col", [(1, 0)])
    return jnp.where(col == owner, own, other)


def solution(mesh):
    return jax.shard_map(
        body,
        mesh=mesh,
        in_specs=(P("dom", "col"), P("dom", None, None), P("dom", None), P("dom"), P("dom", None)),
        out_specs=P("dom", "col"),
        check_vma=False,
    )
```

time: 103 us -> 99.9 us (0.970)
  waiting for transfers between devices: 41 us -> 56.2 us
  starting transfers between devices: 31 us -> 19.1 us
  Pallas kernels: 17.9 us -> 12.7 us
  other arithmetic: 3.65 us -> 1.54 us
  matrix products: 5.79 us -> 7.26 us
    ppermute x8, starting transfers between devices: 19.2 us -> 9.28 us  [scatter(): got = lax.ppermute(send, *route(bit))]
    ppermute x1, waiting for transfers between devices: 19 us -> 24.9 us  [body(): got = lax.ppermute(sent, 'col', [(0, 1), (1, 0)])]
    ppermute x1, waiting for transfers between devices: 4.85 us -> 8.6 us  [body(): other = x + lax.ppermute(x, 'col', [(1, 0)])]
    pallas_call x3 -> x13, Pallas kernels: 15.2 us -> 12.1 us  [the longest x1 5.08 us: gather_rows(): pl.pallas_call(gather_kernel, out_shape=[jax.ShapeDtypeStruct((picked //...]
    ppermute x1, waiting for transfers between devices: 4.52 us -> 7.4 us  [body(): ahead = lax.ppermute(tmat[:early], 'col', [(0, 1)])]
    ppermute x8, waiting for transfers between devices: 12.7 us -> 15.3 us  [scatter(): got = lax.ppermute(send, *route(bit))]
    pallas_call x1, Pallas kernels: 2.7 us -> 0.6 us  [known_product(): pl.pallas_call(known_kernel, grid=(1,), out_shape=jax.ShapeDtypeStruct((w...]
    add x9 -> x0, other arithmetic: 2.09 us -> none  [the longest x7 1.32 us: halving(): return keep + lax.ppermute(send, *route(bit))]
  transfers between devices with their start and end apart: 13 -> 13, of which waited for: 7 -> 7; matrix products, arithmetic and copies ran while one was open for 6% -> 5% of each run, Pallas kernels for 15% -> 9%
where the time goes in v3:
time: 99.9 us; the launch traced here: 100 us
  waiting for transfers between devices  56.2 us (56%)
  starting transfers between devices  19.1 us (19%)
  Pallas kernels  12.7 us (13%)
  matrix products  7.26 us (7%)
  local copies, waits for them, and re-layouts  2.49 us (2%)
  other arithmetic  1.54 us (2%)
    ppermute x1, waiting for transfers between devices, body(): got = lax.ppermute(sent, 'col', [(0, 1), (1, 0)])  24.9 us
    ppermute x8, waiting for transfers between devices, scatter(): got = lax.ppermute(send, *route(bit))  15.3 us
    ppermute x8, starting transfers between devices, scatter(): got = lax.ppermute(send, *route(bit))  9.28 us
    ppermute x1, waiting for transfers between devices, body(): other = x + lax.ppermute(x, 'col', [(1, 0)])  8.6 us
    ppermute x1, waiting for transfers between devices, body(): ahead = lax.ppermute(tmat[:early], 'col', [(0, 1)])  7.4 us
    dot_general x3, matrix products, contract(): lax.dot_general(left, right, (((0,), (0,)), ((), ())), preferred_element_...  7.26 us
    pallas_call x1, Pallas kernels, gather_rows(): pl.pallas_call(gather_kernel, out_shape=[jax.ShapeDtypeStruct((picked //...  5.08 us
    ppermute x1, starting transfers between devices, body(): ahead = lax.ppermute(tmat[:early], 'col', [(0, 1)])  4.89 us
  transfers between devices with their start and end apart: 13, of which 7 were waited for; matrix products, arithmetic and copies ran while one was open for 5% of the time, Pallas kernels for 9%

profile of v3, /device:TPU:0, one launch (start us, length us, event | category | flops | bytes accessed | tf_op | source)
XLA Modules:
  0.0 100.2 jit_solution(16817351725073163048)
XLA Ops:
  0.0 1.2 %slice.13 = bf16[768,512]{1,0:T(8,128)(2,1)S(1)} slice(bf16[4096,512]{1,0:T(8,128)(2,1)} %tmat.3), slice={[0:768], [0:512]} | slice | bytes 1572864 | tf_op jit(solution)/shard_map/slice | solution.py:351
  1.2 4.9 %collective-permute-start.2 = (bf16[768,512]{1,0:T(8,128)(2,1)S(1)}, bf16[768,512]{1,0:T(8,128)(2,1)S(1)}, u32[]{:S(2)}, u32[]{:S(2)}) collective-permute-start(bf16[768,512]{1,0:T(8,128)(2,1)S(1)} %slice.13), channel_id=1, source_target_pairs={{0,1},{2,3},{4,5},{6,7},{8,9},{10,11},{12,13},{14,15},{16,17},{18,... | collective-permute-start | bytes 2359304 | tf_op jit(solution)/shard_map/ppermute | solution.py:351
  6.1 0.7 copy-done.2
  6.8 5.1 %shard_map.56 = (bf16[256,512]{1,0:T(8,128)(2,1)S(1)}, bf16[256,512]{1,0:T(8,128)(2,1)S(1)}, bf16[4096,512]{1,0:T(8,128)(2,1)S(1)}, bf16[256,128,128]{2,1,0:T(8,128)(2,1)S(1)}) custom-call(s32[2,256]{1,0:T(2,128)S(1)} %copy-done.2, bf16[4096,512]{1,0:T(8,128)(2,1)} %tmat.3, bf16[256,128,128]{2,1,0:T(8,128)(2,1)} %blocks.1), custom_call_target="tpu_custom_call" | custom-call | flops 1 | bytes 1 | tf_op jit(solution)/shard_map/pallas_call | solution.py:167
  11.9 0.7 collective-permute-start
  12.6 0.7 collective-permute-start.1
  13.9 0.7 shard_map.55
  14.6 0.8 shard_map.57.own
  15.4 7.4 %collective-permute-done.2.after.right = bf16[768,512]{1,0:T(8,128)(2,1)S(1)} collective-permute-done((bf16[768,512]{1,0:T(8,128)(2,1)S(1)}, bf16[768,512]{1,0:T(8,128)(2,1)S(1)}, u32[]{:S(2)}, u32[]{:S(2)}) %collective-permute-start.2) | collective-permute-done | bytes 786464 | tf_op jit(solution)/shard_map/ppermute | solution.py:351
  22.8 3.3 %shard_map.58.after = bf16[1664,512]{1,0:T(8,128)(2,1)} custom-call(s32[1,128]{1,0:T(1,128)S(1)} %get-tuple-element.32.first, s32[1,128]{1,0:T(1,128)S(1)} %get-tuple-element.33.owner_row, s32[1,512]{1,0:T(1,128)S(1)} %get-tuple-element.34.entries, bf16[256,128,128]{2,1,0:T(8,128)(2,1)S(1)} %get-tuple-element.35.blocks, ...), custom_call_target="tpu_custom_call" | custom-call | flops 1 | bytes 1 | tf_op jit(solution)/shard_map/pallas_call | solution.py:228
  26.1 2.3 %collective-permute-start.3 = (bf16[1664,512]{1,0:T(8,128)(2,1)}, bf16[1664,512]{1,0:T(8,128)(2,1)}, u32[]{:S(2)}, u32[]{:S(2)}) collective-permute-start(bf16[1664,512]{1,0:T(8,128)(2,1)} %shard_map.58.after), channel_id=1, source_target_pairs={{0,1},{1,0},{2,3},{3,2},{4,5},{5,4},{6,7},{7,6},{8,9},{9,8},{10,11... | collective-permute-start | bytes 5111816 | tf_op jit(solution)/shard_map/ppermute | solution.py:355
  28.4 1.2 %shard_map.59.left = bf16[2432,512]{1,0:T(8,128)(2,1)S(1)} custom-call(s32[1,128]{1,0:T(1,128)S(1)} %get-tuple-element.32.first, s32[1,128]{1,0:T(1,128)S(1)} %get-tuple-element.33.owner_row, s32[1,512]{1,0:T(1,128)S(1)} %get-tuple-element.34.entries, bf16[256,128,128]{2,1,0:T(8,128)(2,1)S(1)} %get-tuple-element.35.blocks, ...), custom_call_target="tpu_custom_call" | custom-call | flops 1 | bytes 1 | tf_op jit(solution)/shard_map/pallas_call | solution.py:272
  29.6 1.5 %fusion = f32[512,512]{1,0:T(8,128)S(1)} fusion(bf16[2432,512]{1,0:T(8,128)(2,1)S(1)} %shard_map.59.left, bf16[4096,512]{1,0:T(8,128)(2,1)S(1)} %copy-done.3), kind=kOutput, calls=%fused_computation | convolution fusion | flops 1275068416 | bytes 6029312 | tf_op jit(solution)/shard_map/dot_general | solution.py:20
  31.1 2.6 %fusion.11 = f32[512,512]{1,0:T(8,128)S(1)} fusion(f32[512,512]{1,0:T(8,128)S(1)} %fusion, bf16[1664,512]{1,0:T(8,128)(2,1)} %shard_map.58.after, bf16[4096,512]{1,0:T(8,128)(2,1)S(1)} %copy-done.3), kind=kOutput, calls=%fused_computation.10 | convolution fusion | flops 872677376 | bytes 5505024 | tf_op jit(solution)/shard_map/dot_general | solution.py:20
  33.8 0.7 collective-permute-start.4
  34.6 0.7 collective-permute-start.5
  36.0 0.7 collective-permute-start.6
  36.7 0.7 shard_map.64
  37.9 1.3 %collective-permute-start.7 = (f32[1,32,512]{2,1,0:T(8,128)}, f32[1,32,512]{2,1,0:T(8,128)}, u32[]{:S(2)}, u32[]{:S(2)}) collective-permute-start(f32[1,32,512]{2,1,0:T(8,128)} %get-tuple-element.47), channel_id=1, source_target_pairs={{1,17},{3,19},{5,21},{7,23},{9,25},{11,27},{13,29},{15,31},{17,1},... | collective-permute-start | bytes 196616 | tf_op jit(solution)/shard_map/ppermute | solution.py:316
  39.2 0.9 add_bitcast_fusion.1
  40.1 24.9 %collective-permute-done.3 = bf16[1664,512]{1,0:T(8,128)(2,1)} collective-permute-done((bf16[1664,512]{1,0:T(8,128)(2,1)}, bf16[1664,512]{1,0:T(8,128)(2,1)}, u32[]{:S(2)}, u32[]{:S(2)}) %collective-permute-start.3) | collective-permute-done | bytes 1703968 | tf_op jit(solution)/shard_map/ppermute | solution.py:355
  65.0 3.1 %fusion.8 = f32[512,512]{1,0:T(8,128)S(1)} fusion(f32[512,512]{1,0:T(8,128)S(1)} %shard_map.62, bf16[1664,512]{1,0:T(8,128)(2,1)} %collective-permute-done.3, pred[]{:T(512)S(6)} %eq.2, bf16[4096,512]{1,0:T(8,128)(2,1)} %tmat.3, bf16[2432,512]{1,0:T(8,128)(2,1)S(1)} %shard_map.59.left), kind=kOutput, calls=%fused_computation.9 | convolution fusion | flops 874381312 | bytes 8913920 | tf_op jit(solution)/shard_map/dot_general | solution.py:20
  68.3 1.9 %collective-permute-done.8 = f32[8,32,512]{2,1,0:T(8,128)S(1)} collective-permute-done((f32[8,32,512]{2,1,0:T(8,128)S(1)}, f32[8,32,512]{2,1,0:T(8,128)S(1)}, u32[]{:S(2)}, u32[]{:S(2)}) %collective-permute-start.8) | collective-permute-done | bytes 524320 | tf_op jit(solution)/shard_map/ppermute | solution.py:316
  70.3 2.3 %collective-permute-start.9 = (f32[4,32,512]{2,1,0:T(8,128)S(1)}, f32[4,32,512]{2,1,0:T(8,128)S(1)}, u32[]{:S(2)}, u32[]{:S(2)}) collective-permute-start(f32[4,32,512]{2,1,0:T(8,128)S(1)} %get-tuple-element.54), channel_id=1, source_target_pairs={{0,4},{2,6},{4,0},{6,2},{8,12},{10,14},{12,8},{14,10},{16,20},{18,... | collective-permute-start | bytes 786440 | tf_op jit(solution)/shard_map/ppermute | solution.py:316
  72.6 6.6 %collective-permute-done.9 = f32[4,32,512]{2,1,0:T(8,128)S(1)} collective-permute-done((f32[4,32,512]{2,1,0:T(8,128)S(1)}, f32[4,32,512]{2,1,0:T(8,128)S(1)}, u32[]{:S(2)}, u32[]{:S(2)}) %collective-permute-start.9) | collective-permute-done | bytes 262176 | tf_op jit(solution)/shard_map/ppermute | solution.py:316
  79.3 1.3 %collective-permute-start.10 = (f32[2,32,512]{2,1,0:T(8,128)S(1)}, f32[2,32,512]{2,1,0:T(8,128)S(1)}, u32[]{:S(2)}, u32[]{:S(2)}) collective-permute-start(f32[2,32,512]{2,1,0:T(8,128)S(1)} %get-tuple-element.56), channel_id=1, source_target_pairs={{0,8},{2,10},{4,12},{6,14},{8,0},{10,2},{12,4},{14,6},{16,24},{18,... | collective-permute-start | bytes 393224 | tf_op jit(solution)/shard_map/ppermute | solution.py:316
  80.6 3.8 %collective-permute-done.10 = f32[2,32,512]{2,1,0:T(8,128)S(1)} collective-permute-done((f32[2,32,512]{2,1,0:T(8,128)S(1)}, f32[2,32,512]{2,1,0:T(8,128)S(1)}, u32[]{:S(2)}, u32[]{:S(2)}) %collective-permute-start.10) | collective-permute-done | bytes 131104 | tf_op jit(solution)/shard_map/ppermute | solution.py:316
  84.4 2.3 %collective-permute-start.11 = (f32[1,32,512]{2,1,0:T(8,128)S(1)}, f32[1,32,512]{2,1,0:T(8,128)S(1)}, u32[]{:S(2)}, u32[]{:S(2)}) collective-permute-start(f32[1,32,512]{2,1,0:T(8,128)S(1)} %get-tuple-element.58), channel_id=1, source_target_pairs={{0,16},{2,18},{4,20},{6,22},{8,24},{10,26},{12,28},{14,30},{16,0},... | collective-permute-start | bytes 196616 | tf_op jit(solution)/shard_map/ppermute | solution.py:316
  86.6 3.0 %collective-permute-done.11 = f32[1,32,512]{2,1,0:T(8,128)S(1)} collective-permute-done((f32[1,32,512]{2,1,0:T(8,128)S(1)}, f32[1,32,512]{2,1,0:T(8,128)S(1)}, u32[]{:S(2)}, u32[]{:S(2)}) %collective-permute-start.11) | collective-permute-done | bytes 65568 | tf_op jit(solution)/shard_map/ppermute | solution.py:316
  89.6 1.3 %collective-permute-start.12 = (f32[32,512]{1,0:T(8,128)S(1)}, f32[32,512]{1,0:T(8,128)S(1)}, u32[]{:S(2)}, u32[]{:S(2)}) collective-permute-start(f32[32,512]{1,0:T(8,128)S(1)} %add_bitcast_fusion), channel_id=1, source_target_pairs={{1,0},{3,2},{5,4},{7,6},{9,8},{11,10},{13,12},{15,14},{17,16},{19,... | collective-permute-start | bytes 196616 | tf_op jit(solution)/shard_map/ppermute | solution.py:372
  90.9 8.6 %collective-permute-done.12 = f32[32,512]{1,0:T(8,128)S(1)} collective-permute-done((f32[32,512]{1,0:T(8,128)S(1)}, f32[32,512]{1,0:T(8,128)S(1)}, u32[]{:S(2)}, u32[]{:S(2)}) %collective-permute-start.12) | collective-permute-done | bytes 65568 | tf_op jit(solution)/shard_map/ppermute | solution.py:372
  99.5 0.6 add_select_fusion
  (23 shorter events, 1.7 us)
Async XLA Ops:
  1.2 12.7 %copy-start.1 = (s32[256,2]{0,1:T(2,128)S(1)}, s32[256,2]{0,1:T(2,128)}, u32[]{:S(2)}) copy-start(s32[256,2]{0,1:T(2,128)} %param.7) | copy-start | bytes 6148
  1.2 21.6 %collective-permute-start.2 = (bf16[768,512]{1,0:T(8,128)(2,1)S(1)}, bf16[768,512]{1,0:T(8,128)(2,1)S(1)}, u32[]{:S(2)}, u32[]{:S(2)}) collective-permute-start(bf16[768,512]{1,0:T(8,128)(2,1)S(1)} %slice.13), channel_id=1, source_target_pairs={{0,1},{2,3},{4,5},{6,7},{8,9},{10,11},{12,13},{14,15},{16,17},{18,... | collective-permute-start | bytes 2359304 | tf_op jit(solution)/shard_map/ppermute | solution.py:351
  6.1 0.7 copy-start.2
  11.9 3.5 %collective-permute-start = (bf16[256,512]{1,0:T(8,128)(2,1)S(1)}, bf16[256,512]{1,0:T(8,128)(2,1)S(1)}, u32[]{:S(2)}, u32[]{:S(2)}) collective-permute-start(bf16[256,512]{1,0:T(8,128)(2,1)S(1)} %get-tuple-element.36), channel_id=1, source_target_pairs={{1,3},{5,7},{9,11},{13,15},{17,19},{21,23},{25,27},{29,31},{3,1},{... | collective-permute-start | bytes 786440 | tf_op jit(solution)/shard_map/ppermute | solution.py:337
  12.6 2.9 %collective-permute-start.1 = (bf16[256,512]{1,0:T(8,128)(2,1)S(1)}, bf16[256,512]{1,0:T(8,128)(2,1)S(1)}, u32[]{:S(2)}, u32[]{:S(2)}) collective-permute-start(bf16[256,512]{1,0:T(8,128)(2,1)S(1)} %get-tuple-element.37), channel_id=1, source_target_pairs={{3,5},{7,9},{11,13},{15,17},{19,21},{23,25},{27,29},{5,3},{9,7},{1... | collective-permute-start | bytes 786440 | tf_op jit(solution)/shard_map/ppermute | solution.py:337
  26.1 3.5 %copy-start.3 = (bf16[4096,512]{1,0:T(8,128)(2,1)S(1)}, bf16[4096,512]{1,0:T(8,128)(2,1)}, u32[]{:S(2)}) copy-start(bf16[4096,512]{1,0:T(8,128)(2,1)} %tmat.3) | copy-start | bytes 12582916
  26.1 38.9 %collective-permute-start.3 = (bf16[1664,512]{1,0:T(8,128)(2,1)}, bf16[1664,512]{1,0:T(8,128)(2,1)}, u32[]{:S(2)}, u32[]{:S(2)}) collective-permute-start(bf16[1664,512]{1,0:T(8,128)(2,1)} %shard_map.58.after), channel_id=1, source_target_pairs={{0,1},{1,0},{2,3},{3,2},{4,5},{5,4},{6,7},{7,6},{8,9},{9,8},{10,11... | collective-permute-start | bytes 5111816 | tf_op jit(solution)/shard_map/ppermute | solution.py:355
  33.8 0.7 collective-permute-start.4
  34.6 1.3 %collective-permute-start.5 = (f32[4,32,512]{2,1,0:T(8,128)S(1)}, f32[4,32,512]{2,1,0:T(8,128)S(1)}, u32[]{:S(2)}, u32[]{:S(2)}) collective-permute-start(f32[4,32,512]{2,1,0:T(8,128)S(1)} %get-tuple-element.42), channel_id=1, source_target_pairs={{1,5},{3,7},{5,1},{7,3},{9,13},{11,15},{13,9},{15,11},{17,21},{19,... | collective-permute-start | bytes 786440 | tf_op jit(solution)/shard_map/ppermute | solution.py:316
  36.0 0.7 collective-permute-start.6
  37.3 0.6 copy-start
  37.9 1.3 %collective-permute-start.7 = (f32[1,32,512]{2,1,0:T(8,128)}, f32[1,32,512]{2,1,0:T(8,128)}, u32[]{:S(2)}, u32[]{:S(2)}) collective-permute-start(f32[1,32,512]{2,1,0:T(8,128)} %get-tuple-element.47), channel_id=1, source_target_pairs={{1,17},{3,19},{5,21},{7,23},{9,25},{11,27},{13,29},{15,31},{17,1},... | collective-permute-start | bytes 196616 | tf_op jit(solution)/shard_map/ppermute | solution.py:316
  68.3 2.0 %collective-permute-start.8 = (f32[8,32,512]{2,1,0:T(8,128)S(1)}, f32[8,32,512]{2,1,0:T(8,128)S(1)}, u32[]{:S(2)}, u32[]{:S(2)}) collective-permute-start(f32[8,32,512]{2,1,0:T(8,128)S(1)} %get-tuple-element.52), channel_id=1, source_target_pairs={{0,2},{2,0},{4,6},{6,4},{8,10},{10,8},{12,14},{14,12},{16,18},{18,... | collective-permute-start | bytes 1572872 | tf_op jit(solution)/shard_map/ppermute | solution.py:316
  70.3 8.9 %collective-permute-start.9 = (f32[4,32,512]{2,1,0:T(8,128)S(1)}, f32[4,32,512]{2,1,0:T(8,128)S(1)}, u32[]{:S(2)}, u32[]{:S(2)}) collective-permute-start(f32[4,32,512]{2,1,0:T(8,128)S(1)} %get-tuple-element.54), channel_id=1, source_target_pairs={{0,4},{2,6},{4,0},{6,2},{8,12},{10,14},{12,8},{14,10},{16,20},{18,... | collective-permute-start | bytes 786440 | tf_op jit(solution)/shard_map/ppermute | solution.py:316
  79.3 5.1 %collective-permute-start.10 = (f32[2,32,512]{2,1,0:T(8,128)S(1)}, f32[2,32,512]{2,1,0:T(8,128)S(1)}, u32[]{:S(2)}, u32[]{:S(2)}) collective-permute-start(f32[2,32,512]{2,1,0:T(8,128)S(1)} %get-tuple-element.56), channel_id=1, source_target_pairs={{0,8},{2,10},{4,12},{6,14},{8,0},{10,2},{12,4},{14,6},{16,24},{18,... | collective-permute-start | bytes 393224 | tf_op jit(solution)/shard_map/ppermute | solution.py:316
  84.4 5.2 %collective-permute-start.11 = (f32[1,32,512]{2,1,0:T(8,128)S(1)}, f32[1,32,512]{2,1,0:T(8,128)S(1)}, u32[]{:S(2)}, u32[]{:S(2)}) collective-permute-start(f32[1,32,512]{2,1,0:T(8,128)S(1)} %get-tuple-element.58), channel_id=1, source_target_pairs={{0,16},{2,18},{4,20},{6,22},{8,24},{10,26},{12,28},{14,30},{16,0},... | collective-permute-start | bytes 196616 | tf_op jit(solution)/shard_map/ppermute | solution.py:316
  89.6 9.9 %collective-permute-start.12 = (f32[32,512]{1,0:T(8,128)S(1)}, f32[32,512]{1,0:T(8,128)S(1)}, u32[]{:S(2)}, u32[]{:S(2)}) collective-permute-start(f32[32,512]{1,0:T(8,128)S(1)} %add_bitcast_fusion), channel_id=1, source_target_pairs={{1,0},{3,2},{5,4},{7,6},{9,8},{11,10},{13,12},{15,14},{17,16},{19,... | collective-permute-start | bytes 196616 | tf_op jit(solution)/shard_map/ppermute | solution.py:372

commit v4 on v3

--- a/solution.py
+++ b/solution.py
@@ -132,7 +132,8 @@
 
 
 def gather_kernel(send_rows, tmat, blocks, first_rows, second_rows, panel, near_blocks, picked, sem):
-    depth = picked.shape[0]
+    count = picked.shape[0]
+    depth = 2 * count
     steps = panel.shape[0] // depth
     copy_blocks = pltpu.make_async_copy(blocks, near_blocks, sem.at[steps])
 
@@ -151,11 +152,11 @@
     def _(step):
         part(step).wait()
         begin = pl.multiple_of(step * depth, depth)
-        numbers = lax.broadcasted_iota(jnp.int32, (depth, depth), 1) + begin
+        numbers = lax.broadcasted_iota(jnp.int32, (count, depth), 1) + begin
         picks = jnp.where(wanted == numbers, 1.0, 0.0).astype(panel.dtype)
         picked[...] += jnp.dot(picks, panel[pl.ds(begin, depth), :], preferred_element_type=jnp.float32)
 
-    half = depth // 2
+    half = count // 2
     odd = lax.axis_index("dom") % 2
     first_rows[...] = picked[pl.ds(pl.multiple_of((1 - odd) * half, half), half), :].astype(first_rows.dtype)
     second_rows[...] = picked[pl.ds(pl.multiple_of(odd * half, half), half), :].astype(second_rows.dtype)
@@ -172,7 +173,7 @@
         out_specs=[NEAR] * 4,
         scratch_shapes=[
             pltpu.VMEM((picked, width), jnp.float32),
-            pltpu.SemaphoreType.DMA((tmat.shape[0] // picked + 1,)),
+            pltpu.SemaphoreType.DMA((tmat.shape[0] // (2 * picked) + 1,)),
         ],
         compiler_params=room_for(nbytes(tmat), nbytes(blocks), 6 * picked * width),
         cost_estimate=near_nothing(),
@@ -204,7 +205,7 @@
     halo[pl.ds(pl.multiple_of(odd_partition * sides, sides), sides), :] = odd[...]
 
 
-def pieces_kernel(nrows_blk, row0, nrows, shift, bsize, other0, n_col, first, owner_row, entries, blocks, even, odd, own, tmat, after, out, halo, acc, sem):
+def pieces_kernel(nrows_blk, row0, nrows, shift, bsize, other0, n_col, first, owner_row, entries, blocks, odd, even, own, tmat, out, halo, acc, sem):
     panel_column = lax.axis_index("col") == n_col - 1
 
     @pl.when(panel_column)
@@ -222,13 +223,13 @@
         copy.wait()
 
 
-def piece(lists, blocks, even, odd, own, tmat, after, shift, row0, nrows, other0, n_col):
+def piece(lists, blocks, odd, even, own, tmat, shift, row0, nrows, other0, n_col):
     bsize, width = blocks.shape[1], tmat.shape[1]
     size = nrows * bsize
     return pl.pallas_call(
         functools.partial(pieces_kernel, tmat.shape[0] // bsize, row0, nrows, shift, bsize, other0, n_col),
         out_shape=jax.ShapeDtypeStruct((size, width), tmat.dtype),
-        in_specs=[SCALAR] * 3 + [NEAR] * 4 + [FAR, ANYWHERE],
+        in_specs=[SCALAR] * 3 + [NEAR] * 4 + [FAR],
         out_specs=NEAR,
         scratch_shapes=[
             pltpu.VMEM((2 * even.shape[0], width), tmat.dtype),
@@ -237,10 +238,10 @@
         ],
         compiler_params=room_for(2 * nbytes(even), 6 * size * width),
         cost_estimate=near_nothing(),
-    )(*lists, blocks, even, odd, own, *far(tmat), after)
-
-
-def mass_kernel(nrows_blk, row0, nrows, shift, bsize, first, owner_row, entries, blocks, panel, even, odd, after, out, halo, acc):
+    )(*lists, blocks, odd, even, own, *far(tmat))
+
+
+def mass_kernel(nrows_blk, row0, nrows, shift, bsize, first, owner_row, entries, blocks, panel, odd, even, after, out, halo, acc):
     lists = (first, owner_row, entries)
     acc[...] = jnp.zeros_like(acc)
     place_halo(even, odd, halo)
@@ -267,57 +268,69 @@
     )(left, right)
 
 
-def mass_rows(lists, blocks, panel, even, odd, after, shift, row0, nrows):
+def mass_rows(lists, blocks, panel, odd, even, after, shift, row0, nrows):
     bsize, width = blocks.shape[1], panel.shape[1]
     return pl.pallas_call(
         functools.partial(mass_kernel, panel.shape[0] // bsize, row0, nrows, shift, bsize),
         out_shape=jax.ShapeDtypeStruct((nrows * bsize, width), panel.dtype),
-        in_specs=[SCALAR] * 3 + [NEAR] * 4 + [ANYWHERE],
+        in_specs=[SCALAR] * 3 + [NEAR] * 5,
         out_specs=NEAR,
         scratch_shapes=[
             pltpu.VMEM((2 * even.shape[0], width), panel.dtype),
             pltpu.VMEM((nrows * bsize, width), jnp.float32),
         ],
-        compiler_params=room_for(4 * nbytes(even), 6 * nrows * bsize * width),
-        cost_estimate=near_nothing(),
-    )(*lists, blocks, panel, even, odd, after)
-
-
-def fold_kernel(bit, terms, *refs):
-    parts, (keep, send) = refs[:terms], refs[terms:]
+        compiler_params=room_for(4 * nbytes(even), 6 * nrows * bsize * width, nbytes(after)),
+        cost_estimate=near_nothing(),
+    )(*lists, blocks, panel, odd, even, after)
+
+
+def fold_kernel(bit, inner, counts, *refs):
+    keep, send = refs[-2:]
     mine = (lax.axis_index("dom") // bit) % 2
-    for o in range(keep.shape[0]):
+    for t in range(keep.shape[0]):
+        outer, rest = divmod(t, inner)
         for out, side in ((keep, mine), (send, 1 - mine)):
-            total = parts[0][o, side]
-            for part in parts[1:]:
-                total += part[o, side]
-            out[o] = total
-
-
-def fold(bit, *parts):
-    outer, _, rows, width = parts[0].shape
-    half = jax.ShapeDtypeStruct((outer, rows, width), jnp.float32)
-    return pl.pallas_call(
-        functools.partial(fold_kernel, bit, len(parts)),
+            place = (2 * outer + side) * inner + rest
+            sources, col = refs[:-2], 0
+            for count, begin, width in counts:
+                cols = pl.ds(begin, width)
+                total = sources[0][place, :, cols]
+                for part in sources[1:count]:
+                    total += part[place, :, cols]
+                out[t, :, pl.ds(col, width)] = total
+                sources, col = sources[count:], col + width
+
+
+def fold(bit, inner, *columns):
+    targets, rows, _ = columns[0][0][0].shape
+    half = jax.ShapeDtypeStruct((targets // 2, rows, sum(width for _, _, width in columns)), jnp.float32)
+    arrays = [a for some, _, _ in columns for a in some]
+    return pl.pallas_call(
+        functools.partial(fold_kernel, bit, inner, [(len(some), begin, width) for some, begin, width in columns]),
         out_shape=[half] * 2,
-        in_specs=[NEAR] * len(parts),
+        in_specs=[NEAR] * len(arrays),
         out_specs=[NEAR] * 2,
-        compiler_params=pltpu.CompilerParams(vmem_limit_bytes=12 << 20),
-        cost_estimate=near_nothing(),
-    )(*parts)
-
-
-def scatter(x, bits, route, beside=()):
+        compiler_params=room_for(),
+        cost_estimate=near_nothing(),
+    )(*arrays)
+
+
+def step(route, bit, inner, *columns):
+    keep, send = fold(bit, inner, *columns)
+    return [keep, lax.ppermute(send, *route(bit))]
+
+
+def scatter(x, route):
     targets, rows, width = x.shape
-    parts = (x,)
-    for bit in reversed(bits):
-        targets //= 2
-        keep, send = fold(bit, *(p.reshape(targets, 2, rows, width) for p in parts))
-        got = lax.ppermute(send, *route(bit))
-        if beside and bit == bits[-2]:
-            got, *beside = lax.optimization_barrier((got, *beside))
-        parts = (keep, got)
-    return (parts[0] + parts[1]).reshape(rows, width), *beside
+    half = width // 2
+    whole = step(route, 1, 1, ([x], 0, width))
+    left, right = step(route, 2, 1, (whole, 0, half)), step(route, 4, 2, (whole, half, half))
+    left, right = step(route, 4, 1, (left, 0, half)), step(route, 2, 1, (right, 0, half))
+    bit, columns = 8, [(left, 0, half), (right, 0, half)]
+    while bit < targets:
+        columns = [(step(route, bit, 1, *columns), 0, width)]
+        bit *= 2
+    return jnp.concatenate([a + b for (a, b), _, _ in columns], 2).reshape(rows, width)
 
 
 def body(tmat, stored_mass_blocks, block_index, live_block_count, send_rows):
@@ -341,8 +354,8 @@
     *rows, panel, blocks = gather_rows(send_rows, tmat, stored_mass_blocks)
     even, odd = exchange(rows[0], 0), exchange(rows[1], 1)
 
-    if n_col != 2 or n_dom < 4 or n_dom & (n_dom - 1):
-        mass = mass_rows(lists, blocks, panel, even, odd, even, shift, 0, nrows_blk)
+    if n_col != 2 or n_dom < 8 or n_dom & (n_dom - 1):
+        mass = mass_rows(lists, blocks, panel, odd, even, even, shift, 0, nrows_blk)
         total = lax.psum(contract(lax.psum(mass, "col"), tmat), "dom")
         return lax.dynamic_slice_in_dim(total, dom * share, share, 0)
 
@@ -351,10 +364,11 @@
     ahead = lax.ppermute(tmat[:early], "col", [(0, 1)])
 
     own_a = own_products(lists, blocks, panel, shift, nb, na)
-    sent = piece(lists, blocks, even, odd, own_a, tmat, ahead, shift, nb, na, early, n_col)
+    sent = piece(lists, blocks, odd, even, own_a, tmat, shift, nb, na, early, n_col)
+    sent, ahead = lax.optimization_barrier((sent, ahead))
     got = lax.ppermute(sent, "col", [(0, 1), (1, 0)])
-    mass_b = mass_rows(lists, blocks, panel, even, odd, sent, shift, 0, nb)
-    own = contract(sent, tmat[cut:]) + contract(mass_b, tmat[:cut])
+    mass_b = mass_rows(lists, blocks, panel, odd, even, sent, shift, 0, nb)
+    own = contract(sent, panel[cut:]) + contract(mass_b, panel[:cut])
     known = known_product(mass_b, ahead)
 
     def both(bit):
@@ -363,12 +377,18 @@
     def panel_column(bit):
         return ("dom", "col"), [(i * n_col + owner, (i ^ bit) * n_col + owner) for i in range(n_dom)]
 
-    bits = [n_dom >> (b + 1) for b in range(n_dom.bit_length() - 1)]
-    own, known = scatter(own.reshape(n_dom, share, width), bits, panel_column, (known,))
-    got, own = lax.optimization_barrier((got, own))
-
-    x = contract(jnp.where(col == owner, mass_b[early:], got), jnp.where(col == owner, got, tmat[cut:])) + known
-    (x,) = scatter(x.reshape(n_dom, share, width), bits, both)
+    parts, bit = [own.reshape(n_dom, share, width)], 1
+    while bit < n_dom // 2:
+        parts = step(panel_column, bit, 1, (parts, 0, width))
+        if bit == 2:
+            parts[1], known = lax.optimization_barrier((parts[1], known))
+        bit *= 2
+    got, parts[1] = lax.optimization_barrier((got, parts[1]))
+    parts = step(panel_column, bit, 1, (parts, 0, width))
+    own = (parts[0] + parts[1]).reshape(share, width)
+
+    x = contract(jnp.where(col == owner, mass_b[early:], got), jnp.where(col == owner, got, panel[cut:])) + known
+    x = scatter(x.reshape(n_dom, share, width), both)
     other = x + lax.ppermute(x, "col", [(1, 0)])
     return jnp.where(col == owner, own, other)
 

time: 99.9 us -> 92.3 us (0.924)
  waiting for transfers between devices: 56.2 us -> 45.8 us
  starting transfers between devices: 19.1 us -> 21.2 us
  Pallas kernels: 12.7 us -> 14.2 us
    ppermute x8 -> x10, waiting for transfers between devices: 15.3 us -> 10.7 us  [step(): return [keep, lax.ppermute(send, *route(bit))]]
    ppermute x1, waiting for transfers between devices: 8.6 us -> 4.85 us  [body(): other = x + lax.ppermute(x, 'col', [(1, 0)])]
    ppermute x1, waiting for transfers between devices: 7.4 us -> 4.43 us  [body(): ahead = lax.ppermute(tmat[:early], 'col', [(0, 1)])]
    ppermute x8 -> x10, starting transfers between devices: 9.28 us -> 11.2 us  [step(): return [keep, lax.ppermute(send, *route(bit))]]
  transfers between devices with their start and end apart: 13 -> 15, of which waited for: 7 -> 8; matrix products, arithmetic and copies ran while one was open for 5% -> 4% of each run, Pallas kernels for 9% -> 15%
where the time goes in v4:
time: 92.3 us; the launch traced here: 92.5 us
  waiting for transfers between devices  45.8 us (50%)
  starting transfers between devices  21.2 us (23%)
  Pallas kernels  14.2 us (15%)
  matrix products  7.26 us (8%)
  local copies, waits for them, and re-layouts  2.52 us (3%)
  between operations  0.95 us (1%)
    ppermute x1, waiting for transfers between devices, body(): got = lax.ppermute(sent, 'col', [(0, 1), (1, 0)])  25.8 us
    ppermute x10, starting transfers between devices, step(): return [keep, lax.ppermute(send, *route(bit))]  11.2 us
    ppermute x10, waiting for transfers between devices, step(): return [keep, lax.ppermute(send, *route(bit))]  10.7 us
    dot_general x3, matrix products, contract(): lax.dot_general(left, right, (((0,), (0,)), ((), ())), preferred_element_...  7.26 us
    ppermute x1, starting transfers between devices, body(): ahead = lax.ppermute(tmat[:early], 'col', [(0, 1)])  4.89 us
    ppermute x1, waiting for transfers between devices, body(): other = x + lax.ppermute(x, 'col', [(1, 0)])  4.85 us
    pallas_call x1, Pallas kernels, gather_rows(): pl.pallas_call(gather_kernel, out_shape=[jax.ShapeDtypeStruct((picked //...  4.75 us
    ppermute x1, waiting for transfers between devices, body(): ahead = lax.ppermute(tmat[:early], 'col', [(0, 1)])  4.43 us
  transfers between devices with their start and end apart: 15, of which 8 were waited for; matrix products, arithmetic and copies ran while one was open for 4% of the time, Pallas kernels for 15%

profile of v4, /device:TPU:0, one launch (start us, length us, event | category | flops | bytes accessed | tf_op | source)
XLA Modules:
  0.0 92.5 jit_solution(2097753374673049036)
XLA Ops:
  0.0 1.2 %slice.13 = bf16[768,512]{1,0:T(8,128)(2,1)S(1)} slice(bf16[4096,512]{1,0:T(8,128)(2,1)} %tmat.3), slice={[0:768], [0:512]} | slice | bytes 1572864 | tf_op jit(solution)/shard_map/slice | solution.py:364
  1.2 4.9 %collective-permute-start.2 = (bf16[768,512]{1,0:T(8,128)(2,1)S(1)}, bf16[768,512]{1,0:T(8,128)(2,1)S(1)}, u32[]{:S(2)}, u32[]{:S(2)}) collective-permute-start(bf16[768,512]{1,0:T(8,128)(2,1)S(1)} %slice.13), channel_id=1, source_target_pairs={{0,1},{2,3},{4,5},{6,7},{8,9},{10,11},{12,13},{14,15},{16,17},{18,... | collective-permute-start | bytes 2359304 | tf_op jit(solution)/shard_map/ppermute | solution.py:364
  6.1 0.7 copy-done.4
  6.8 4.7 %shard_map.56 = (bf16[256,512]{1,0:T(8,128)(2,1)S(1)}, bf16[256,512]{1,0:T(8,128)(2,1)S(1)}, bf16[4096,512]{1,0:T(8,128)(2,1)S(1)}, bf16[256,128,128]{2,1,0:T(8,128)(2,1)S(1)}) custom-call(s32[2,256]{1,0:T(2,128)S(1)} %copy-done.4, bf16[4096,512]{1,0:T(8,128)(2,1)} %tmat.3, bf16[256,128,128]{2,1,0:T(8,128)(2,1)} %blocks.1), custom_call_target="tpu_custom_call" | custom-call | flops 1 | bytes 1 | tf_op jit(solution)/shard_map/pallas_call | solution.py:168
  11.6 0.7 collective-permute-start
  12.2 0.7 collective-permute-start.1
  13.6 0.7 shard_map.55
  14.3 0.8 shard_map.57.own
  15.1 3.2 %shard_map.58.after = bf16[1664,512]{1,0:T(8,128)(2,1)} custom-call(s32[1,128]{1,0:T(1,128)S(1)} %get-tuple-element.38.first, s32[1,128]{1,0:T(1,128)S(1)} %get-tuple-element.39.owner_row, s32[1,512]{1,0:T(1,128)S(1)} %get-tuple-element.40.entries, bf16[256,128,128]{2,1,0:T(8,128)(2,1)S(1)} %get-tuple-element.41.blocks, ...), custom_call_target="tpu_custom_call" | custom-call | flops 1 | bytes 1 | tf_op jit(solution)/shard_map/pallas_call | solution.py:229
  18.4 4.4 %collective-permute-done.2.right = bf16[768,512]{1,0:T(8,128)(2,1)S(1)} collective-permute-done((bf16[768,512]{1,0:T(8,128)(2,1)S(1)}, bf16[768,512]{1,0:T(8,128)(2,1)S(1)}, u32[]{:S(2)}, u32[]{:S(2)}) %collective-permute-start.2) | collective-permute-done | bytes 786464 | tf_op jit(solution)/shard_map/ppermute | solution.py:364
  22.8 2.5 %collective-permute-start.5 = (bf16[1664,512]{1,0:T(8,128)(2,1)}, bf16[1664,512]{1,0:T(8,128)(2,1)}, u32[]{:S(2)}, u32[]{:S(2)}) collective-permute-start(bf16[1664,512]{1,0:T(8,128)(2,1)} %shard_map.58.after), channel_id=1, source_target_pairs={{0,1},{1,0},{2,3},{3,2},{4,5},{5,4},{6,7},{7,6},{8,9},{9,8},{10,11... | collective-permute-start | bytes 5111816 | tf_op jit(solution)/shard_map/ppermute | solution.py:369
  25.3 2.1 %shard_map.59.left = bf16[2432,512]{1,0:T(8,128)(2,1)S(1)} custom-call(s32[1,128]{1,0:T(1,128)S(1)} %get-tuple-element.38.first, s32[1,128]{1,0:T(1,128)S(1)} %get-tuple-element.39.owner_row, s32[1,512]{1,0:T(1,128)S(1)} %get-tuple-element.40.entries, bf16[256,128,128]{2,1,0:T(8,128)(2,1)S(1)} %get-tuple-element.41.blocks, ...), custom_call_target="tpu_custom_call" | custom-call | flops 1 | bytes 1 | tf_op jit(solution)/shard_map/pallas_call | solution.py:273
  27.4 1.5 %fusion = f32[512,512]{1,0:T(8,128)S(1)} fusion(bf16[2432,512]{1,0:T(8,128)(2,1)S(1)} %shard_map.59.left, bf16[4096,512]{1,0:T(8,128)(2,1)S(1)} %get-tuple-element.44.panel), kind=kOutput, calls=%fused_computation | convolution fusion | flops 1275068416 | bytes 6029312 | tf_op jit(solution)/shard_map/dot_general | solution.py:20
  29.0 2.6 %fusion.11 = f32[512,512]{1,0:T(8,128)S(1)} fusion(f32[512,512]{1,0:T(8,128)S(1)} %fusion, bf16[1664,512]{1,0:T(8,128)(2,1)} %shard_map.58.after, bf16[4096,512]{1,0:T(8,128)(2,1)S(1)} %get-tuple-element.44.panel), kind=kOutput, calls=%fused_computation.10 | convolution fusion | flops 872677376 | bytes 5505024 | tf_op jit(solution)/shard_map/dot_general | solution.py:20
  31.7 0.7 collective-permute-start.3
  32.5 0.7 collective-permute-start.4
  33.8 0.7 shard_map.63
  35.1 1.3 %collective-permute-start.6 = (f32[2,32,512]{2,1,0:T(8,128)}, f32[2,32,512]{2,1,0:T(8,128)}, u32[]{:S(2)}, u32[]{:S(2)}) collective-permute-start(f32[2,32,512]{2,1,0:T(8,128)} %get-tuple-element.53), channel_id=1, source_target_pairs={{1,9},{3,11},{5,13},{7,15},{9,1},{11,3},{13,5},{15,7},{17,25},{19,... | collective-permute-start | bytes 393224 | tf_op jit(solution)/shard_map/ppermute | solution.py:320
  36.5 25.8 %collective-permute-done.5 = bf16[1664,512]{1,0:T(8,128)(2,1)} collective-permute-done((bf16[1664,512]{1,0:T(8,128)(2,1)}, bf16[1664,512]{1,0:T(8,128)(2,1)}, u32[]{:S(2)}, u32[]{:S(2)}) %collective-permute-start.5) | collective-permute-done | bytes 1703968 | tf_op jit(solution)/shard_map/ppermute | solution.py:369
  62.2 3.1 %fusion.8 = f32[512,512]{1,0:T(8,128)S(1)} fusion(f32[512,512]{1,0:T(8,128)S(1)} %shard_map.62, bf16[1664,512]{1,0:T(8,128)(2,1)} %collective-permute-done.5, pred[]{:T(512)S(6)} %eq.2, bf16[4096,512]{1,0:T(8,128)(2,1)} %copy-done, bf16[2432,512]{1,0:T(8,128)(2,1)S(1)} %shard_map.59.left), kind=kOutput, calls=%fused_computation.9 | convolution fusion | flops 874381312 | bytes 8913920 | tf_op jit(solution)/shard_map/dot_general | solution.py:20
  65.5 1.9 %collective-permute-done.8.refs_1_ = f32[8,32,512]{2,1,0:T(8,128)S(1)} collective-permute-done((f32[8,32,512]{2,1,0:T(8,128)S(1)}, f32[8,32,512]{2,1,0:T(8,128)S(1)}, u32[]{:S(2)}, u32[]{:S(2)}) %collective-permute-start.8) | collective-permute-done | bytes 524320 | tf_op jit(solution)/shard_map/ppermute | solution.py:320
  67.5 1.7 %collective-permute-start.11 = (f32[4,32,256]{2,1,0:T(8,128)S(1)}, f32[4,32,256]{2,1,0:T(8,128)S(1)}, u32[]{:S(2)}, u32[]{:S(2)}) collective-permute-start(f32[4,32,256]{2,1,0:T(8,128)S(1)} %get-tuple-element.66), channel_id=1, source_target_pairs={{0,8},{2,10},{4,12},{6,14},{8,0},{10,2},{12,4},{14,6},{16,24},{18,... | collective-permute-start | bytes 393224 | tf_op jit(solution)/shard_map/ppermute | solution.py:320
  69.3 1.2 %collective-permute-start.9 = (f32[4,32,256]{2,1,0:T(8,128)S(1)}, f32[4,32,256]{2,1,0:T(8,128)S(1)}, u32[]{:S(2)}, u32[]{:S(2)}) collective-permute-start(f32[4,32,256]{2,1,0:T(8,128)S(1)} %get-tuple-element.62), channel_id=1, source_target_pairs={{0,4},{2,6},{4,0},{6,2},{8,12},{10,14},{12,8},{14,10},{16,20},{18,... | collective-permute-start | bytes 393224 | tf_op jit(solution)/shard_map/ppermute | solution.py:320
  70.5 2.6 %collective-permute-done.11.refs_1_ = f32[4,32,256]{2,1,0:T(8,128)S(1)} collective-permute-done((f32[4,32,256]{2,1,0:T(8,128)S(1)}, f32[4,32,256]{2,1,0:T(8,128)S(1)}, u32[]{:S(2)}, u32[]{:S(2)}) %collective-permute-start.11) | collective-permute-done | bytes 131104 | tf_op jit(solution)/shard_map/ppermute | solution.py:320
  73.1 2.3 %collective-permute-start.12 = (f32[2,32,256]{2,1,0:T(8,128)S(1)}, f32[2,32,256]{2,1,0:T(8,128)S(1)}, u32[]{:S(2)}, u32[]{:S(2)}) collective-permute-start(f32[2,32,256]{2,1,0:T(8,128)S(1)} %get-tuple-element.68), channel_id=1, source_target_pairs={{0,4},{2,6},{4,0},{6,2},{8,12},{10,14},{12,8},{14,10},{16,20},{18,... | collective-permute-start | bytes 196616 | tf_op jit(solution)/shard_map/ppermute | solution.py:320
  76.1 1.6 %collective-permute-done.12.refs_3_ = f32[2,32,256]{2,1,0:T(8,128)S(1)} collective-permute-done((f32[2,32,256]{2,1,0:T(8,128)S(1)}, f32[2,32,256]{2,1,0:T(8,128)S(1)}, u32[]{:S(2)}, u32[]{:S(2)}) %collective-permute-start.12) | collective-permute-done | bytes 65568 | tf_op jit(solution)/shard_map/ppermute | solution.py:320
  77.7 2.1 %collective-permute-done.10.refs_1_ = f32[2,32,256]{2,1,0:T(8,128)S(1)} collective-permute-done((f32[2,32,256]{2,1,0:T(8,128)S(1)}, f32[2,32,256]{2,1,0:T(8,128)S(1)}, u32[]{:S(2)}, u32[]{:S(2)}) %collective-permute-start.10) | collective-permute-done | bytes 65568 | tf_op jit(solution)/shard_map/ppermute | solution.py:320
  79.8 1.8 %collective-permute-start.13 = (f32[1,32,512]{2,1,0:T(8,128)S(1)}, f32[1,32,512]{2,1,0:T(8,128)S(1)}, u32[]{:S(2)}, u32[]{:S(2)}) collective-permute-start(f32[1,32,512]{2,1,0:T(8,128)S(1)} %get-tuple-element.70), channel_id=1, source_target_pairs={{0,16},{2,18},{4,20},{6,22},{8,24},{10,26},{12,28},{14,30},{16,0},... | collective-permute-start | bytes 196616 | tf_op jit(solution)/shard_map/ppermute | solution.py:320
  81.6 0.9 shard_map.64
  83.2 2.5 %collective-permute-done.13 = f32[1,32,512]{2,1,0:T(8,128)S(1)} collective-permute-done((f32[1,32,512]{2,1,0:T(8,128)S(1)}, f32[1,32,512]{2,1,0:T(8,128)S(1)}, u32[]{:S(2)}, u32[]{:S(2)}) %collective-permute-start.13) | collective-permute-done | bytes 65568 | tf_op jit(solution)/shard_map/ppermute | solution.py:320
  85.7 1.3 %collective-permute-start.14 = (f32[32,512]{1,0:T(8,128)S(1)}, f32[32,512]{1,0:T(8,128)S(1)}, u32[]{:S(2)}, u32[]{:S(2)}) collective-permute-start(f32[32,512]{1,0:T(8,128)S(1)} %add_bitcast_fusion), channel_id=1, source_target_pairs={{1,0},{3,2},{5,4},{7,6},{9,8},{11,10},{13,12},{15,14},{17,16},{19,... | collective-permute-start | bytes 196616 | tf_op jit(solution)/shard_map/ppermute | solution.py:392
  87.0 4.8 %collective-permute-done.14 = f32[32,512]{1,0:T(8,128)S(1)} collective-permute-done((f32[32,512]{1,0:T(8,128)S(1)}, f32[32,512]{1,0:T(8,128)S(1)}, u32[]{:S(2)}, u32[]{:S(2)}) %collective-permute-start.14) | collective-permute-done | bytes 65568 | tf_op jit(solution)/shard_map/ppermute | solution.py:392
  (30 shorter events, 3.7 us)
Async XLA Ops:
  1.2 12.4 %copy-start.3 = (s32[256,2]{0,1:T(2,128)S(1)}, s32[256,2]{0,1:T(2,128)}, u32[]{:S(2)}) copy-start(s32[256,2]{0,1:T(2,128)} %param.7) | copy-start | bytes 6148
  1.2 21.6 %collective-permute-start.2 = (bf16[768,512]{1,0:T(8,128)(2,1)S(1)}, bf16[768,512]{1,0:T(8,128)(2,1)S(1)}, u32[]{:S(2)}, u32[]{:S(2)}) collective-permute-start(bf16[768,512]{1,0:T(8,128)(2,1)S(1)} %slice.13), channel_id=1, source_target_pairs={{0,1},{2,3},{4,5},{6,7},{8,9},{10,11},{12,13},{14,15},{16,17},{18,... | collective-permute-start | bytes 2359304 | tf_op jit(solution)/shard_map/ppermute | solution.py:364
  6.1 0.7 copy-start.4
  11.5 17.4 %copy-start = (bf16[4096,512]{1,0:T(8,128)(2,1)}, bf16[4096,512]{1,0:T(8,128)(2,1)S(1)}, u32[]{:S(2)}) copy-start(bf16[4096,512]{1,0:T(8,128)(2,1)S(1)} %get-tuple-element.44.panel) | copy-start | bytes 12582916
  11.6 3.6 %collective-permute-start = (bf16[256,512]{1,0:T(8,128)(2,1)S(1)}, bf16[256,512]{1,0:T(8,128)(2,1)S(1)}, u32[]{:S(2)}, u32[]{:S(2)}) collective-permute-start(bf16[256,512]{1,0:T(8,128)(2,1)S(1)} %get-tuple-element.42), channel_id=1, source_target_pairs={{3,5},{7,9},{11,13},{15,17},{19,21},{23,25},{27,29},{5,3},{9,7},{1... | collective-permute-start | bytes 786440 | tf_op jit(solution)/shard_map/ppermute | solution.py:350
  12.2 2.9 %collective-permute-start.1 = (bf16[256,512]{1,0:T(8,128)(2,1)S(1)}, bf16[256,512]{1,0:T(8,128)(2,1)S(1)}, u32[]{:S(2)}, u32[]{:S(2)}) collective-permute-start(bf16[256,512]{1,0:T(8,128)(2,1)S(1)} %get-tuple-element.43), channel_id=1, source_target_pairs={{1,3},{5,7},{9,11},{13,15},{17,19},{21,23},{25,27},{29,31},{3,1},{... | collective-permute-start | bytes 786440 | tf_op jit(solution)/shard_map/ppermute | solution.py:350
  22.8 39.4 %collective-permute-start.5 = (bf16[1664,512]{1,0:T(8,128)(2,1)}, bf16[1664,512]{1,0:T(8,128)(2,1)}, u32[]{:S(2)}, u32[]{:S(2)}) collective-permute-start(bf16[1664,512]{1,0:T(8,128)(2,1)} %shard_map.58.after), channel_id=1, source_target_pairs={{0,1},{1,0},{2,3},{3,2},{4,5},{5,4},{6,7},{7,6},{8,9},{9,8},{10,11... | collective-permute-start | bytes 5111816 | tf_op jit(solution)/shard_map/ppermute | solution.py:369
  31.7 0.7 collective-permute-start.3
  32.5 1.3 %collective-permute-start.4 = (f32[4,32,512]{2,1,0:T(8,128)S(1)}, f32[4,32,512]{2,1,0:T(8,128)S(1)}, u32[]{:S(2)}, u32[]{:S(2)}) collective-permute-start(f32[4,32,512]{2,1,0:T(8,128)S(1)} %get-tuple-element.49), channel_id=1, source_target_pairs={{1,5},{3,7},{5,1},{7,3},{9,13},{11,15},{13,9},{15,11},{17,21},{19,... | collective-permute-start | bytes 786440 | tf_op jit(solution)/shard_map/ppermute | solution.py:320
  34.5 0.6 copy-start.1
  35.1 1.3 %collective-permute-start.6 = (f32[2,32,512]{2,1,0:T(8,128)}, f32[2,32,512]{2,1,0:T(8,128)}, u32[]{:S(2)}, u32[]{:S(2)}) collective-permute-start(f32[2,32,512]{2,1,0:T(8,128)} %get-tuple-element.53), channel_id=1, source_target_pairs={{1,9},{3,11},{5,13},{7,15},{9,1},{11,3},{13,5},{15,7},{17,25},{19,... | collective-permute-start | bytes 393224 | tf_op jit(solution)/shard_map/ppermute | solution.py:320
  65.4 16.2 %copy-start.2 = (f32[2,32,512]{2,1,0:T(8,128)S(1)}, f32[2,32,512]{2,1,0:T(8,128)}, u32[]{:S(2)}) copy-start(f32[2,32,512]{2,1,0:T(8,128)} %copy-done.1) | copy-start | bytes 393220
  65.5 2.0 %collective-permute-start.8 = (f32[8,32,512]{2,1,0:T(8,128)S(1)}, f32[8,32,512]{2,1,0:T(8,128)S(1)}, u32[]{:S(2)}, u32[]{:S(2)}) collective-permute-start(f32[8,32,512]{2,1,0:T(8,128)S(1)} %get-tuple-element.60), channel_id=1, source_target_pairs={{0,2},{2,0},{4,6},{6,4},{8,10},{10,8},{12,14},{14,12},{16,18},{18,... | collective-permute-start | bytes 1572872 | tf_op jit(solution)/shard_map/ppermute | solution.py:320
  67.5 5.6 %collective-permute-start.11 = (f32[4,32,256]{2,1,0:T(8,128)S(1)}, f32[4,32,256]{2,1,0:T(8,128)S(1)}, u32[]{:S(2)}, u32[]{:S(2)}) collective-permute-start(f32[4,32,256]{2,1,0:T(8,128)S(1)} %get-tuple-element.66), channel_id=1, source_target_pairs={{0,8},{2,10},{4,12},{6,14},{8,0},{10,2},{12,4},{14,6},{16,24},{18,... | collective-permute-start | bytes 393224 | tf_op jit(solution)/shard_map/ppermute | solution.py:320
  69.3 6.2 %collective-permute-start.9 = (f32[4,32,256]{2,1,0:T(8,128)S(1)}, f32[4,32,256]{2,1,0:T(8,128)S(1)}, u32[]{:S(2)}, u32[]{:S(2)}) collective-permute-start(f32[4,32,256]{2,1,0:T(8,128)S(1)} %get-tuple-element.62), channel_id=1, source_target_pairs={{0,4},{2,6},{4,0},{6,2},{8,12},{10,14},{12,8},{14,10},{16,20},{18,... | collective-permute-start | bytes 393224 | tf_op jit(solution)/shard_map/ppermute | solution.py:320
  73.1 4.6 %collective-permute-start.12 = (f32[2,32,256]{2,1,0:T(8,128)S(1)}, f32[2,32,256]{2,1,0:T(8,128)S(1)}, u32[]{:S(2)}, u32[]{:S(2)}) collective-permute-start(f32[2,32,256]{2,1,0:T(8,128)S(1)} %get-tuple-element.68), channel_id=1, source_target_pairs={{0,4},{2,6},{4,0},{6,2},{8,12},{10,14},{12,8},{14,10},{16,20},{18,... | collective-permute-start | bytes 196616 | tf_op jit(solution)/shard_map/ppermute | solution.py:320
  75.4 4.3 %collective-permute-start.10 = (f32[2,32,256]{2,1,0:T(8,128)S(1)}, f32[2,32,256]{2,1,0:T(8,128)S(1)}, u32[]{:S(2)}, u32[]{:S(2)}) collective-permute-start(f32[2,32,256]{2,1,0:T(8,128)S(1)} %get-tuple-element.64), channel_id=1, source_target_pairs={{0,8},{2,10},{4,12},{6,14},{8,0},{10,2},{12,4},{14,6},{16,24},{18,... | collective-permute-start | bytes 196616 | tf_op jit(solution)/shard_map/ppermute | solution.py:320
  79.8 5.9 %collective-permute-start.13 = (f32[1,32,512]{2,1,0:T(8,128)S(1)}, f32[1,32,512]{2,1,0:T(8,128)S(1)}, u32[]{:S(2)}, u32[]{:S(2)}) collective-permute-start(f32[1,32,512]{2,1,0:T(8,128)S(1)} %get-tuple-element.70), channel_id=1, source_target_pairs={{0,16},{2,18},{4,20},{6,22},{8,24},{10,26},{12,28},{14,30},{16,0},... | collective-permute-start | bytes 196616 | tf_op jit(solution)/shard_map/ppermute | solution.py:320
  82.5 4.5 %collective-permute-start.7 = (f32[1,32,512]{2,1,0:T(8,128)S(1)}, f32[1,32,512]{2,1,0:T(8,128)S(1)}, u32[]{:S(2)}, u32[]{:S(2)}) collective-permute-start(f32[1,32,512]{2,1,0:T(8,128)S(1)} %get-tuple-element.56), channel_id=1, source_target_pairs={{1,17},{3,19},{5,21},{7,23},{9,25},{11,27},{13,29},{15,31},{17,1},... | collective-permute-start | bytes 196616 | tf_op jit(solution)/shard_map/ppermute | solution.py:320
  85.7 6.2 %collective-permute-start.14 = (f32[32,512]{1,0:T(8,128)S(1)}, f32[32,512]{1,0:T(8,128)S(1)}, u32[]{:S(2)}, u32[]{:S(2)}) collective-permute-start(f32[32,512]{1,0:T(8,128)S(1)} %add_bitcast_fusion), channel_id=1, source_target_pairs={{1,0},{3,2},{5,4},{7,6},{9,8},{11,10},{13,12},{15,14},{17,16},{19,... | collective-permute-start | bytes 196616 | tf_op jit(solution)/shard_map/ppermute | solution.py:392

commit v5 on v4

--- a/solution.py
+++ b/solution.py
@@ -251,21 +251,113 @@
     out[...] = acc[...].astype(out.dtype)
 
 
-def known_kernel(left, right, out):
-    out[...] = contract(left[...], right[...])
-
-
-def known_product(left, right):
-    rows, width = right.shape[0], left.shape[1]
-    return pl.pallas_call(
-        known_kernel,
-        grid=(1,),
-        out_shape=jax.ShapeDtypeStruct((width, right.shape[1]), jnp.float32),
-        in_specs=[pl.BlockSpec((rows, width), lambda i: (0, 0)), pl.BlockSpec(right.shape, lambda i: (0, 0))],
-        out_specs=pl.BlockSpec((width, right.shape[1]), lambda i: (0, 0)),
-        compiler_params=room_for(4 * nbytes(right), 8 * width * width),
-        cost_estimate=near_nothing(),
-    )(left, right)
+def add_contract(total, left, right, left0=0, right0=0, rows=None):
+    depth = (left.shape[0] if rows is None else rows) // 4
+
+    @pl.loop(0, 4)
+    def _(i):
+        begin = pl.multiple_of(i * depth, depth)
+        total[...] += contract(left[pl.ds(left0 + begin, depth), :], right[pl.ds(right0 + begin, depth), :])
+
+
+def panel_kernel(nrows_blk, nrows, shift, bsize, first, owner_row, entries, blocks, panel, odd, even, sent, out, result, halo, acc, near_sent, sem):
+    copy = pltpu.make_async_copy(sent, near_sent, sem)
+    copy.start()
+    mass_kernel(nrows_blk, 0, nrows, shift, bsize, first, owner_row, entries, blocks, panel, odd, even, None, out, halo, acc)
+    result[...] = jnp.zeros_like(result)
+    add_contract(result, out, panel)
+    copy.wait()
+    add_contract(result, near_sent, panel, right0=nrows * bsize)
+
+
+def panel_work(lists, blocks, panel, odd, even, sent, shift, nrows):
+    bsize, width = blocks.shape[1], panel.shape[1]
+    return pl.pallas_call(
+        functools.partial(panel_kernel, panel.shape[0] // bsize, nrows, shift, bsize),
+        out_shape=[
+            jax.ShapeDtypeStruct((nrows * bsize, width), panel.dtype),
+            jax.ShapeDtypeStruct((width, width), jnp.float32),
+        ],
+        in_specs=[SCALAR] * 3 + [NEAR] * 4 + [ANYWHERE],
+        out_specs=[NEAR] * 2,
+        scratch_shapes=[
+            pltpu.VMEM((2 * even.shape[0], width), panel.dtype),
+            pltpu.VMEM((nrows * bsize, width), jnp.float32),
+            pltpu.VMEM(sent.shape, sent.dtype),
+            pltpu.SemaphoreType.DMA,
+        ],
+        compiler_params=room_for(4 * nbytes(even), 6 * nrows * bsize * width, 2 * nbytes(sent), 4 * width * width),
+        cost_estimate=near_nothing(),
+    )(*lists, blocks, panel, odd, even, sent)
+
+
+def partner_kernel(n_col, mass, ahead, panel, known, partner):
+    early, rows = ahead.shape[0], partner.shape[0]
+    panel_column = lax.axis_index("col") == n_col - 1
+    known[...] = jnp.zeros_like(known)
+
+    @pl.when(panel_column)
+    def _():
+        add_contract(known, mass, ahead, rows=early)
+        partner[...] = mass[pl.ds(early, rows), :]
+
+    @pl.when(jnp.logical_not(panel_column))
+    def _():
+        partner[...] = panel[pl.ds(panel.shape[0] - rows, rows), :]
+
+
+def partner_rows(mass, ahead, panel, rows, n_col):
+    width = mass.shape[1]
+    return pl.pallas_call(
+        functools.partial(partner_kernel, n_col),
+        out_shape=[jax.ShapeDtypeStruct((width, width), jnp.float32), jax.ShapeDtypeStruct((rows, width), mass.dtype)],
+        in_specs=[NEAR] * 3,
+        out_specs=[NEAR] * 2,
+        compiler_params=room_for(2 * nbytes(ahead), 4 * width * width, 4 * rows * width),
+        cost_estimate=near_nothing(),
+    )(mass, ahead, panel)
+
+
+def meet_kernel(n_col, got, partner, known, out, near_got, sem):
+    parts = sem.shape[0]
+    depth = got.shape[0] // parts
+
+    def part(i):
+        some = pl.ds(pl.multiple_of(i * depth, depth), depth)
+        return some, pltpu.make_async_copy(got.at[some], near_got.at[some], sem.at[i])
+
+    for i in range(parts):
+        part(i)[1].start()
+    out[...] = known[...]
+    panel_column = lax.axis_index("col") == n_col - 1
+
+    @pl.when(panel_column)
+    def _():
+        @pl.loop(0, parts)
+        def _(i):
+            some, copy = part(i)
+            copy.wait()
+            out[...] += contract(partner[some, :], near_got[some, :])
+
+    @pl.when(jnp.logical_not(panel_column))
+    def _():
+        @pl.loop(0, parts)
+        def _(i):
+            some, copy = part(i)
+            copy.wait()
+            out[...] += contract(near_got[some, :], partner[some, :])
+
+
+def meet(got, partner, known, n_col):
+    return pl.pallas_call(
+        functools.partial(meet_kernel, n_col),
+        out_shape=jax.ShapeDtypeStruct(known.shape, jnp.float32),
+        in_specs=[ANYWHERE, NEAR, NEAR],
+        out_specs=NEAR,
+        scratch_shapes=[pltpu.VMEM(got.shape, got.dtype), pltpu.SemaphoreType.DMA((4,))],
+        compiler_params=room_for(2 * nbytes(got), 2 * nbytes(known)),
+        cost_estimate=near_nothing(),
+    )(got, partner, known)
 
 
 def mass_rows(lists, blocks, panel, odd, even, after, shift, row0, nrows):
@@ -327,10 +419,10 @@
     left, right = step(route, 2, 1, (whole, 0, half)), step(route, 4, 2, (whole, half, half))
     left, right = step(route, 4, 1, (left, 0, half)), step(route, 2, 1, (right, 0, half))
     bit, columns = 8, [(left, 0, half), (right, 0, half)]
-    while bit < targets:
+    while bit < targets // 2:
         columns = [(step(route, bit, 1, *columns), 0, width)]
         bit *= 2
-    return jnp.concatenate([a + b for (a, b), _, _ in columns], 2).reshape(rows, width)
+    return columns
 
 
 def body(tmat, stored_mass_blocks, block_index, live_block_count, send_rows):
@@ -354,7 +446,7 @@
     *rows, panel, blocks = gather_rows(send_rows, tmat, stored_mass_blocks)
     even, odd = exchange(rows[0], 0), exchange(rows[1], 1)
 
-    if n_col != 2 or n_dom < 8 or n_dom & (n_dom - 1):
+    if n_col != 2 or n_dom < 16 or n_dom & (n_dom - 1):
         mass = mass_rows(lists, blocks, panel, odd, even, even, shift, 0, nrows_blk)
         total = lax.psum(contract(lax.psum(mass, "col"), tmat), "dom")
         return lax.dynamic_slice_in_dim(total, dom * share, share, 0)
@@ -367,9 +459,8 @@
     sent = piece(lists, blocks, odd, even, own_a, tmat, shift, nb, na, early, n_col)
     sent, ahead = lax.optimization_barrier((sent, ahead))
     got = lax.ppermute(sent, "col", [(0, 1), (1, 0)])
-    mass_b = mass_rows(lists, blocks, panel, odd, even, sent, shift, 0, nb)
-    own = contract(sent, panel[cut:]) + contract(mass_b, panel[:cut])
-    known = known_product(mass_b, ahead)
+    mass_b, own = panel_work(lists, blocks, panel, odd, even, sent, shift, nb)
+    known, partner = partner_rows(mass_b, ahead, panel, na * bsize, n_col)
 
     def both(bit):
         return "dom", [(i, i ^ bit) for i in range(n_dom)]
@@ -381,16 +472,16 @@
     while bit < n_dom // 2:
         parts = step(panel_column, bit, 1, (parts, 0, width))
         if bit == 2:
-            parts[1], known = lax.optimization_barrier((parts[1], known))
+            parts[1], known, partner = lax.optimization_barrier((parts[1], known, partner))
         bit *= 2
     got, parts[1] = lax.optimization_barrier((got, parts[1]))
-    parts = step(panel_column, bit, 1, (parts, 0, width))
-    own = (parts[0] + parts[1]).reshape(share, width)
-
-    x = contract(jnp.where(col == owner, mass_b[early:], got), jnp.where(col == owner, got, panel[cut:])) + known
-    x = scatter(x.reshape(n_dom, share, width), both)
+
+    x = meet(got, partner, known, n_col)
+    keep, got = step(both, bit, 1, *scatter(x.reshape(n_dom, share, width), both))
+    own_keep, own_got = step(panel_column, bit, 1, (parts, 0, width))
+    x = keep + got
     other = x + lax.ppermute(x, "col", [(1, 0)])
-    return jnp.where(col == owner, own, other)
+    return jnp.where(col == owner, own_keep + own_got, other).reshape(share, width)
 
 
 def solution(mesh):

time: 92.3 us -> 90.6 us (0.982)
  matrix products: 7.26 us -> 0 us
  Pallas kernels: 14.2 us -> 17.7 us
  waiting for transfers between devices: 45.8 us -> 47.3 us
    dot_general x3 -> x0, matrix products: 7.26 us -> none  [contract(): lax.dot_general(left, right, (((0,), (0,)), ((), ())), preferred_element_...]
    pallas_call x2 -> x3, Pallas kernels: 2.71 us -> 8.97 us  [the longest x1 5.89 us: panel_work(): pl.pallas_call(functools.partial(panel_kernel, panel.shape[0] // bsize, n...]
    ppermute x1, waiting for transfers between devices: 25.8 us -> 27.9 us  [body(): got = lax.ppermute(sent, 'col', [(0, 1), (1, 0)])]
    ppermute x10, waiting for transfers between devices: 10.7 us -> 8.82 us  [step(): return [keep, lax.ppermute(send, *route(bit))]]
    pallas_call x10, Pallas kernels: 1.98 us -> 0.43 us  [fold(): pl.pallas_call(functools.partial(fold_kernel, bit, inner, [(len(some), be...]
    ppermute x1, waiting for transfers between devices: 4.43 us -> 5.67 us  [body(): ahead = lax.ppermute(tmat[:early], 'col', [(0, 1)])]
    pallas_call x1, Pallas kernels: 3.25 us -> 2.05 us  [piece(): pl.pallas_call(functools.partial(pieces_kernel, tmat.shape[0] // bsize, r...]
  transfers between devices with their start and end apart: 15 -> 15, of which waited for: 8 -> 8; matrix products, arithmetic and copies ran while one was open for 4% -> 0% of each run, Pallas kernels for 15% -> 16%
where the time goes in v5:
time: 90.6 us; the launch traced here: 90.3 us
  waiting for transfers between devices  47.3 us (52%)
  starting transfers between devices  21.9 us (24%)
  Pallas kernels  17.7 us (20%)
  local copies, waits for them, and re-layouts  1.87 us (2%)
  between operations  0.91 us (1%)
    ppermute x1, waiting for transfers between devices, body(): got = lax.ppermute(sent, 'col', [(0, 1), (1, 0)])  27.9 us
    ppermute x10, starting transfers between devices, step(): return [keep, lax.ppermute(send, *route(bit))]  11.9 us
    ppermute x10, waiting for transfers between devices, step(): return [keep, lax.ppermute(send, *route(bit))]  8.82 us
    pallas_call x1, Pallas kernels, panel_work(): pl.pallas_call(functools.partial(panel_kernel, panel.shape[0] // bsize, n...  5.89 us
    ppermute x1, waiting for transfers between devices, body(): ahead = lax.ppermute(tmat[:early], 'col', [(0, 1)])  5.67 us
    ppermute x1, starting transfers between devices, body(): ahead = lax.ppermute(tmat[:early], 'col', [(0, 1)])  4.89 us
    ppermute x1, waiting for transfers between devices, body(): other = x + lax.ppermute(x, 'col', [(1, 0)])  4.85 us
    pallas_call x1, Pallas kernels, gather_rows(): pl.pallas_call(gather_kernel, out_shape=[jax.ShapeDtypeStruct((picked //...  4.75 us
  transfers between devices with their start and end apart: 15, of which 8 were waited for; matrix products, arithmetic and copies ran while one was open for 0% of the time, Pallas kernels for 16%

profile of v5, /device:TPU:0, one launch (start us, length us, event | category | flops | bytes accessed | tf_op | source)
XLA Modules:
  0.0 90.3 jit_solution(13073933625172353980)
XLA Ops:
  0.0 1.2 %slice.3 = bf16[768,512]{1,0:T(8,128)(2,1)S(1)} slice(bf16[4096,512]{1,0:T(8,128)(2,1)} %tmat.3), slice={[0:768], [0:512]} | slice | bytes 1572864 | tf_op jit(solution)/shard_map/slice | solution.py:456
  1.2 4.9 %collective-permute-start.2 = (bf16[768,512]{1,0:T(8,128)(2,1)S(1)}, bf16[768,512]{1,0:T(8,128)(2,1)S(1)}, u32[]{:S(2)}, u32[]{:S(2)}) collective-permute-start(bf16[768,512]{1,0:T(8,128)(2,1)S(1)} %slice.3), channel_id=1, source_target_pairs={{0,1},{2,3},{4,5},{6,7},{8,9},{10,11},{12,13},{14,15},{16,17},{18,... | collective-permute-start | bytes 2359304 | tf_op jit(solution)/shard_map/ppermute | solution.py:456
  6.1 0.7 copy-done.1
  6.8 4.7 %shard_map.56 = (bf16[256,512]{1,0:T(8,128)(2,1)S(1)}, bf16[256,512]{1,0:T(8,128)(2,1)S(1)}, bf16[4096,512]{1,0:T(8,128)(2,1)S(1)}, bf16[256,128,128]{2,1,0:T(8,128)(2,1)S(1)}) custom-call(s32[2,256]{1,0:T(2,128)S(1)} %copy-done.1, bf16[4096,512]{1,0:T(8,128)(2,1)} %tmat.3, bf16[256,128,128]{2,1,0:T(8,128)(2,1)} %blocks.1), custom_call_target="tpu_custom_call" | custom-call | flops 1 | bytes 1 | tf_op jit(solution)/shard_map/pallas_call | solution.py:168
  11.5 0.7 collective-permute-start
  12.2 0.7 collective-permute-start.1
  13.6 0.7 shard_map.55
  14.3 0.8 shard_map.57.own
  15.1 2.1 %shard_map.58.sent = bf16[1664,512]{1,0:T(8,128)(2,1)S(1)} custom-call(s32[1,128]{1,0:T(1,128)S(1)} %get-tuple-element.43.first, s32[1,128]{1,0:T(1,128)S(1)} %get-tuple-element.44.owner_row, s32[1,512]{1,0:T(1,128)S(1)} %get-tuple-element.45.entries, bf16[256,128,128]{2,1,0:T(8,128)(2,1)S(1)} %get-tuple-element.46.blocks, ...), custom_call_target="tpu_custom_call" | custom-call | flops 1 | bytes 1 | tf_op jit(solution)/shard_map/pallas_call | solution.py:229
  17.2 5.7 %collective-permute-done.2.ahead = bf16[768,512]{1,0:T(8,128)(2,1)S(1)} collective-permute-done((bf16[768,512]{1,0:T(8,128)(2,1)S(1)}, bf16[768,512]{1,0:T(8,128)(2,1)S(1)}, u32[]{:S(2)}, u32[]{:S(2)}) %collective-permute-start.2) | collective-permute-done | bytes 786464 | tf_op jit(solution)/shard_map/ppermute | solution.py:456
  22.8 2.5 %collective-permute-start.5 = (bf16[1664,512]{1,0:T(8,128)(2,1)S(1)}, bf16[1664,512]{1,0:T(8,128)(2,1)S(1)}, u32[]{:S(2)}, u32[]{:S(2)}) collective-permute-start(bf16[1664,512]{1,0:T(8,128)(2,1)S(1)} %shard_map.58.sent), channel_id=1, source_target_pairs={{0,1},{1,0},{2,3},{3,2},{4,5},{5,4},{6,7},{7,6},{8,9},{9,8},{10,11... | collective-permute-start | bytes 5111816 | tf_op jit(solution)/shard_map/ppermute | solution.py:461
  25.3 5.9 %shard_map.59 = (bf16[2432,512]{1,0:T(8,128)(2,1)S(1)}, f32[512,512]{1,0:T(8,128)S(1)}) custom-call(s32[1,128]{1,0:T(1,128)S(1)} %get-tuple-element.43.first, s32[1,128]{1,0:T(1,128)S(1)} %get-tuple-element.44.owner_row, s32[1,512]{1,0:T(1,128)S(1)} %get-tuple-element.45.entries, bf16[256,128,128]{2,1,0:T(8,128)(2,1)S(1)} %get-tuple-element.46.blocks, ...), custom_call_target="tpu_custom_call" | custom-call | flops 1 | bytes 1 | tf_op jit(solution)/shard_map/pallas_call | solution.py:275
  31.3 0.7 collective-permute-start.3
  32.1 0.7 collective-permute-start.4
  32.8 0.2 shard_map.62
  33.0 0.7 collective-permute-start.6
  33.7 27.9 %collective-permute-done.5.got = bf16[1664,512]{1,0:T(8,128)(2,1)S(1)} collective-permute-done((bf16[1664,512]{1,0:T(8,128)(2,1)S(1)}, bf16[1664,512]{1,0:T(8,128)(2,1)S(1)}, u32[]{:S(2)}, u32[]{:S(2)}) %collective-permute-start.5) | collective-permute-done | bytes 1703968 | tf_op jit(solution)/shard_map/ppermute | solution.py:461
  61.6 2.9 %shard_map.65 = f32[512,512]{1,0:T(8,128)S(1)} custom-call(bf16[1664,512]{1,0:T(8,128)(2,1)S(1)} %collective-permute-done.5.got, bf16[1664,512]{1,0:T(8,128)(2,1)S(1)} %get-tuple-element.67.partner, f32[512,512]{1,0:T(8,128)S(1)} %get-tuple-element.68.known), custom_call_target="tpu_custom_call" | custom-call | flops 1 | bytes 1 | tf_op jit(solution)/shard_map/pallas_call | solution.py:352
  64.7 1.9 %collective-permute-done.8.refs_1_ = f32[8,32,512]{2,1,0:T(8,128)S(1)} collective-permute-done((f32[8,32,512]{2,1,0:T(8,128)S(1)}, f32[8,32,512]{2,1,0:T(8,128)S(1)}, u32[]{:S(2)}, u32[]{:S(2)}) %collective-permute-start.8) | collective-permute-done | bytes 524320 | tf_op jit(solution)/shard_map/ppermute | solution.py:412
  66.7 1.6 %collective-permute-start.11 = (f32[4,32,256]{2,1,0:T(8,128)S(1)}, f32[4,32,256]{2,1,0:T(8,128)S(1)}, u32[]{:S(2)}, u32[]{:S(2)}) collective-permute-start(f32[4,32,256]{2,1,0:T(8,128)S(1)} %get-tuple-element.76), channel_id=1, source_target_pairs={{0,8},{2,10},{4,12},{6,14},{8,0},{10,2},{12,4},{14,6},{16,24},{18,... | collective-permute-start | bytes 393224 | tf_op jit(solution)/shard_map/ppermute | solution.py:412
  68.3 1.6 %collective-permute-start.9 = (f32[4,32,256]{2,1,0:T(8,128)S(1)}, f32[4,32,256]{2,1,0:T(8,128)S(1)}, u32[]{:S(2)}, u32[]{:S(2)}) collective-permute-start(f32[4,32,256]{2,1,0:T(8,128)S(1)} %get-tuple-element.72), channel_id=1, source_target_pairs={{0,4},{2,6},{4,0},{6,2},{8,12},{10,14},{12,8},{14,10},{16,20},{18,... | collective-permute-start | bytes 393224 | tf_op jit(solution)/shard_map/ppermute | solution.py:412
  69.9 2.3 %collective-permute-done.11.refs_1_ = f32[4,32,256]{2,1,0:T(8,128)S(1)} collective-permute-done((f32[4,32,256]{2,1,0:T(8,128)S(1)}, f32[4,32,256]{2,1,0:T(8,128)S(1)}, u32[]{:S(2)}, u32[]{:S(2)}) %collective-permute-start.11) | collective-permute-done | bytes 131104 | tf_op jit(solution)/shard_map/ppermute | solution.py:412
  72.3 1.6 %collective-permute-start.12 = (f32[2,32,256]{2,1,0:T(8,128)S(1)}, f32[2,32,256]{2,1,0:T(8,128)S(1)}, u32[]{:S(2)}, u32[]{:S(2)}) collective-permute-start(f32[2,32,256]{2,1,0:T(8,128)S(1)} %get-tuple-element.78), channel_id=1, source_target_pairs={{0,4},{2,6},{4,0},{6,2},{8,12},{10,14},{12,8},{14,10},{16,20},{18,... | collective-permute-start | bytes 196616 | tf_op jit(solution)/shard_map/ppermute | solution.py:412
  73.9 1.6 %collective-permute-start.10 = (f32[2,32,256]{2,1,0:T(8,128)S(1)}, f32[2,32,256]{2,1,0:T(8,128)S(1)}, u32[]{:S(2)}, u32[]{:S(2)}) collective-permute-start(f32[2,32,256]{2,1,0:T(8,128)S(1)} %get-tuple-element.74), channel_id=1, source_target_pairs={{0,8},{2,10},{4,12},{6,14},{8,0},{10,2},{12,4},{14,6},{16,24},{18,... | collective-permute-start | bytes 196616 | tf_op jit(solution)/shard_map/ppermute | solution.py:412
  75.5 1.1 %collective-permute-done.12.refs_3_ = f32[2,32,256]{2,1,0:T(8,128)S(1)} collective-permute-done((f32[2,32,256]{2,1,0:T(8,128)S(1)}, f32[2,32,256]{2,1,0:T(8,128)S(1)}, u32[]{:S(2)}, u32[]{:S(2)}) %collective-permute-start.12) | collective-permute-done | bytes 65568 | tf_op jit(solution)/shard_map/ppermute | solution.py:412
  76.6 1.6 %collective-permute-done.10.refs_1_ = f32[2,32,256]{2,1,0:T(8,128)S(1)} collective-permute-done((f32[2,32,256]{2,1,0:T(8,128)S(1)}, f32[2,32,256]{2,1,0:T(8,128)S(1)}, u32[]{:S(2)}, u32[]{:S(2)}) %collective-permute-start.10) | collective-permute-done | bytes 65568 | tf_op jit(solution)/shard_map/ppermute | solution.py:412
  78.2 2.6 %collective-permute-start.13 = (f32[1,32,512]{2,1,0:T(8,128)S(1)}, f32[1,32,512]{2,1,0:T(8,128)S(1)}, u32[]{:S(2)}, u32[]{:S(2)}) collective-permute-start(f32[1,32,512]{2,1,0:T(8,128)S(1)} %get-tuple-element.80), channel_id=1, source_target_pairs={{0,16},{2,18},{4,20},{6,22},{8,24},{10,26},{12,28},{14,30},{16,0},... | collective-permute-start | bytes 196616 | tf_op jit(solution)/shard_map/ppermute | solution.py:412
  80.9 0.7 collective-permute-start.7
  81.6 1.9 %collective-permute-done.13 = f32[1,32,512]{2,1,0:T(8,128)S(1)} collective-permute-done((f32[1,32,512]{2,1,0:T(8,128)S(1)}, f32[1,32,512]{2,1,0:T(8,128)S(1)}, u32[]{:S(2)}, u32[]{:S(2)}) %collective-permute-start.13) | collective-permute-done | bytes 65568 | tf_op jit(solution)/shard_map/ppermute | solution.py:412
  83.5 1.3 %collective-permute-start.14 = (f32[1,32,512]{2,1,0:T(8,128)S(1)}, f32[1,32,512]{2,1,0:T(8,128)S(1)}, u32[]{:S(2)}, u32[]{:S(2)}) collective-permute-start(f32[1,32,512]{2,1,0:T(8,128)S(1)} %add.10), channel_id=1, source_target_pairs={{1,0},{3,2},{5,4},{7,6},{9,8},{11,10},{13,12},{15,14},{17,16},{19,... | collective-permute-start | bytes 196616 | tf_op jit(solution)/shard_map/ppermute | solution.py:483
  84.8 4.8 %collective-permute-done.14 = f32[1,32,512]{2,1,0:T(8,128)S(1)} collective-permute-done((f32[1,32,512]{2,1,0:T(8,128)S(1)}, f32[1,32,512]{2,1,0:T(8,128)S(1)}, u32[]{:S(2)}, u32[]{:S(2)}) %collective-permute-start.14) | collective-permute-done | bytes 65568 | tf_op jit(solution)/shard_map/ppermute | solution.py:483
  89.6 0.6 select_bitcast_fusion
  (22 shorter events, 0.5 us)
Async XLA Ops:
  1.2 12.4 %copy-start = (s32[256,2]{0,1:T(2,128)S(1)}, s32[256,2]{0,1:T(2,128)}, u32[]{:S(2)}) copy-start(s32[256,2]{0,1:T(2,128)} %param.7) | copy-start | bytes 6148
  1.2 21.6 %collective-permute-start.2 = (bf16[768,512]{1,0:T(8,128)(2,1)S(1)}, bf16[768,512]{1,0:T(8,128)(2,1)S(1)}, u32[]{:S(2)}, u32[]{:S(2)}) collective-permute-start(bf16[768,512]{1,0:T(8,128)(2,1)S(1)} %slice.3), channel_id=1, source_target_pairs={{0,1},{2,3},{4,5},{6,7},{8,9},{10,11},{12,13},{14,15},{16,17},{18,... | collective-permute-start | bytes 2359304 | tf_op jit(solution)/shard_map/ppermute | solution.py:456
  6.1 0.7 copy-start.1
  11.5 3.5 %collective-permute-start = (bf16[256,512]{1,0:T(8,128)(2,1)S(1)}, bf16[256,512]{1,0:T(8,128)(2,1)S(1)}, u32[]{:S(2)}, u32[]{:S(2)}) collective-permute-start(bf16[256,512]{1,0:T(8,128)(2,1)S(1)} %get-tuple-element.48), channel_id=1, source_target_pairs={{3,5},{7,9},{11,13},{15,17},{19,21},{23,25},{27,29},{5,3},{9,7},{1... | collective-permute-start | bytes 786440 | tf_op jit(solution)/shard_map/ppermute | solution.py:442
  12.2 2.9 %collective-permute-start.1 = (bf16[256,512]{1,0:T(8,128)(2,1)S(1)}, bf16[256,512]{1,0:T(8,128)(2,1)S(1)}, u32[]{:S(2)}, u32[]{:S(2)}) collective-permute-start(bf16[256,512]{1,0:T(8,128)(2,1)S(1)} %get-tuple-element.49), channel_id=1, source_target_pairs={{1,3},{5,7},{9,11},{13,15},{17,19},{21,23},{25,27},{29,31},{3,1},{... | collective-permute-start | bytes 786440 | tf_op jit(solution)/shard_map/ppermute | solution.py:442
  22.8 38.8 %collective-permute-start.5 = (bf16[1664,512]{1,0:T(8,128)(2,1)S(1)}, bf16[1664,512]{1,0:T(8,128)(2,1)S(1)}, u32[]{:S(2)}, u32[]{:S(2)}) collective-permute-start(bf16[1664,512]{1,0:T(8,128)(2,1)S(1)} %shard_map.58.sent), channel_id=1, source_target_pairs={{0,1},{1,0},{2,3},{3,2},{4,5},{5,4},{6,7},{7,6},{8,9},{9,8},{10,11... | collective-permute-start | bytes 5111816 | tf_op jit(solution)/shard_map/ppermute | solution.py:461
  31.3 0.7 collective-permute-start.3
  32.1 0.9 collective-permute-start.4
  33.0 0.7 collective-permute-start.6
  64.6 2.0 %collective-permute-start.8 = (f32[8,32,512]{2,1,0:T(8,128)S(1)}, f32[8,32,512]{2,1,0:T(8,128)S(1)}, u32[]{:S(2)}, u32[]{:S(2)}) collective-permute-start(f32[8,32,512]{2,1,0:T(8,128)S(1)} %get-tuple-element.70), channel_id=1, source_target_pairs={{0,2},{2,0},{4,6},{6,4},{8,10},{10,8},{12,14},{14,12},{16,18},{18,... | collective-permute-start | bytes 1572872 | tf_op jit(solution)/shard_map/ppermute | solution.py:412
  66.7 5.6 %collective-permute-start.11 = (f32[4,32,256]{2,1,0:T(8,128)S(1)}, f32[4,32,256]{2,1,0:T(8,128)S(1)}, u32[]{:S(2)}, u32[]{:S(2)}) collective-permute-start(f32[4,32,256]{2,1,0:T(8,128)S(1)} %get-tuple-element.76), channel_id=1, source_target_pairs={{0,8},{2,10},{4,12},{6,14},{8,0},{10,2},{12,4},{14,6},{16,24},{18,... | collective-permute-start | bytes 393224 | tf_op jit(solution)/shard_map/ppermute | solution.py:412
  68.3 5.5 %collective-permute-start.9 = (f32[4,32,256]{2,1,0:T(8,128)S(1)}, f32[4,32,256]{2,1,0:T(8,128)S(1)}, u32[]{:S(2)}, u32[]{:S(2)}) collective-permute-start(f32[4,32,256]{2,1,0:T(8,128)S(1)} %get-tuple-element.72), channel_id=1, source_target_pairs={{0,4},{2,6},{4,0},{6,2},{8,12},{10,14},{12,8},{14,10},{16,20},{18,... | collective-permute-start | bytes 393224 | tf_op jit(solution)/shard_map/ppermute | solution.py:412
  72.3 4.3 %collective-permute-start.12 = (f32[2,32,256]{2,1,0:T(8,128)S(1)}, f32[2,32,256]{2,1,0:T(8,128)S(1)}, u32[]{:S(2)}, u32[]{:S(2)}) collective-permute-start(f32[2,32,256]{2,1,0:T(8,128)S(1)} %get-tuple-element.78), channel_id=1, source_target_pairs={{0,4},{2,6},{4,0},{6,2},{8,12},{10,14},{12,8},{14,10},{16,20},{18,... | collective-permute-start | bytes 196616 | tf_op jit(solution)/shard_map/ppermute | solution.py:412
  73.9 4.3 %collective-permute-start.10 = (f32[2,32,256]{2,1,0:T(8,128)S(1)}, f32[2,32,256]{2,1,0:T(8,128)S(1)}, u32[]{:S(2)}, u32[]{:S(2)}) collective-permute-start(f32[2,32,256]{2,1,0:T(8,128)S(1)} %get-tuple-element.74), channel_id=1, source_target_pairs={{0,8},{2,10},{4,12},{6,14},{8,0},{10,2},{12,4},{14,6},{16,24},{18,... | collective-permute-start | bytes 196616 | tf_op jit(solution)/shard_map/ppermute | solution.py:412
  78.2 5.2 %collective-permute-start.13 = (f32[1,32,512]{2,1,0:T(8,128)S(1)}, f32[1,32,512]{2,1,0:T(8,128)S(1)}, u32[]{:S(2)}, u32[]{:S(2)}) collective-permute-start(f32[1,32,512]{2,1,0:T(8,128)S(1)} %get-tuple-element.80), channel_id=1, source_target_pairs={{0,16},{2,18},{4,20},{6,22},{8,24},{10,26},{12,28},{14,30},{16,0},... | collective-permute-start | bytes 196616 | tf_op jit(solution)/shard_map/ppermute | solution.py:412
  80.9 3.9 %collective-permute-start.7 = (f32[1,32,512]{2,1,0:T(8,128)S(1)}, f32[1,32,512]{2,1,0:T(8,128)S(1)}, u32[]{:S(2)}, u32[]{:S(2)}) collective-permute-start(f32[1,32,512]{2,1,0:T(8,128)S(1)} %get-tuple-element.65), channel_id=1, source_target_pairs={{1,17},{3,19},{5,21},{7,23},{9,25},{11,27},{13,29},{15,31},{17,1},... | collective-permute-start | bytes 196616 | tf_op jit(solution)/shard_map/ppermute | solution.py:412
  83.5 6.2 %collective-permute-start.14 = (f32[1,32,512]{2,1,0:T(8,128)S(1)}, f32[1,32,512]{2,1,0:T(8,128)S(1)}, u32[]{:S(2)}, u32[]{:S(2)}) collective-permute-start(f32[1,32,512]{2,1,0:T(8,128)S(1)} %add.10), channel_id=1, source_target_pairs={{1,0},{3,2},{5,4},{7,6},{9,8},{11,10},{13,12},{15,14},{17,16},{19,... | collective-permute-start | bytes 196616 | tf_op jit(solution)/shard_map/ppermute | solution.py:483

commit v6 on v5

--- a/solution.py
+++ b/solution.py
@@ -251,10 +251,10 @@
     out[...] = acc[...].astype(out.dtype)
 
 
-def add_contract(total, left, right, left0=0, right0=0, rows=None):
-    depth = (left.shape[0] if rows is None else rows) // 4
-
-    @pl.loop(0, 4)
+def add_contract(total, left, right, left0=0, right0=0, rows=None, steps=4):
+    depth = (left.shape[0] if rows is None else rows) // steps
+
+    @pl.loop(0, steps)
     def _(i):
         begin = pl.multiple_of(i * depth, depth)
         total[...] += contract(left[pl.ds(left0 + begin, depth), :], right[pl.ds(right0 + begin, depth), :])
@@ -318,44 +318,26 @@
     )(mass, ahead, panel)
 
 
-def meet_kernel(n_col, got, partner, known, out, near_got, sem):
-    parts = sem.shape[0]
-    depth = got.shape[0] // parts
-
-    def part(i):
-        some = pl.ds(pl.multiple_of(i * depth, depth), depth)
-        return some, pltpu.make_async_copy(got.at[some], near_got.at[some], sem.at[i])
-
-    for i in range(parts):
-        part(i)[1].start()
+def meet_kernel(n_col, got, partner, known, out):
+    panel_column = lax.axis_index("col") == n_col - 1
     out[...] = known[...]
-    panel_column = lax.axis_index("col") == n_col - 1
 
     @pl.when(panel_column)
     def _():
-        @pl.loop(0, parts)
-        def _(i):
-            some, copy = part(i)
-            copy.wait()
-            out[...] += contract(partner[some, :], near_got[some, :])
+        add_contract(out, partner, got, steps=2)
 
     @pl.when(jnp.logical_not(panel_column))
     def _():
-        @pl.loop(0, parts)
-        def _(i):
-            some, copy = part(i)
-            copy.wait()
-            out[...] += contract(near_got[some, :], partner[some, :])
+        add_contract(out, got, partner, steps=2)
 
 
 def meet(got, partner, known, n_col):
     return pl.pallas_call(
         functools.partial(meet_kernel, n_col),
         out_shape=jax.ShapeDtypeStruct(known.shape, jnp.float32),
-        in_specs=[ANYWHERE, NEAR, NEAR],
+        in_specs=[NEAR] * 3,
         out_specs=NEAR,
-        scratch_shapes=[pltpu.VMEM(got.shape, got.dtype), pltpu.SemaphoreType.DMA((4,))],
-        compiler_params=room_for(2 * nbytes(got), 2 * nbytes(known)),
+        compiler_params=room_for(4 * nbytes(got), 2 * nbytes(known)),
         cost_estimate=near_nothing(),
     )(got, partner, known)
 

time: 90.6 us -> 89.3 us (0.986)
  Pallas kernels: 17.7 us -> 16.4 us
    pallas_call x1, Pallas kernels: 2.89 us -> 1.55 us  [meet(): pl.pallas_call(functools.partial(meet_kernel, n_col), out_shape=jax.Shape...]
where the time goes in v6:
time: 89.3 us; the launch traced here: 88.9 us
  waiting for transfers between devices  47.3 us (53%)
  starting transfers between devices  21.9 us (25%)
  Pallas kernels  16.4 us (18%)
  local copies, waits for them, and re-layouts  1.87 us (2%)
  between operations  0.91 us (1%)
    ppermute x1, waiting for transfers between devices, body(): got = lax.ppermute(sent, 'col', [(0, 1), (1, 0)])  27.9 us
    ppermute x10, starting transfers between devices, step(): return [keep, lax.ppermute(send, *route(bit))]  11.9 us
    ppermute x10, waiting for transfers between devices, step(): return [keep, lax.ppermute(send, *route(bit))]  8.82 us
    pallas_call x1, Pallas kernels, panel_work(): pl.pallas_call(functools.partial(panel_kernel, panel.shape[0] // bsize, n...  5.89 us
    ppermute x1, waiting for transfers between devices, body(): ahead = lax.ppermute(tmat[:early], 'col', [(0, 1)])  5.67 us
    ppermute x1, starting transfers between devices, body(): ahead = lax.ppermute(tmat[:early], 'col', [(0, 1)])  4.89 us
    ppermute x1, waiting for transfers between devices, body(): other = x + lax.ppermute(x, 'col', [(1, 0)])  4.85 us
    pallas_call x1, Pallas kernels, gather_rows(): pl.pallas_call(gather_kernel, out_shape=[jax.ShapeDtypeStruct((picked //...  4.75 us
  transfers between devices with their start and end apart: 15, of which 8 were waited for; matrix products, arithmetic and copies ran while one was open for 0% of the time, Pallas kernels for 16%

profile of v6, /device:TPU:0, one launch (start us, length us, event | category | flops | bytes accessed | tf_op | source)
XLA Modules:
  0.0 88.9 jit_solution(10679976886452831179)
XLA Ops:
  0.0 1.2 %slice.3 = bf16[768,512]{1,0:T(8,128)(2,1)S(1)} slice(bf16[4096,512]{1,0:T(8,128)(2,1)} %tmat.3), slice={[0:768], [0:512]} | slice | bytes 1572864 | tf_op jit(solution)/shard_map/slice | solution.py:438
  1.2 4.9 %collective-permute-start.2 = (bf16[768,512]{1,0:T(8,128)(2,1)S(1)}, bf16[768,512]{1,0:T(8,128)(2,1)S(1)}, u32[]{:S(2)}, u32[]{:S(2)}) collective-permute-start(bf16[768,512]{1,0:T(8,128)(2,1)S(1)} %slice.3), channel_id=1, source_target_pairs={{0,1},{2,3},{4,5},{6,7},{8,9},{10,11},{12,13},{14,15},{16,17},{18,... | collective-permute-start | bytes 2359304 | tf_op jit(solution)/shard_map/ppermute | solution.py:438
  6.1 0.7 copy-done.1
  6.8 4.7 %shard_map.56 = (bf16[256,512]{1,0:T(8,128)(2,1)S(1)}, bf16[256,512]{1,0:T(8,128)(2,1)S(1)}, bf16[4096,512]{1,0:T(8,128)(2,1)S(1)}, bf16[256,128,128]{2,1,0:T(8,128)(2,1)S(1)}) custom-call(s32[2,256]{1,0:T(2,128)S(1)} %copy-done.1, bf16[4096,512]{1,0:T(8,128)(2,1)} %tmat.3, bf16[256,128,128]{2,1,0:T(8,128)(2,1)} %blocks.1), custom_call_target="tpu_custom_call" | custom-call | flops 1 | bytes 1 | tf_op jit(solution)/shard_map/pallas_call | solution.py:168
  11.5 0.7 collective-permute-start
  12.2 0.7 collective-permute-start.1
  13.6 0.7 shard_map.55
  14.3 0.8 shard_map.57.own
  15.1 2.1 %shard_map.58.sent = bf16[1664,512]{1,0:T(8,128)(2,1)S(1)} custom-call(s32[1,128]{1,0:T(1,128)S(1)} %get-tuple-element.43.first, s32[1,128]{1,0:T(1,128)S(1)} %get-tuple-element.44.owner_row, s32[1,512]{1,0:T(1,128)S(1)} %get-tuple-element.45.entries, bf16[256,128,128]{2,1,0:T(8,128)(2,1)S(1)} %get-tuple-element.46.blocks, ...), custom_call_target="tpu_custom_call" | custom-call | flops 1 | bytes 1 | tf_op jit(solution)/shard_map/pallas_call | solution.py:229
  17.2 5.7 %collective-permute-done.2.ahead = bf16[768,512]{1,0:T(8,128)(2,1)S(1)} collective-permute-done((bf16[768,512]{1,0:T(8,128)(2,1)S(1)}, bf16[768,512]{1,0:T(8,128)(2,1)S(1)}, u32[]{:S(2)}, u32[]{:S(2)}) %collective-permute-start.2) | collective-permute-done | bytes 786464 | tf_op jit(solution)/shard_map/ppermute | solution.py:438
  22.8 2.5 %collective-permute-start.5 = (bf16[1664,512]{1,0:T(8,128)(2,1)S(1)}, bf16[1664,512]{1,0:T(8,128)(2,1)S(1)}, u32[]{:S(2)}, u32[]{:S(2)}) collective-permute-start(bf16[1664,512]{1,0:T(8,128)(2,1)S(1)} %shard_map.58.sent), channel_id=1, source_target_pairs={{0,1},{1,0},{2,3},{3,2},{4,5},{5,4},{6,7},{7,6},{8,9},{9,8},{10,11... | collective-permute-start | bytes 5111816 | tf_op jit(solution)/shard_map/ppermute | solution.py:443
  25.3 5.9 %shard_map.59 = (bf16[2432,512]{1,0:T(8,128)(2,1)S(1)}, f32[512,512]{1,0:T(8,128)S(1)}) custom-call(s32[1,128]{1,0:T(1,128)S(1)} %get-tuple-element.43.first, s32[1,128]{1,0:T(1,128)S(1)} %get-tuple-element.44.owner_row, s32[1,512]{1,0:T(1,128)S(1)} %get-tuple-element.45.entries, bf16[256,128,128]{2,1,0:T(8,128)(2,1)S(1)} %get-tuple-element.46.blocks, ...), custom_call_target="tpu_custom_call" | custom-call | flops 1 | bytes 1 | tf_op jit(solution)/shard_map/pallas_call | solution.py:275
  31.3 0.7 collective-permute-start.3
  32.1 0.7 collective-permute-start.4
  32.8 0.2 shard_map.62
  33.0 0.7 collective-permute-start.6
  33.7 27.9 %collective-permute-done.5.got = bf16[1664,512]{1,0:T(8,128)(2,1)S(1)} collective-permute-done((bf16[1664,512]{1,0:T(8,128)(2,1)S(1)}, bf16[1664,512]{1,0:T(8,128)(2,1)S(1)}, u32[]{:S(2)}, u32[]{:S(2)}) %collective-permute-start.5) | collective-permute-done | bytes 1703968 | tf_op jit(solution)/shard_map/ppermute | solution.py:443
  61.6 1.6 %shard_map.65 = f32[512,512]{1,0:T(8,128)S(1)} custom-call(bf16[1664,512]{1,0:T(8,128)(2,1)S(1)} %collective-permute-done.5.got, bf16[1664,512]{1,0:T(8,128)(2,1)S(1)} %get-tuple-element.67.partner, f32[512,512]{1,0:T(8,128)S(1)} %get-tuple-element.68.known), custom_call_target="tpu_custom_call" | custom-call | flops 1 | bytes 1 | tf_op jit(solution)/shard_map/pallas_call | solution.py:335
  63.4 1.9 %collective-permute-done.8.refs_1_ = f32[8,32,512]{2,1,0:T(8,128)S(1)} collective-permute-done((f32[8,32,512]{2,1,0:T(8,128)S(1)}, f32[8,32,512]{2,1,0:T(8,128)S(1)}, u32[]{:S(2)}, u32[]{:S(2)}) %collective-permute-start.8) | collective-permute-done | bytes 524320 | tf_op jit(solution)/shard_map/ppermute | solution.py:394
  65.3 1.6 %collective-permute-start.11 = (f32[4,32,256]{2,1,0:T(8,128)S(1)}, f32[4,32,256]{2,1,0:T(8,128)S(1)}, u32[]{:S(2)}, u32[]{:S(2)}) collective-permute-start(f32[4,32,256]{2,1,0:T(8,128)S(1)} %get-tuple-element.76), channel_id=1, source_target_pairs={{0,8},{2,10},{4,12},{6,14},{8,0},{10,2},{12,4},{14,6},{16,24},{18,... | collective-permute-start | bytes 393224 | tf_op jit(solution)/shard_map/ppermute | solution.py:394
  67.0 1.6 %collective-permute-start.9 = (f32[4,32,256]{2,1,0:T(8,128)S(1)}, f32[4,32,256]{2,1,0:T(8,128)S(1)}, u32[]{:S(2)}, u32[]{:S(2)}) collective-permute-start(f32[4,32,256]{2,1,0:T(8,128)S(1)} %get-tuple-element.72), channel_id=1, source_target_pairs={{0,4},{2,6},{4,0},{6,2},{8,12},{10,14},{12,8},{14,10},{16,20},{18,... | collective-permute-start | bytes 393224 | tf_op jit(solution)/shard_map/ppermute | solution.py:394
  68.6 2.3 %collective-permute-done.11.refs_1_ = f32[4,32,256]{2,1,0:T(8,128)S(1)} collective-permute-done((f32[4,32,256]{2,1,0:T(8,128)S(1)}, f32[4,32,256]{2,1,0:T(8,128)S(1)}, u32[]{:S(2)}, u32[]{:S(2)}) %collective-permute-start.11) | collective-permute-done | bytes 131104 | tf_op jit(solution)/shard_map/ppermute | solution.py:394
  70.9 1.6 %collective-permute-start.12 = (f32[2,32,256]{2,1,0:T(8,128)S(1)}, f32[2,32,256]{2,1,0:T(8,128)S(1)}, u32[]{:S(2)}, u32[]{:S(2)}) collective-permute-start(f32[2,32,256]{2,1,0:T(8,128)S(1)} %get-tuple-element.78), channel_id=1, source_target_pairs={{0,4},{2,6},{4,0},{6,2},{8,12},{10,14},{12,8},{14,10},{16,20},{18,... | collective-permute-start | bytes 196616 | tf_op jit(solution)/shard_map/ppermute | solution.py:394
  72.5 1.6 %collective-permute-start.10 = (f32[2,32,256]{2,1,0:T(8,128)S(1)}, f32[2,32,256]{2,1,0:T(8,128)S(1)}, u32[]{:S(2)}, u32[]{:S(2)}) collective-permute-start(f32[2,32,256]{2,1,0:T(8,128)S(1)} %get-tuple-element.74), channel_id=1, source_target_pairs={{0,8},{2,10},{4,12},{6,14},{8,0},{10,2},{12,4},{14,6},{16,24},{18,... | collective-permute-start | bytes 196616 | tf_op jit(solution)/shard_map/ppermute | solution.py:394
  74.2 1.1 %collective-permute-done.12.refs_3_ = f32[2,32,256]{2,1,0:T(8,128)S(1)} collective-permute-done((f32[2,32,256]{2,1,0:T(8,128)S(1)}, f32[2,32,256]{2,1,0:T(8,128)S(1)}, u32[]{:S(2)}, u32[]{:S(2)}) %collective-permute-start.12) | collective-permute-done | bytes 65568 | tf_op jit(solution)/shard_map/ppermute | solution.py:394
  75.3 1.6 %collective-permute-done.10.refs_1_ = f32[2,32,256]{2,1,0:T(8,128)S(1)} collective-permute-done((f32[2,32,256]{2,1,0:T(8,128)S(1)}, f32[2,32,256]{2,1,0:T(8,128)S(1)}, u32[]{:S(2)}, u32[]{:S(2)}) %collective-permute-start.10) | collective-permute-done | bytes 65568 | tf_op jit(solution)/shard_map/ppermute | solution.py:394
  76.9 2.7 %collective-permute-start.13 = (f32[1,32,512]{2,1,0:T(8,128)S(1)}, f32[1,32,512]{2,1,0:T(8,128)S(1)}, u32[]{:S(2)}, u32[]{:S(2)}) collective-permute-start(f32[1,32,512]{2,1,0:T(8,128)S(1)} %get-tuple-element.80), channel_id=1, source_target_pairs={{0,16},{2,18},{4,20},{6,22},{8,24},{10,26},{12,28},{14,30},{16,0},... | collective-permute-start | bytes 196616 | tf_op jit(solution)/shard_map/ppermute | solution.py:394
  79.6 0.7 collective-permute-start.7
  80.2 1.9 %collective-permute-done.13 = f32[1,32,512]{2,1,0:T(8,128)S(1)} collective-permute-done((f32[1,32,512]{2,1,0:T(8,128)S(1)}, f32[1,32,512]{2,1,0:T(8,128)S(1)}, u32[]{:S(2)}, u32[]{:S(2)}) %collective-permute-start.13) | collective-permute-done | bytes 65568 | tf_op jit(solution)/shard_map/ppermute | solution.py:394
  82.1 1.3 %collective-permute-start.14 = (f32[1,32,512]{2,1,0:T(8,128)S(1)}, f32[1,32,512]{2,1,0:T(8,128)S(1)}, u32[]{:S(2)}, u32[]{:S(2)}) collective-permute-start(f32[1,32,512]{2,1,0:T(8,128)S(1)} %add.10), channel_id=1, source_target_pairs={{1,0},{3,2},{5,4},{7,6},{9,8},{11,10},{13,12},{15,14},{17,16},{19,... | collective-permute-start | bytes 196616 | tf_op jit(solution)/shard_map/ppermute | solution.py:465
  83.5 4.8 %collective-permute-done.14 = f32[1,32,512]{2,1,0:T(8,128)S(1)} collective-permute-done((f32[1,32,512]{2,1,0:T(8,128)S(1)}, f32[1,32,512]{2,1,0:T(8,128)S(1)}, u32[]{:S(2)}, u32[]{:S(2)}) %collective-permute-start.14) | collective-permute-done | bytes 65568 | tf_op jit(solution)/shard_map/ppermute | solution.py:465
  88.3 0.6 select_bitcast_fusion
  (22 shorter events, 0.5 us)
Async XLA Ops:
  1.2 12.4 %copy-start = (s32[256,2]{0,1:T(2,128)S(1)}, s32[256,2]{0,1:T(2,128)}, u32[]{:S(2)}) copy-start(s32[256,2]{0,1:T(2,128)} %param.7) | copy-start | bytes 6148
  1.2 21.6 %collective-permute-start.2 = (bf16[768,512]{1,0:T(8,128)(2,1)S(1)}, bf16[768,512]{1,0:T(8,128)(2,1)S(1)}, u32[]{:S(2)}, u32[]{:S(2)}) collective-permute-start(bf16[768,512]{1,0:T(8,128)(2,1)S(1)} %slice.3), channel_id=1, source_target_pairs={{0,1},{2,3},{4,5},{6,7},{8,9},{10,11},{12,13},{14,15},{16,17},{18,... | collective-permute-start | bytes 2359304 | tf_op jit(solution)/shard_map/ppermute | solution.py:438
  6.1 0.7 copy-start.1
  11.5 3.5 %collective-permute-start = (bf16[256,512]{1,0:T(8,128)(2,1)S(1)}, bf16[256,512]{1,0:T(8,128)(2,1)S(1)}, u32[]{:S(2)}, u32[]{:S(2)}) collective-permute-start(bf16[256,512]{1,0:T(8,128)(2,1)S(1)} %get-tuple-element.48), channel_id=1, source_target_pairs={{3,5},{7,9},{11,13},{15,17},{19,21},{23,25},{27,29},{5,3},{9,7},{1... | collective-permute-start | bytes 786440 | tf_op jit(solution)/shard_map/ppermute | solution.py:424
  12.2 2.9 %collective-permute-start.1 = (bf16[256,512]{1,0:T(8,128)(2,1)S(1)}, bf16[256,512]{1,0:T(8,128)(2,1)S(1)}, u32[]{:S(2)}, u32[]{:S(2)}) collective-permute-start(bf16[256,512]{1,0:T(8,128)(2,1)S(1)} %get-tuple-element.49), channel_id=1, source_target_pairs={{1,3},{5,7},{9,11},{13,15},{17,19},{21,23},{25,27},{29,31},{3,1},{... | collective-permute-start | bytes 786440 | tf_op jit(solution)/shard_map/ppermute | solution.py:424
  22.8 38.8 %collective-permute-start.5 = (bf16[1664,512]{1,0:T(8,128)(2,1)S(1)}, bf16[1664,512]{1,0:T(8,128)(2,1)S(1)}, u32[]{:S(2)}, u32[]{:S(2)}) collective-permute-start(bf16[1664,512]{1,0:T(8,128)(2,1)S(1)} %shard_map.58.sent), channel_id=1, source_target_pairs={{0,1},{1,0},{2,3},{3,2},{4,5},{5,4},{6,7},{7,6},{8,9},{9,8},{10,11... | collective-permute-start | bytes 5111816 | tf_op jit(solution)/shard_map/ppermute | solution.py:443
  31.3 0.7 collective-permute-start.3
  32.1 0.9 collective-permute-start.4
  33.0 0.7 collective-permute-start.6
  63.3 2.0 %collective-permute-start.8 = (f32[8,32,512]{2,1,0:T(8,128)S(1)}, f32[8,32,512]{2,1,0:T(8,128)S(1)}, u32[]{:S(2)}, u32[]{:S(2)}) collective-permute-start(f32[8,32,512]{2,1,0:T(8,128)S(1)} %get-tuple-element.70), channel_id=1, source_target_pairs={{0,2},{2,0},{4,6},{6,4},{8,10},{10,8},{12,14},{14,12},{16,18},{18,... | collective-permute-start | bytes 1572872 | tf_op jit(solution)/shard_map/ppermute | solution.py:394
  65.3 5.6 %collective-permute-start.11 = (f32[4,32,256]{2,1,0:T(8,128)S(1)}, f32[4,32,256]{2,1,0:T(8,128)S(1)}, u32[]{:S(2)}, u32[]{:S(2)}) collective-permute-start(f32[4,32,256]{2,1,0:T(8,128)S(1)} %get-tuple-element.76), channel_id=1, source_target_pairs={{0,8},{2,10},{4,12},{6,14},{8,0},{10,2},{12,4},{14,6},{16,24},{18,... | collective-permute-start | bytes 393224 | tf_op jit(solution)/shard_map/ppermute | solution.py:394
  67.0 5.5 %collective-permute-start.9 = (f32[4,32,256]{2,1,0:T(8,128)S(1)}, f32[4,32,256]{2,1,0:T(8,128)S(1)}, u32[]{:S(2)}, u32[]{:S(2)}) collective-permute-start(f32[4,32,256]{2,1,0:T(8,128)S(1)} %get-tuple-element.72), channel_id=1, source_target_pairs={{0,4},{2,6},{4,0},{6,2},{8,12},{10,14},{12,8},{14,10},{16,20},{18,... | collective-permute-start | bytes 393224 | tf_op jit(solution)/shard_map/ppermute | solution.py:394
  70.9 4.3 %collective-permute-start.12 = (f32[2,32,256]{2,1,0:T(8,128)S(1)}, f32[2,32,256]{2,1,0:T(8,128)S(1)}, u32[]{:S(2)}, u32[]{:S(2)}) collective-permute-start(f32[2,32,256]{2,1,0:T(8,128)S(1)} %get-tuple-element.78), channel_id=1, source_target_pairs={{0,4},{2,6},{4,0},{6,2},{8,12},{10,14},{12,8},{14,10},{16,20},{18,... | collective-permute-start | bytes 196616 | tf_op jit(solution)/shard_map/ppermute | solution.py:394
  72.5 4.3 %collective-permute-start.10 = (f32[2,32,256]{2,1,0:T(8,128)S(1)}, f32[2,32,256]{2,1,0:T(8,128)S(1)}, u32[]{:S(2)}, u32[]{:S(2)}) collective-permute-start(f32[2,32,256]{2,1,0:T(8,128)S(1)} %get-tuple-element.74), channel_id=1, source_target_pairs={{0,8},{2,10},{4,12},{6,14},{8,0},{10,2},{12,4},{14,6},{16,24},{18,... | collective-permute-start | bytes 196616 | tf_op jit(solution)/shard_map/ppermute | solution.py:394
  76.9 5.2 %collective-permute-start.13 = (f32[1,32,512]{2,1,0:T(8,128)S(1)}, f32[1,32,512]{2,1,0:T(8,128)S(1)}, u32[]{:S(2)}, u32[]{:S(2)}) collective-permute-start(f32[1,32,512]{2,1,0:T(8,128)S(1)} %get-tuple-element.80), channel_id=1, source_target_pairs={{0,16},{2,18},{4,20},{6,22},{8,24},{10,26},{12,28},{14,30},{16,0},... | collective-permute-start | bytes 196616 | tf_op jit(solution)/shard_map/ppermute | solution.py:394
  79.6 3.9 %collective-permute-start.7 = (f32[1,32,512]{2,1,0:T(8,128)S(1)}, f32[1,32,512]{2,1,0:T(8,128)S(1)}, u32[]{:S(2)}, u32[]{:S(2)}) collective-permute-start(f32[1,32,512]{2,1,0:T(8,128)S(1)} %get-tuple-element.65), channel_id=1, source_target_pairs={{1,17},{3,19},{5,21},{7,23},{9,25},{11,27},{13,29},{15,31},{17,1},... | collective-permute-start | bytes 196616 | tf_op jit(solution)/shard_map/ppermute | solution.py:394
  82.1 6.2 %collective-permute-start.14 = (f32[1,32,512]{2,1,0:T(8,128)S(1)}, f32[1,32,512]{2,1,0:T(8,128)S(1)}, u32[]{:S(2)}, u32[]{:S(2)}) collective-permute-start(f32[1,32,512]{2,1,0:T(8,128)S(1)} %add.10), channel_id=1, source_target_pairs={{1,0},{3,2},{5,4},{7,6},{9,8},{11,10},{13,12},{15,14},{17,16},{19,... | collective-permute-start | bytes 196616 | tf_op jit(solution)/shard_map/ppermute | solution.py:465

commit v7 on v6

--- a/solution.py
+++ b/solution.py
@@ -358,53 +358,33 @@
     )(*lists, blocks, panel, odd, even, after)
 
 
-def fold_kernel(bit, inner, counts, *refs):
-    keep, send = refs[-2:]
+def fold_kernel(bit, *refs):
+    *parts, keep, send = refs
     mine = (lax.axis_index("dom") // bit) % 2
     for t in range(keep.shape[0]):
-        outer, rest = divmod(t, inner)
         for out, side in ((keep, mine), (send, 1 - mine)):
-            place = (2 * outer + side) * inner + rest
-            sources, col = refs[:-2], 0
-            for count, begin, width in counts:
-                cols = pl.ds(begin, width)
-                total = sources[0][place, :, cols]
-                for part in sources[1:count]:
-                    total += part[place, :, cols]
-                out[t, :, pl.ds(col, width)] = total
-                sources, col = sources[count:], col + width
-
-
-def fold(bit, inner, *columns):
-    targets, rows, _ = columns[0][0][0].shape
-    half = jax.ShapeDtypeStruct((targets // 2, rows, sum(width for _, _, width in columns)), jnp.float32)
-    arrays = [a for some, _, _ in columns for a in some]
-    return pl.pallas_call(
-        functools.partial(fold_kernel, bit, inner, [(len(some), begin, width) for some, begin, width in columns]),
-        out_shape=[half] * 2,
-        in_specs=[NEAR] * len(arrays),
+            total = parts[0][2 * t + side]
+            for part in parts[1:]:
+                total += part[2 * t + side].astype(jnp.float32)
+            out[t] = total.astype(out.dtype)
+
+
+def fold(bit, parts, kind):
+    targets, rows, width = parts[0].shape
+    shape = (targets // 2, rows, width)
+    return pl.pallas_call(
+        functools.partial(fold_kernel, bit),
+        out_shape=[jax.ShapeDtypeStruct(shape, jnp.float32), jax.ShapeDtypeStruct(shape, kind)],
+        in_specs=[NEAR] * len(parts),
         out_specs=[NEAR] * 2,
         compiler_params=room_for(),
         cost_estimate=near_nothing(),
-    )(*arrays)
-
-
-def step(route, bit, inner, *columns):
-    keep, send = fold(bit, inner, *columns)
+    )(*parts)
+
+
+def step(route, bit, parts, kind=jnp.float32):
+    keep, send = fold(bit, parts, kind)
     return [keep, lax.ppermute(send, *route(bit))]
-
-
-def scatter(x, route):
-    targets, rows, width = x.shape
-    half = width // 2
-    whole = step(route, 1, 1, ([x], 0, width))
-    left, right = step(route, 2, 1, (whole, 0, half)), step(route, 4, 2, (whole, half, half))
-    left, right = step(route, 4, 1, (left, 0, half)), step(route, 2, 1, (right, 0, half))
-    bit, columns = 8, [(left, 0, half), (right, 0, half)]
-    while bit < targets // 2:
-        columns = [(step(route, bit, 1, *columns), 0, width)]
-        bit *= 2
-    return columns
 
 
 def body(tmat, stored_mass_blocks, block_index, live_block_count, send_rows):
@@ -452,16 +432,18 @@
 
     parts, bit = [own.reshape(n_dom, share, width)], 1
     while bit < n_dom // 2:
-        parts = step(panel_column, bit, 1, (parts, 0, width))
+        parts = step(panel_column, bit, parts)
         if bit == 2:
             parts[1], known, partner = lax.optimization_barrier((parts[1], known, partner))
         bit *= 2
     got, parts[1] = lax.optimization_barrier((got, parts[1]))
 
     x = meet(got, partner, known, n_col)
-    keep, got = step(both, bit, 1, *scatter(x.reshape(n_dom, share, width), both))
-    own_keep, own_got = step(panel_column, bit, 1, (parts, 0, width))
-    x = keep + got
+    sums = [x.reshape(n_dom, share, width)]
+    for b in range(bit.bit_length()):
+        sums = step(both, 1 << b, sums, jnp.bfloat16 if b == 1 else jnp.float32)
+    own_keep, own_got = step(panel_column, bit, parts)
+    x = sums[0] + sums[1]
     other = x + lax.ppermute(x, "col", [(1, 0)])
     return jnp.where(col == owner, own_keep + own_got, other).reshape(share, width)
 

time: 89.3 us -> 88.4 us (0.990)
  starting transfers between devices: 21.9 us -> 18.7 us
  waiting for transfers between devices: 47.3 us -> 49.6 us
    ppermute x10 -> x8, starting transfers between devices: 11.9 us -> 8.66 us  [step(): return [keep, lax.ppermute(send, *route(bit))]]
    ppermute x10 -> x8, waiting for transfers between devices: 8.82 us -> 11.2 us  [step(): return [keep, lax.ppermute(send, *route(bit))]]
  transfers between devices with their start and end apart: 15 -> 13, of which waited for: 8 -> 7; matrix products, arithmetic and copies ran while one was open for 0% -> 0% of each run, Pallas kernels for 16% -> 17%
where the time goes in v7:
time: 88.4 us; the launch traced here: 88.1 us
  waiting for transfers between devices  49.6 us (56%)
  starting transfers between devices  18.7 us (21%)
  Pallas kernels  16.3 us (18%)
  local copies, waits for them, and re-layouts  1.87 us (2%)
  between operations  0.9 us (1%)
    ppermute x1, waiting for transfers between devices, body(): got = lax.ppermute(sent, 'col', [(0, 1), (1, 0)])  27.9 us
    ppermute x8, waiting for transfers between devices, step(): return [keep, lax.ppermute(send, *route(bit))]  11.2 us
    ppermute x8, starting transfers between devices, step(): return [keep, lax.ppermute(send, *route(bit))]  8.66 us
    pallas_call x1, Pallas kernels, panel_work(): pl.pallas_call(functools.partial(panel_kernel, panel.shape[0] // bsize, n...  5.89 us
    ppermute x1, waiting for transfers between devices, body(): ahead = lax.ppermute(tmat[:early], 'col', [(0, 1)])  5.67 us
    ppermute x1, starting transfers between devices, body(): ahead = lax.ppermute(tmat[:early], 'col', [(0, 1)])  4.89 us
    ppermute x1, waiting for transfers between devices, body(): other = x + lax.ppermute(x, 'col', [(1, 0)])  4.85 us
    pallas_call x1, Pallas kernels, gather_rows(): pl.pallas_call(gather_kernel, out_shape=[jax.ShapeDtypeStruct((picked //...  4.75 us
  transfers between devices with their start and end apart: 13, of which 7 were waited for; matrix products, arithmetic and copies ran while one was open for 0% of the time, Pallas kernels for 17%

profile of v7, /device:TPU:0, one launch (start us, length us, event | category | flops | bytes accessed | tf_op | source)
XLA Modules:
  0.0 88.1 jit_solution(17559397672657297489)
XLA Ops:
  0.0 1.2 %slice.3 = bf16[768,512]{1,0:T(8,128)(2,1)S(1)} slice(bf16[4096,512]{1,0:T(8,128)(2,1)} %tmat.3), slice={[0:768], [0:512]} | slice | bytes 1572864 | tf_op jit(solution)/shard_map/slice | solution.py:418
  1.2 4.9 %collective-permute-start.2 = (bf16[768,512]{1,0:T(8,128)(2,1)S(1)}, bf16[768,512]{1,0:T(8,128)(2,1)S(1)}, u32[]{:S(2)}, u32[]{:S(2)}) collective-permute-start(bf16[768,512]{1,0:T(8,128)(2,1)S(1)} %slice.3), channel_id=1, source_target_pairs={{0,1},{2,3},{4,5},{6,7},{8,9},{10,11},{12,13},{14,15},{16,17},{18,... | collective-permute-start | bytes 2359304 | tf_op jit(solution)/shard_map/ppermute | solution.py:418
  6.1 0.7 copy-done.1
  6.8 4.7 %shard_map.56 = (bf16[256,512]{1,0:T(8,128)(2,1)S(1)}, bf16[256,512]{1,0:T(8,128)(2,1)S(1)}, bf16[4096,512]{1,0:T(8,128)(2,1)S(1)}, bf16[256,128,128]{2,1,0:T(8,128)(2,1)S(1)}) custom-call(s32[2,256]{1,0:T(2,128)S(1)} %copy-done.1, bf16[4096,512]{1,0:T(8,128)(2,1)} %tmat.3, bf16[256,128,128]{2,1,0:T(8,128)(2,1)} %blocks.1), custom_call_target="tpu_custom_call" | custom-call | flops 1 | bytes 1 | tf_op jit(solution)/shard_map/pallas_call | solution.py:168
  11.5 0.7 collective-permute-start
  12.2 0.7 collective-permute-start.1
  13.6 0.7 shard_map.55
  14.3 0.8 shard_map.57.own
  15.1 2.1 %shard_map.58.sent = bf16[1664,512]{1,0:T(8,128)(2,1)S(1)} custom-call(s32[1,128]{1,0:T(1,128)S(1)} %get-tuple-element.39.first, s32[1,128]{1,0:T(1,128)S(1)} %get-tuple-element.40.owner_row, s32[1,512]{1,0:T(1,128)S(1)} %get-tuple-element.41.entries, bf16[256,128,128]{2,1,0:T(8,128)(2,1)S(1)} %get-tuple-element.42.blocks, ...), custom_call_target="tpu_custom_call" | custom-call | flops 1 | bytes 1 | tf_op jit(solution)/shard_map/pallas_call | solution.py:229
  17.2 5.7 %collective-permute-done.2.ahead = bf16[768,512]{1,0:T(8,128)(2,1)S(1)} collective-permute-done((bf16[768,512]{1,0:T(8,128)(2,1)S(1)}, bf16[768,512]{1,0:T(8,128)(2,1)S(1)}, u32[]{:S(2)}, u32[]{:S(2)}) %collective-permute-start.2) | collective-permute-done | bytes 786464 | tf_op jit(solution)/shard_map/ppermute | solution.py:418
  22.8 2.5 %collective-permute-start.5 = (bf16[1664,512]{1,0:T(8,128)(2,1)S(1)}, bf16[1664,512]{1,0:T(8,128)(2,1)S(1)}, u32[]{:S(2)}, u32[]{:S(2)}) collective-permute-start(bf16[1664,512]{1,0:T(8,128)(2,1)S(1)} %shard_map.58.sent), channel_id=1, source_target_pairs={{0,1},{1,0},{2,3},{3,2},{4,5},{5,4},{6,7},{7,6},{8,9},{9,8},{10,11... | collective-permute-start | bytes 5111816 | tf_op jit(solution)/shard_map/ppermute | solution.py:423
  25.3 5.9 %shard_map.59 = (bf16[2432,512]{1,0:T(8,128)(2,1)S(1)}, f32[512,512]{1,0:T(8,128)S(1)}) custom-call(s32[1,128]{1,0:T(1,128)S(1)} %get-tuple-element.39.first, s32[1,128]{1,0:T(1,128)S(1)} %get-tuple-element.40.owner_row, s32[1,512]{1,0:T(1,128)S(1)} %get-tuple-element.41.entries, bf16[256,128,128]{2,1,0:T(8,128)(2,1)S(1)} %get-tuple-element.42.blocks, ...), custom_call_target="tpu_custom_call" | custom-call | flops 1 | bytes 1 | tf_op jit(solution)/shard_map/pallas_call | solution.py:275
  31.2 0.1 shard_map.60
  31.3 0.7 collective-permute-start.3
  32.0 0.1 shard_map.61
  32.1 0.7 collective-permute-start.4
  32.8 0.2 shard_map.62
  33.0 0.7 collective-permute-start.6
  33.7 27.9 %collective-permute-done.5.got = bf16[1664,512]{1,0:T(8,128)(2,1)S(1)} collective-permute-done((bf16[1664,512]{1,0:T(8,128)(2,1)S(1)}, bf16[1664,512]{1,0:T(8,128)(2,1)S(1)}, u32[]{:S(2)}, u32[]{:S(2)}) %collective-permute-start.5) | collective-permute-done | bytes 1703968 | tf_op jit(solution)/shard_map/ppermute | solution.py:423
  61.6 1.6 %shard_map.65 = f32[512,512]{1,0:T(8,128)S(1)} custom-call(bf16[1664,512]{1,0:T(8,128)(2,1)S(1)} %collective-permute-done.5.got, bf16[1664,512]{1,0:T(8,128)(2,1)S(1)} %get-tuple-element.63.partner, f32[512,512]{1,0:T(8,128)S(1)} %get-tuple-element.64.known), custom_call_target="tpu_custom_call" | custom-call | flops 1 | bytes 1 | tf_op jit(solution)/shard_map/pallas_call | solution.py:335
  63.2 0.1 shard_map.66
  63.4 1.9 %collective-permute-done.8.refs_1_ = f32[8,32,512]{2,1,0:T(8,128)S(1)} collective-permute-done((f32[8,32,512]{2,1,0:T(8,128)S(1)}, f32[8,32,512]{2,1,0:T(8,128)S(1)}, u32[]{:S(2)}, u32[]{:S(2)}) %collective-permute-start.8) | collective-permute-done | bytes 524320 | tf_op jit(solution)/shard_map/ppermute | solution.py:387
  65.3 1.6 %collective-permute-start.9 = (bf16[4,32,512]{2,1,0:T(8,128)(2,1)S(1)}, bf16[4,32,512]{2,1,0:T(8,128)(2,1)S(1)}, u32[]{:S(2)}, u32[]{:S(2)}) collective-permute-start(bf16[4,32,512]{2,1,0:T(8,128)(2,1)S(1)} %get-tuple-element.68), channel_id=1, source_target_pairs={{0,4},{2,6},{4,0},{6,2},{8,12},{10,14},{12,8},{14,10},{16,20},{18,... | collective-permute-start | bytes 393224 | tf_op jit(solution)/shard_map/ppermute | solution.py:387
  66.9 4.0 %collective-permute-done.9.refs_1_ = bf16[4,32,512]{2,1,0:T(8,128)(2,1)S(1)} collective-permute-done((bf16[4,32,512]{2,1,0:T(8,128)(2,1)S(1)}, bf16[4,32,512]{2,1,0:T(8,128)(2,1)S(1)}, u32[]{:S(2)}, u32[]{:S(2)}) %collective-permute-start.9) | collective-permute-done | bytes 131104 | tf_op jit(solution)/shard_map/ppermute | solution.py:387
  71.0 1.6 %collective-permute-start.10 = (f32[2,32,512]{2,1,0:T(8,128)S(1)}, f32[2,32,512]{2,1,0:T(8,128)S(1)}, u32[]{:S(2)}, u32[]{:S(2)}) collective-permute-start(f32[2,32,512]{2,1,0:T(8,128)S(1)} %get-tuple-element.70), channel_id=1, source_target_pairs={{0,8},{2,10},{4,12},{6,14},{8,0},{10,2},{12,4},{14,6},{16,24},{18,... | collective-permute-start | bytes 393224 | tf_op jit(solution)/shard_map/ppermute | solution.py:387
  72.6 3.4 %collective-permute-done.10.refs_1_ = f32[2,32,512]{2,1,0:T(8,128)S(1)} collective-permute-done((f32[2,32,512]{2,1,0:T(8,128)S(1)}, f32[2,32,512]{2,1,0:T(8,128)S(1)}, u32[]{:S(2)}, u32[]{:S(2)}) %collective-permute-start.10) | collective-permute-done | bytes 131104 | tf_op jit(solution)/shard_map/ppermute | solution.py:387
  76.0 2.7 %collective-permute-start.11 = (f32[1,32,512]{2,1,0:T(8,128)S(1)}, f32[1,32,512]{2,1,0:T(8,128)S(1)}, u32[]{:S(2)}, u32[]{:S(2)}) collective-permute-start(f32[1,32,512]{2,1,0:T(8,128)S(1)} %get-tuple-element.72), channel_id=1, source_target_pairs={{0,16},{2,18},{4,20},{6,22},{8,24},{10,26},{12,28},{14,30},{16,0},... | collective-permute-start | bytes 196616 | tf_op jit(solution)/shard_map/ppermute | solution.py:387
  78.7 0.7 collective-permute-start.7
  79.4 1.9 %collective-permute-done.11 = f32[1,32,512]{2,1,0:T(8,128)S(1)} collective-permute-done((f32[1,32,512]{2,1,0:T(8,128)S(1)}, f32[1,32,512]{2,1,0:T(8,128)S(1)}, u32[]{:S(2)}, u32[]{:S(2)}) %collective-permute-start.11) | collective-permute-done | bytes 65568 | tf_op jit(solution)/shard_map/ppermute | solution.py:387
  81.3 1.3 %collective-permute-start.12 = (f32[1,32,512]{2,1,0:T(8,128)S(1)}, f32[1,32,512]{2,1,0:T(8,128)S(1)}, u32[]{:S(2)}, u32[]{:S(2)}) collective-permute-start(f32[1,32,512]{2,1,0:T(8,128)S(1)} %add.10), channel_id=1, source_target_pairs={{1,0},{3,2},{5,4},{7,6},{9,8},{11,10},{13,12},{15,14},{17,16},{19,... | collective-permute-start | bytes 196616 | tf_op jit(solution)/shard_map/ppermute | solution.py:447
  82.6 4.8 %collective-permute-done.12 = f32[1,32,512]{2,1,0:T(8,128)S(1)} collective-permute-done((f32[1,32,512]{2,1,0:T(8,128)S(1)}, f32[1,32,512]{2,1,0:T(8,128)S(1)}, u32[]{:S(2)}, u32[]{:S(2)}) %collective-permute-start.12) | collective-permute-done | bytes 65568 | tf_op jit(solution)/shard_map/ppermute | solution.py:447
  87.4 0.6 select_bitcast_fusion
  (16 shorter events, 0.3 us)
Async XLA Ops:
  1.2 12.4 %copy-start = (s32[256,2]{0,1:T(2,128)S(1)}, s32[256,2]{0,1:T(2,128)}, u32[]{:S(2)}) copy-start(s32[256,2]{0,1:T(2,128)} %param.7) | copy-start | bytes 6148
  1.2 21.6 %collective-permute-start.2 = (bf16[768,512]{1,0:T(8,128)(2,1)S(1)}, bf16[768,512]{1,0:T(8,128)(2,1)S(1)}, u32[]{:S(2)}, u32[]{:S(2)}) collective-permute-start(bf16[768,512]{1,0:T(8,128)(2,1)S(1)} %slice.3), channel_id=1, source_target_pairs={{0,1},{2,3},{4,5},{6,7},{8,9},{10,11},{12,13},{14,15},{16,17},{18,... | collective-permute-start | bytes 2359304 | tf_op jit(solution)/shard_map/ppermute | solution.py:418
  6.1 0.7 copy-start.1
  11.5 3.5 %collective-permute-start = (bf16[256,512]{1,0:T(8,128)(2,1)S(1)}, bf16[256,512]{1,0:T(8,128)(2,1)S(1)}, u32[]{:S(2)}, u32[]{:S(2)}) collective-permute-start(bf16[256,512]{1,0:T(8,128)(2,1)S(1)} %get-tuple-element.44), channel_id=1, source_target_pairs={{3,5},{7,9},{11,13},{15,17},{19,21},{23,25},{27,29},{5,3},{9,7},{1... | collective-permute-start | bytes 786440 | tf_op jit(solution)/shard_map/ppermute | solution.py:404
  12.2 2.9 %collective-permute-start.1 = (bf16[256,512]{1,0:T(8,128)(2,1)S(1)}, bf16[256,512]{1,0:T(8,128)(2,1)S(1)}, u32[]{:S(2)}, u32[]{:S(2)}) collective-permute-start(bf16[256,512]{1,0:T(8,128)(2,1)S(1)} %get-tuple-element.45), channel_id=1, source_target_pairs={{1,3},{5,7},{9,11},{13,15},{17,19},{21,23},{25,27},{29,31},{3,1},{... | collective-permute-start | bytes 786440 | tf_op jit(solution)/shard_map/ppermute | solution.py:404
  22.8 38.8 %collective-permute-start.5 = (bf16[1664,512]{1,0:T(8,128)(2,1)S(1)}, bf16[1664,512]{1,0:T(8,128)(2,1)S(1)}, u32[]{:S(2)}, u32[]{:S(2)}) collective-permute-start(bf16[1664,512]{1,0:T(8,128)(2,1)S(1)} %shard_map.58.sent), channel_id=1, source_target_pairs={{0,1},{1,0},{2,3},{3,2},{4,5},{5,4},{6,7},{7,6},{8,9},{9,8},{10,11... | collective-permute-start | bytes 5111816 | tf_op jit(solution)/shard_map/ppermute | solution.py:423
  31.3 0.7 collective-permute-start.3
  32.1 0.9 collective-permute-start.4
  33.0 0.7 collective-permute-start.6
  63.3 2.0 %collective-permute-start.8 = (f32[8,32,512]{2,1,0:T(8,128)S(1)}, f32[8,32,512]{2,1,0:T(8,128)S(1)}, u32[]{:S(2)}, u32[]{:S(2)}) collective-permute-start(f32[8,32,512]{2,1,0:T(8,128)S(1)} %get-tuple-element.66), channel_id=1, source_target_pairs={{0,2},{2,0},{4,6},{6,4},{8,10},{10,8},{12,14},{14,12},{16,18},{18,... | collective-permute-start | bytes 1572872 | tf_op jit(solution)/shard_map/ppermute | solution.py:387
  65.3 5.6 %collective-permute-start.9 = (bf16[4,32,512]{2,1,0:T(8,128)(2,1)S(1)}, bf16[4,32,512]{2,1,0:T(8,128)(2,1)S(1)}, u32[]{:S(2)}, u32[]{:S(2)}) collective-permute-start(bf16[4,32,512]{2,1,0:T(8,128)(2,1)S(1)} %get-tuple-element.68), channel_id=1, source_target_pairs={{0,4},{2,6},{4,0},{6,2},{8,12},{10,14},{12,8},{14,10},{16,20},{18,... | collective-permute-start | bytes 393224 | tf_op jit(solution)/shard_map/ppermute | solution.py:387
  71.0 5.0 %collective-permute-start.10 = (f32[2,32,512]{2,1,0:T(8,128)S(1)}, f32[2,32,512]{2,1,0:T(8,128)S(1)}, u32[]{:S(2)}, u32[]{:S(2)}) collective-permute-start(f32[2,32,512]{2,1,0:T(8,128)S(1)} %get-tuple-element.70), channel_id=1, source_target_pairs={{0,8},{2,10},{4,12},{6,14},{8,0},{10,2},{12,4},{14,6},{16,24},{18,... | collective-permute-start | bytes 393224 | tf_op jit(solution)/shard_map/ppermute | solution.py:387
  76.0 5.2 %collective-permute-start.11 = (f32[1,32,512]{2,1,0:T(8,128)S(1)}, f32[1,32,512]{2,1,0:T(8,128)S(1)}, u32[]{:S(2)}, u32[]{:S(2)}) collective-permute-start(f32[1,32,512]{2,1,0:T(8,128)S(1)} %get-tuple-element.72), channel_id=1, source_target_pairs={{0,16},{2,18},{4,20},{6,22},{8,24},{10,26},{12,28},{14,30},{16,0},... | collective-permute-start | bytes 196616 | tf_op jit(solution)/shard_map/ppermute | solution.py:387
  78.7 3.9 %collective-permute-start.7 = (f32[1,32,512]{2,1,0:T(8,128)S(1)}, f32[1,32,512]{2,1,0:T(8,128)S(1)}, u32[]{:S(2)}, u32[]{:S(2)}) collective-permute-start(f32[1,32,512]{2,1,0:T(8,128)S(1)} %get-tuple-element.61), channel_id=1, source_target_pairs={{1,17},{3,19},{5,21},{7,23},{9,25},{11,27},{13,29},{15,31},{17,1},... | collective-permute-start | bytes 196616 | tf_op jit(solution)/shard_map/ppermute | solution.py:387
  81.3 6.2 %collective-permute-start.12 = (f32[1,32,512]{2,1,0:T(8,128)S(1)}, f32[1,32,512]{2,1,0:T(8,128)S(1)}, u32[]{:S(2)}, u32[]{:S(2)}) collective-permute-start(f32[1,32,512]{2,1,0:T(8,128)S(1)} %add.10), channel_id=1, source_target_pairs={{1,0},{3,2},{5,4},{7,6},{9,8},{11,10},{13,12},{15,14},{17,16},{19,... | collective-permute-start | bytes 196616 | tf_op jit(solution)/shard_map/ppermute | solution.py:447

commit v8 on v7

--- a/solution.py
+++ b/solution.py
@@ -415,7 +415,7 @@
 
     cut = nb * bsize
     early = cut - na * bsize
-    ahead = lax.ppermute(tmat[:early], "col", [(0, 1)])
+    ahead = lax.ppermute(tmat[:early], "col", [(0, 1), (1, 0)])
 
     own_a = own_products(lists, blocks, panel, shift, nb, na)
     sent = piece(lists, blocks, odd, even, own_a, tmat, shift, nb, na, early, n_col)
@@ -444,7 +444,7 @@
         sums = step(both, 1 << b, sums, jnp.bfloat16 if b == 1 else jnp.float32)
     own_keep, own_got = step(panel_column, bit, parts)
     x = sums[0] + sums[1]
-    other = x + lax.ppermute(x, "col", [(1, 0)])
+    other = x + lax.ppermute(x, "col", [(0, 1), (1, 0)])
     return jnp.where(col == owner, own_keep + own_got, other).reshape(share, width)
 
 

time: 88.4 us -> 85.8 us (0.971)
  starting transfers between devices: 18.7 us -> 16.6 us
    ppermute x2, waiting for transfers between devices: 10.5 us -> 9 us  [the longest x1 6.48 us: body(): ahead = lax.ppermute(tmat[:early], 'col', [(0, 1), (1, 0)])]
    ppermute x2, starting transfers between devices: 6.18 us -> 4.81 us  [the longest x1 3 us: body(): ahead = lax.ppermute(tmat[:early], 'col', [(0, 1), (1, 0)])]
where the time goes in v8:
time: 85.8 us; the launch traced here: 85.1 us
  waiting for transfers between devices  48.8 us (57%)
  starting transfers between devices  16.6 us (19%)
  Pallas kernels  16.3 us (19%)
  local copies, waits for them, and re-layouts  1.87 us (2%)
  between operations  0.87 us (1%)
    ppermute x1, waiting for transfers between devices, body(): got = lax.ppermute(sent, 'col', [(0, 1), (1, 0)])  28.2 us
    ppermute x8, waiting for transfers between devices, step(): return [keep, lax.ppermute(send, *route(bit))]  11.5 us
    ppermute x8, starting transfers between devices, step(): return [keep, lax.ppermute(send, *route(bit))]  8.71 us
    ppermute x1, waiting for transfers between devices, body(): ahead = lax.ppermute(tmat[:early], 'col', [(0, 1), (1, 0)])  6.48 us
    pallas_call x1, Pallas kernels, panel_work(): pl.pallas_call(functools.partial(panel_kernel, panel.shape[0] // bsize, n...  5.89 us
    pallas_call x1, Pallas kernels, gather_rows(): pl.pallas_call(gather_kernel, out_shape=[jax.ShapeDtypeStruct((picked //...  4.75 us
    ppermute x1, starting transfers between devices, body(): ahead = lax.ppermute(tmat[:early], 'col', [(0, 1), (1, 0)])  3 us
    ppermute x1, waiting for transfers between devices, body(): other = x + lax.ppermute(x, 'col', [(0, 1), (1, 0)])  2.52 us
  transfers between devices with their start and end apart: 13, of which 7 were waited for; matrix products, arithmetic and copies ran while one was open for 0% of the time, Pallas kernels for 17%

profile of v8, /device:TPU:0, one launch (start us, length us, event | category | flops | bytes accessed | tf_op | source)
XLA Modules:
  0.0 85.1 jit_solution(11899091277388613704)
XLA Ops:
  0.0 1.2 %slice.3 = bf16[768,512]{1,0:T(8,128)(2,1)S(1)} slice(bf16[4096,512]{1,0:T(8,128)(2,1)} %tmat.3), slice={[0:768], [0:512]} | slice | bytes 1572864 | tf_op jit(solution)/shard_map/slice | solution.py:418
  1.2 3.0 %collective-permute-start.2 = (bf16[768,512]{1,0:T(8,128)(2,1)S(1)}, bf16[768,512]{1,0:T(8,128)(2,1)S(1)}, u32[]{:S(2)}, u32[]{:S(2)}) collective-permute-start(bf16[768,512]{1,0:T(8,128)(2,1)S(1)} %slice.3), channel_id=1, source_target_pairs={{0,1},{1,0},{2,3},{3,2},{4,5},{5,4},{6,7},{7,6},{8,9},{9,8},{10,11... | collective-permute-start | bytes 2359304 | tf_op jit(solution)/shard_map/ppermute | solution.py:418
  4.2 0.7 copy-done.1
  4.9 4.7 %shard_map.56 = (bf16[256,512]{1,0:T(8,128)(2,1)S(1)}, bf16[256,512]{1,0:T(8,128)(2,1)S(1)}, bf16[4096,512]{1,0:T(8,128)(2,1)S(1)}, bf16[256,128,128]{2,1,0:T(8,128)(2,1)S(1)}) custom-call(s32[2,256]{1,0:T(2,128)S(1)} %copy-done.1, bf16[4096,512]{1,0:T(8,128)(2,1)} %tmat.3, bf16[256,128,128]{2,1,0:T(8,128)(2,1)} %blocks.1), custom_call_target="tpu_custom_call" | custom-call | flops 1 | bytes 1 | tf_op jit(solution)/shard_map/pallas_call | solution.py:168
  9.6 0.7 collective-permute-start
  10.3 0.7 collective-permute-start.1
  11.7 0.7 shard_map.55
  12.4 0.8 shard_map.57.own
  13.2 2.1 %shard_map.58.sent = bf16[1664,512]{1,0:T(8,128)(2,1)S(1)} custom-call(s32[1,128]{1,0:T(1,128)S(1)} %get-tuple-element.39.first, s32[1,128]{1,0:T(1,128)S(1)} %get-tuple-element.40.owner_row, s32[1,512]{1,0:T(1,128)S(1)} %get-tuple-element.41.entries, bf16[256,128,128]{2,1,0:T(8,128)(2,1)S(1)} %get-tuple-element.42.blocks, ...), custom_call_target="tpu_custom_call" | custom-call | flops 1 | bytes 1 | tf_op jit(solution)/shard_map/pallas_call | solution.py:229
  15.3 6.5 %collective-permute-done.2.ahead = bf16[768,512]{1,0:T(8,128)(2,1)S(1)} collective-permute-done((bf16[768,512]{1,0:T(8,128)(2,1)S(1)}, bf16[768,512]{1,0:T(8,128)(2,1)S(1)}, u32[]{:S(2)}, u32[]{:S(2)}) %collective-permute-start.2) | collective-permute-done | bytes 786464 | tf_op jit(solution)/shard_map/ppermute | solution.py:418
  21.7 1.7 %collective-permute-start.5 = (bf16[1664,512]{1,0:T(8,128)(2,1)S(1)}, bf16[1664,512]{1,0:T(8,128)(2,1)S(1)}, u32[]{:S(2)}, u32[]{:S(2)}) collective-permute-start(bf16[1664,512]{1,0:T(8,128)(2,1)S(1)} %shard_map.58.sent), channel_id=1, source_target_pairs={{0,1},{1,0},{2,3},{3,2},{4,5},{5,4},{6,7},{7,6},{8,9},{9,8},{10,11... | collective-permute-start | bytes 5111816 | tf_op jit(solution)/shard_map/ppermute | solution.py:423
  23.5 5.9 %shard_map.59 = (bf16[2432,512]{1,0:T(8,128)(2,1)S(1)}, f32[512,512]{1,0:T(8,128)S(1)}) custom-call(s32[1,128]{1,0:T(1,128)S(1)} %get-tuple-element.39.first, s32[1,128]{1,0:T(1,128)S(1)} %get-tuple-element.40.owner_row, s32[1,512]{1,0:T(1,128)S(1)} %get-tuple-element.41.entries, bf16[256,128,128]{2,1,0:T(8,128)(2,1)S(1)} %get-tuple-element.42.blocks, ...), custom_call_target="tpu_custom_call" | custom-call | flops 1 | bytes 1 | tf_op jit(solution)/shard_map/pallas_call | solution.py:275
  29.4 0.1 shard_map.60
  29.5 0.7 collective-permute-start.3
  30.2 0.1 shard_map.61
  30.3 0.7 collective-permute-start.4
  31.0 0.2 shard_map.62
  31.2 0.7 collective-permute-start.6
  31.9 28.2 %collective-permute-done.5.got = bf16[1664,512]{1,0:T(8,128)(2,1)S(1)} collective-permute-done((bf16[1664,512]{1,0:T(8,128)(2,1)S(1)}, bf16[1664,512]{1,0:T(8,128)(2,1)S(1)}, u32[]{:S(2)}, u32[]{:S(2)}) %collective-permute-start.5) | collective-permute-done | bytes 1703968 | tf_op jit(solution)/shard_map/ppermute | solution.py:423
  60.1 1.6 %shard_map.65 = f32[512,512]{1,0:T(8,128)S(1)} custom-call(bf16[1664,512]{1,0:T(8,128)(2,1)S(1)} %collective-permute-done.5.got, bf16[1664,512]{1,0:T(8,128)(2,1)S(1)} %get-tuple-element.63.partner, f32[512,512]{1,0:T(8,128)S(1)} %get-tuple-element.64.known), custom_call_target="tpu_custom_call" | custom-call | flops 1 | bytes 1 | tf_op jit(solution)/shard_map/pallas_call | solution.py:335
  61.7 0.1 shard_map.66
  61.9 1.9 %collective-permute-done.8.refs_1_ = f32[8,32,512]{2,1,0:T(8,128)S(1)} collective-permute-done((f32[8,32,512]{2,1,0:T(8,128)S(1)}, f32[8,32,512]{2,1,0:T(8,128)S(1)}, u32[]{:S(2)}, u32[]{:S(2)}) %collective-permute-start.8) | collective-permute-done | bytes 524320 | tf_op jit(solution)/shard_map/ppermute | solution.py:387
  63.8 1.5 %collective-permute-start.9 = (bf16[4,32,512]{2,1,0:T(8,128)(2,1)S(1)}, bf16[4,32,512]{2,1,0:T(8,128)(2,1)S(1)}, u32[]{:S(2)}, u32[]{:S(2)}) collective-permute-start(bf16[4,32,512]{2,1,0:T(8,128)(2,1)S(1)} %get-tuple-element.68), channel_id=1, source_target_pairs={{0,4},{2,6},{4,0},{6,2},{8,12},{10,14},{12,8},{14,10},{16,20},{18,... | collective-permute-start | bytes 393224 | tf_op jit(solution)/shard_map/ppermute | solution.py:387
  65.3 4.1 %collective-permute-done.9.refs_1_ = bf16[4,32,512]{2,1,0:T(8,128)(2,1)S(1)} collective-permute-done((bf16[4,32,512]{2,1,0:T(8,128)(2,1)S(1)}, bf16[4,32,512]{2,1,0:T(8,128)(2,1)S(1)}, u32[]{:S(2)}, u32[]{:S(2)}) %collective-permute-start.9) | collective-permute-done | bytes 131104 | tf_op jit(solution)/shard_map/ppermute | solution.py:387
  69.5 2.1 %collective-permute-start.10 = (f32[2,32,512]{2,1,0:T(8,128)S(1)}, f32[2,32,512]{2,1,0:T(8,128)S(1)}, u32[]{:S(2)}, u32[]{:S(2)}) collective-permute-start(f32[2,32,512]{2,1,0:T(8,128)S(1)} %get-tuple-element.70), channel_id=1, source_target_pairs={{0,8},{2,10},{4,12},{6,14},{8,0},{10,2},{12,4},{14,6},{16,24},{18,... | collective-permute-start | bytes 393224 | tf_op jit(solution)/shard_map/ppermute | solution.py:387
  71.6 3.3 %collective-permute-done.10.refs_1_ = f32[2,32,512]{2,1,0:T(8,128)S(1)} collective-permute-done((f32[2,32,512]{2,1,0:T(8,128)S(1)}, f32[2,32,512]{2,1,0:T(8,128)S(1)}, u32[]{:S(2)}, u32[]{:S(2)}) %collective-permute-start.10) | collective-permute-done | bytes 131104 | tf_op jit(solution)/shard_map/ppermute | solution.py:387
  74.9 2.3 %collective-permute-start.11 = (f32[1,32,512]{2,1,0:T(8,128)S(1)}, f32[1,32,512]{2,1,0:T(8,128)S(1)}, u32[]{:S(2)}, u32[]{:S(2)}) collective-permute-start(f32[1,32,512]{2,1,0:T(8,128)S(1)} %get-tuple-element.72), channel_id=1, source_target_pairs={{0,16},{2,18},{4,20},{6,22},{8,24},{10,26},{12,28},{14,30},{16,0},... | collective-permute-start | bytes 196616 | tf_op jit(solution)/shard_map/ppermute | solution.py:387
  77.2 0.7 collective-permute-start.7
  77.9 2.3 %collective-permute-done.11 = f32[1,32,512]{2,1,0:T(8,128)S(1)} collective-permute-done((f32[1,32,512]{2,1,0:T(8,128)S(1)}, f32[1,32,512]{2,1,0:T(8,128)S(1)}, u32[]{:S(2)}, u32[]{:S(2)}) %collective-permute-start.11) | collective-permute-done | bytes 65568 | tf_op jit(solution)/shard_map/ppermute | solution.py:387
  80.1 1.8 %collective-permute-start.12 = (f32[1,32,512]{2,1,0:T(8,128)S(1)}, f32[1,32,512]{2,1,0:T(8,128)S(1)}, u32[]{:S(2)}, u32[]{:S(2)}) collective-permute-start(f32[1,32,512]{2,1,0:T(8,128)S(1)} %add.10), channel_id=1, source_target_pairs={{0,1},{1,0},{2,3},{3,2},{4,5},{5,4},{6,7},{7,6},{8,9},{9,8},{10,11... | collective-permute-start | bytes 196616 | tf_op jit(solution)/shard_map/ppermute | solution.py:447
  81.9 2.5 %collective-permute-done.12 = f32[1,32,512]{2,1,0:T(8,128)S(1)} collective-permute-done((f32[1,32,512]{2,1,0:T(8,128)S(1)}, f32[1,32,512]{2,1,0:T(8,128)S(1)}, u32[]{:S(2)}, u32[]{:S(2)}) %collective-permute-start.12) | collective-permute-done | bytes 65568 | tf_op jit(solution)/shard_map/ppermute | solution.py:447
  84.5 0.6 select_bitcast_fusion
  (16 shorter events, 0.3 us)
Async XLA Ops:
  1.2 10.5 %copy-start = (s32[256,2]{0,1:T(2,128)S(1)}, s32[256,2]{0,1:T(2,128)}, u32[]{:S(2)}) copy-start(s32[256,2]{0,1:T(2,128)} %param.7) | copy-start | bytes 6148
  1.2 20.5 %collective-permute-start.2 = (bf16[768,512]{1,0:T(8,128)(2,1)S(1)}, bf16[768,512]{1,0:T(8,128)(2,1)S(1)}, u32[]{:S(2)}, u32[]{:S(2)}) collective-permute-start(bf16[768,512]{1,0:T(8,128)(2,1)S(1)} %slice.3), channel_id=1, source_target_pairs={{0,1},{1,0},{2,3},{3,2},{4,5},{5,4},{6,7},{7,6},{8,9},{9,8},{10,11... | collective-permute-start | bytes 2359304 | tf_op jit(solution)/shard_map/ppermute | solution.py:418
  4.2 0.7 copy-start.1
  9.6 3.5 %collective-permute-start = (bf16[256,512]{1,0:T(8,128)(2,1)S(1)}, bf16[256,512]{1,0:T(8,128)(2,1)S(1)}, u32[]{:S(2)}, u32[]{:S(2)}) collective-permute-start(bf16[256,512]{1,0:T(8,128)(2,1)S(1)} %get-tuple-element.44), channel_id=1, source_target_pairs={{3,5},{7,9},{11,13},{15,17},{19,21},{23,25},{27,29},{5,3},{9,7},{1... | collective-permute-start | bytes 786440 | tf_op jit(solution)/shard_map/ppermute | solution.py:404
  10.3 2.9 %collective-permute-start.1 = (bf16[256,512]{1,0:T(8,128)(2,1)S(1)}, bf16[256,512]{1,0:T(8,128)(2,1)S(1)}, u32[]{:S(2)}, u32[]{:S(2)}) collective-permute-start(bf16[256,512]{1,0:T(8,128)(2,1)S(1)} %get-tuple-element.45), channel_id=1, source_target_pairs={{1,3},{5,7},{9,11},{13,15},{17,19},{21,23},{25,27},{29,31},{3,1},{... | collective-permute-start | bytes 786440 | tf_op jit(solution)/shard_map/ppermute | solution.py:404
  21.7 38.4 %collective-permute-start.5 = (bf16[1664,512]{1,0:T(8,128)(2,1)S(1)}, bf16[1664,512]{1,0:T(8,128)(2,1)S(1)}, u32[]{:S(2)}, u32[]{:S(2)}) collective-permute-start(bf16[1664,512]{1,0:T(8,128)(2,1)S(1)} %shard_map.58.sent), channel_id=1, source_target_pairs={{0,1},{1,0},{2,3},{3,2},{4,5},{5,4},{6,7},{7,6},{8,9},{9,8},{10,11... | collective-permute-start | bytes 5111816 | tf_op jit(solution)/shard_map/ppermute | solution.py:423
  29.5 0.7 collective-permute-start.3
  30.3 0.9 %collective-permute-start.4 = (f32[4,32,512]{2,1,0:T(8,128)S(1)}, f32[4,32,512]{2,1,0:T(8,128)S(1)}, u32[]{:S(2)}, u32[]{:S(2)}) collective-permute-start(f32[4,32,512]{2,1,0:T(8,128)S(1)} %get-tuple-element.51), channel_id=1, source_target_pairs={{1,5},{3,7},{5,1},{7,3},{9,13},{11,15},{13,9},{15,11},{17,21},{19,... | collective-permute-start | bytes 786440 | tf_op jit(solution)/shard_map/ppermute | solution.py:387
  31.2 0.7 collective-permute-start.6
  61.8 2.0 %collective-permute-start.8 = (f32[8,32,512]{2,1,0:T(8,128)S(1)}, f32[8,32,512]{2,1,0:T(8,128)S(1)}, u32[]{:S(2)}, u32[]{:S(2)}) collective-permute-start(f32[8,32,512]{2,1,0:T(8,128)S(1)} %get-tuple-element.66), channel_id=1, source_target_pairs={{0,2},{2,0},{4,6},{6,4},{8,10},{10,8},{12,14},{14,12},{16,18},{18,... | collective-permute-start | bytes 1572872 | tf_op jit(solution)/shard_map/ppermute | solution.py:387
  63.8 5.6 %collective-permute-start.9 = (bf16[4,32,512]{2,1,0:T(8,128)(2,1)S(1)}, bf16[4,32,512]{2,1,0:T(8,128)(2,1)S(1)}, u32[]{:S(2)}, u32[]{:S(2)}) collective-permute-start(bf16[4,32,512]{2,1,0:T(8,128)(2,1)S(1)} %get-tuple-element.68), channel_id=1, source_target_pairs={{0,4},{2,6},{4,0},{6,2},{8,12},{10,14},{12,8},{14,10},{16,20},{18,... | collective-permute-start | bytes 393224 | tf_op jit(solution)/shard_map/ppermute | solution.py:387
  69.5 5.4 %collective-permute-start.10 = (f32[2,32,512]{2,1,0:T(8,128)S(1)}, f32[2,32,512]{2,1,0:T(8,128)S(1)}, u32[]{:S(2)}, u32[]{:S(2)}) collective-permute-start(f32[2,32,512]{2,1,0:T(8,128)S(1)} %get-tuple-element.70), channel_id=1, source_target_pairs={{0,8},{2,10},{4,12},{6,14},{8,0},{10,2},{12,4},{14,6},{16,24},{18,... | collective-permute-start | bytes 393224 | tf_op jit(solution)/shard_map/ppermute | solution.py:387
  74.9 5.2 %collective-permute-start.11 = (f32[1,32,512]{2,1,0:T(8,128)S(1)}, f32[1,32,512]{2,1,0:T(8,128)S(1)}, u32[]{:S(2)}, u32[]{:S(2)}) collective-permute-start(f32[1,32,512]{2,1,0:T(8,128)S(1)} %get-tuple-element.72), channel_id=1, source_target_pairs={{0,16},{2,18},{4,20},{6,22},{8,24},{10,26},{12,28},{14,30},{16,0},... | collective-permute-start | bytes 196616 | tf_op jit(solution)/shard_map/ppermute | solution.py:387
  77.2 4.8 %collective-permute-start.7 = (f32[1,32,512]{2,1,0:T(8,128)S(1)}, f32[1,32,512]{2,1,0:T(8,128)S(1)}, u32[]{:S(2)}, u32[]{:S(2)}) collective-permute-start(f32[1,32,512]{2,1,0:T(8,128)S(1)} %get-tuple-element.61), channel_id=1, source_target_pairs={{1,17},{3,19},{5,21},{7,23},{9,25},{11,27},{13,29},{15,31},{17,1},... | collective-permute-start | bytes 196616 | tf_op jit(solution)/shard_map/ppermute | solution.py:387
  80.1 4.3 %collective-permute-start.12 = (f32[1,32,512]{2,1,0:T(8,128)S(1)}, f32[1,32,512]{2,1,0:T(8,128)S(1)}, u32[]{:S(2)}, u32[]{:S(2)}) collective-permute-start(f32[1,32,512]{2,1,0:T(8,128)S(1)} %add.10), channel_id=1, source_target_pairs={{0,1},{1,0},{2,3},{3,2},{4,5},{5,4},{6,7},{7,6},{8,9},{9,8},{10,11... | collective-permute-start | bytes 196616 | tf_op jit(solution)/shard_map/ppermute | solution.py:447

commit v9 on v8

--- a/solution.py
+++ b/solution.py
@@ -251,7 +251,7 @@
     out[...] = acc[...].astype(out.dtype)
 
 
-def add_contract(total, left, right, left0=0, right0=0, rows=None, steps=4):
+def add_contract(total, left, right, left0=0, right0=0, rows=None, steps=2):
     depth = (left.shape[0] if rows is None else rows) // steps
 
     @pl.loop(0, steps)
@@ -324,11 +324,11 @@
 
     @pl.when(panel_column)
     def _():
-        add_contract(out, partner, got, steps=2)
+        add_contract(out, partner, got, steps=1)
 
     @pl.when(jnp.logical_not(panel_column))
     def _():
-        add_contract(out, got, partner, steps=2)
+        add_contract(out, got, partner, steps=1)
 
 
 def meet(got, partner, known, n_col):

time: 85.8 us -> 84.7 us (0.987)
  Pallas kernels: 16.3 us -> 14.9 us
  waiting for transfers between devices: 48.8 us -> 49.9 us
    pallas_call x1, Pallas kernels: 5.89 us -> 4.8 us  [panel_work(): pl.pallas_call(functools.partial(panel_kernel, panel.shape[0] // bsize, n...]
    ppermute x1, waiting for transfers between devices: 28.2 us -> 29.3 us  [body(): got = lax.ppermute(sent, 'col', [(0, 1), (1, 0)])]
  transfers between devices with their start and end apart: 13 -> 13, of which waited for: 7 -> 7; matrix products, arithmetic and copies ran while one was open for 0% -> 0% of each run, Pallas kernels for 17% -> 16%
where the time goes in v9:
time: 84.7 us; the launch traced here: 84.4 us
  waiting for transfers between devices  49.9 us (59%)
  starting transfers between devices  16.2 us (19%)
  Pallas kernels  14.9 us (18%)
  local copies, waits for them, and re-layouts  1.87 us (2%)
  between operations  0.87 us (1%)
    ppermute x1, waiting for transfers between devices, body(): got = lax.ppermute(sent, 'col', [(0, 1), (1, 0)])  29.3 us
    ppermute x8, waiting for transfers between devices, step(): return [keep, lax.ppermute(send, *route(bit))]  11.2 us
    ppermute x8, starting transfers between devices, step(): return [keep, lax.ppermute(send, *route(bit))]  8.62 us
    ppermute x1, waiting for transfers between devices, body(): ahead = lax.ppermute(tmat[:early], 'col', [(0, 1), (1, 0)])  6.48 us
    pallas_call x1, Pallas kernels, panel_work(): pl.pallas_call(functools.partial(panel_kernel, panel.shape[0] // bsize, n...  4.8 us
    pallas_call x1, Pallas kernels, gather_rows(): pl.pallas_call(gather_kernel, out_shape=[jax.ShapeDtypeStruct((picked //...  4.75 us
    ppermute x1, starting transfers between devices, body(): ahead = lax.ppermute(tmat[:early], 'col', [(0, 1), (1, 0)])  3 us
    ppermute x1, waiting for transfers between devices, body(): other = x + lax.ppermute(x, 'col', [(0, 1), (1, 0)])  2.83 us
  transfers between devices with their start and end apart: 13, of which 7 were waited for; matrix products, arithmetic and copies ran while one was open for 0% of the time, Pallas kernels for 16%

profile of v9, /device:TPU:0, one launch (start us, length us, event | category | flops | bytes accessed | tf_op | source)
XLA Modules:
  0.0 84.4 jit_solution(2630854866965720073)
XLA Ops:
  0.0 1.2 %slice.3 = bf16[768,512]{1,0:T(8,128)(2,1)S(1)} slice(bf16[4096,512]{1,0:T(8,128)(2,1)} %tmat.3), slice={[0:768], [0:512]} | slice | bytes 1572864 | tf_op jit(solution)/shard_map/slice | solution.py:418
  1.2 3.0 %collective-permute-start.2 = (bf16[768,512]{1,0:T(8,128)(2,1)S(1)}, bf16[768,512]{1,0:T(8,128)(2,1)S(1)}, u32[]{:S(2)}, u32[]{:S(2)}) collective-permute-start(bf16[768,512]{1,0:T(8,128)(2,1)S(1)} %slice.3), channel_id=1, source_target_pairs={{0,1},{1,0},{2,3},{3,2},{4,5},{5,4},{6,7},{7,6},{8,9},{9,8},{10,11... | collective-permute-start | bytes 2359304 | tf_op jit(solution)/shard_map/ppermute | solution.py:418
  4.2 0.7 copy-done.1
  4.9 4.7 %shard_map.56 = (bf16[256,512]{1,0:T(8,128)(2,1)S(1)}, bf16[256,512]{1,0:T(8,128)(2,1)S(1)}, bf16[4096,512]{1,0:T(8,128)(2,1)S(1)}, bf16[256,128,128]{2,1,0:T(8,128)(2,1)S(1)}) custom-call(s32[2,256]{1,0:T(2,128)S(1)} %copy-done.1, bf16[4096,512]{1,0:T(8,128)(2,1)} %tmat.3, bf16[256,128,128]{2,1,0:T(8,128)(2,1)} %blocks.1), custom_call_target="tpu_custom_call" | custom-call | flops 1 | bytes 1 | tf_op jit(solution)/shard_map/pallas_call | solution.py:168
  9.6 0.7 collective-permute-start
  10.3 0.7 collective-permute-start.1
  11.7 0.7 shard_map.55
  12.4 0.8 shard_map.57.own
  13.2 2.1 %shard_map.58.sent = bf16[1664,512]{1,0:T(8,128)(2,1)S(1)} custom-call(s32[1,128]{1,0:T(1,128)S(1)} %get-tuple-element.39.first, s32[1,128]{1,0:T(1,128)S(1)} %get-tuple-element.40.owner_row, s32[1,512]{1,0:T(1,128)S(1)} %get-tuple-element.41.entries, bf16[256,128,128]{2,1,0:T(8,128)(2,1)S(1)} %get-tuple-element.42.blocks, ...), custom_call_target="tpu_custom_call" | custom-call | flops 1 | bytes 1 | tf_op jit(solution)/shard_map/pallas_call | solution.py:229
  15.3 6.5 %collective-permute-done.2.ahead = bf16[768,512]{1,0:T(8,128)(2,1)S(1)} collective-permute-done((bf16[768,512]{1,0:T(8,128)(2,1)S(1)}, bf16[768,512]{1,0:T(8,128)(2,1)S(1)}, u32[]{:S(2)}, u32[]{:S(2)}) %collective-permute-start.2) | collective-permute-done | bytes 786464 | tf_op jit(solution)/shard_map/ppermute | solution.py:418
  21.7 1.7 %collective-permute-start.5 = (bf16[1664,512]{1,0:T(8,128)(2,1)S(1)}, bf16[1664,512]{1,0:T(8,128)(2,1)S(1)}, u32[]{:S(2)}, u32[]{:S(2)}) collective-permute-start(bf16[1664,512]{1,0:T(8,128)(2,1)S(1)} %shard_map.58.sent), channel_id=1, source_target_pairs={{0,1},{1,0},{2,3},{3,2},{4,5},{5,4},{6,7},{7,6},{8,9},{9,8},{10,11... | collective-permute-start | bytes 5111816 | tf_op jit(solution)/shard_map/ppermute | solution.py:423
  23.5 4.8 %shard_map.59 = (bf16[2432,512]{1,0:T(8,128)(2,1)S(1)}, f32[512,512]{1,0:T(8,128)S(1)}) custom-call(s32[1,128]{1,0:T(1,128)S(1)} %get-tuple-element.39.first, s32[1,128]{1,0:T(1,128)S(1)} %get-tuple-element.40.owner_row, s32[1,512]{1,0:T(1,128)S(1)} %get-tuple-element.41.entries, bf16[256,128,128]{2,1,0:T(8,128)(2,1)S(1)} %get-tuple-element.42.blocks, ...), custom_call_target="tpu_custom_call" | custom-call | flops 1 | bytes 1 | tf_op jit(solution)/shard_map/pallas_call | solution.py:275
  28.3 0.1 shard_map.60
  28.4 0.7 collective-permute-start.3
  29.1 0.1 shard_map.61
  29.2 0.7 collective-permute-start.4
  29.9 0.2 shard_map.62
  30.1 0.7 collective-permute-start.6
  30.8 29.3 %collective-permute-done.5.got = bf16[1664,512]{1,0:T(8,128)(2,1)S(1)} collective-permute-done((bf16[1664,512]{1,0:T(8,128)(2,1)S(1)}, bf16[1664,512]{1,0:T(8,128)(2,1)S(1)}, u32[]{:S(2)}, u32[]{:S(2)}) %collective-permute-start.5) | collective-permute-done | bytes 1703968 | tf_op jit(solution)/shard_map/ppermute | solution.py:423
  60.1 1.2 %shard_map.65 = f32[512,512]{1,0:T(8,128)S(1)} custom-call(bf16[1664,512]{1,0:T(8,128)(2,1)S(1)} %collective-permute-done.5.got, bf16[1664,512]{1,0:T(8,128)(2,1)S(1)} %get-tuple-element.63.partner, f32[512,512]{1,0:T(8,128)S(1)} %get-tuple-element.64.known), custom_call_target="tpu_custom_call" | custom-call | flops 1 | bytes 1 | tf_op jit(solution)/shard_map/pallas_call | solution.py:335
  61.4 0.1 shard_map.66
  61.5 1.9 %collective-permute-done.8.refs_1_ = f32[8,32,512]{2,1,0:T(8,128)S(1)} collective-permute-done((f32[8,32,512]{2,1,0:T(8,128)S(1)}, f32[8,32,512]{2,1,0:T(8,128)S(1)}, u32[]{:S(2)}, u32[]{:S(2)}) %collective-permute-start.8) | collective-permute-done | bytes 524320 | tf_op jit(solution)/shard_map/ppermute | solution.py:387
  63.5 1.5 %collective-permute-start.9 = (bf16[4,32,512]{2,1,0:T(8,128)(2,1)S(1)}, bf16[4,32,512]{2,1,0:T(8,128)(2,1)S(1)}, u32[]{:S(2)}, u32[]{:S(2)}) collective-permute-start(bf16[4,32,512]{2,1,0:T(8,128)(2,1)S(1)} %get-tuple-element.68), channel_id=1, source_target_pairs={{0,4},{2,6},{4,0},{6,2},{8,12},{10,14},{12,8},{14,10},{16,20},{18,... | collective-permute-start | bytes 393224 | tf_op jit(solution)/shard_map/ppermute | solution.py:387
  65.0 4.1 %collective-permute-done.9.refs_1_ = bf16[4,32,512]{2,1,0:T(8,128)(2,1)S(1)} collective-permute-done((bf16[4,32,512]{2,1,0:T(8,128)(2,1)S(1)}, bf16[4,32,512]{2,1,0:T(8,128)(2,1)S(1)}, u32[]{:S(2)}, u32[]{:S(2)}) %collective-permute-start.9) | collective-permute-done | bytes 131104 | tf_op jit(solution)/shard_map/ppermute | solution.py:387
  69.1 1.7 %collective-permute-start.10 = (f32[2,32,512]{2,1,0:T(8,128)S(1)}, f32[2,32,512]{2,1,0:T(8,128)S(1)}, u32[]{:S(2)}, u32[]{:S(2)}) collective-permute-start(f32[2,32,512]{2,1,0:T(8,128)S(1)} %get-tuple-element.70), channel_id=1, source_target_pairs={{0,8},{2,10},{4,12},{6,14},{8,0},{10,2},{12,4},{14,6},{16,24},{18,... | collective-permute-start | bytes 393224 | tf_op jit(solution)/shard_map/ppermute | solution.py:387
  70.8 3.4 %collective-permute-done.10.refs_1_ = f32[2,32,512]{2,1,0:T(8,128)S(1)} collective-permute-done((f32[2,32,512]{2,1,0:T(8,128)S(1)}, f32[2,32,512]{2,1,0:T(8,128)S(1)}, u32[]{:S(2)}, u32[]{:S(2)}) %collective-permute-start.10) | collective-permute-done | bytes 131104 | tf_op jit(solution)/shard_map/ppermute | solution.py:387
  74.2 2.7 %collective-permute-start.11 = (f32[1,32,512]{2,1,0:T(8,128)S(1)}, f32[1,32,512]{2,1,0:T(8,128)S(1)}, u32[]{:S(2)}, u32[]{:S(2)}) collective-permute-start(f32[1,32,512]{2,1,0:T(8,128)S(1)} %get-tuple-element.72), channel_id=1, source_target_pairs={{0,16},{2,18},{4,20},{6,22},{8,24},{10,26},{12,28},{14,30},{16,0},... | collective-permute-start | bytes 196616 | tf_op jit(solution)/shard_map/ppermute | solution.py:387
  76.9 0.7 collective-permute-start.7
  77.5 1.9 %collective-permute-done.11 = f32[1,32,512]{2,1,0:T(8,128)S(1)} collective-permute-done((f32[1,32,512]{2,1,0:T(8,128)S(1)}, f32[1,32,512]{2,1,0:T(8,128)S(1)}, u32[]{:S(2)}, u32[]{:S(2)}) %collective-permute-start.11) | collective-permute-done | bytes 65568 | tf_op jit(solution)/shard_map/ppermute | solution.py:387
  79.4 1.5 %collective-permute-start.12 = (f32[1,32,512]{2,1,0:T(8,128)S(1)}, f32[1,32,512]{2,1,0:T(8,128)S(1)}, u32[]{:S(2)}, u32[]{:S(2)}) collective-permute-start(f32[1,32,512]{2,1,0:T(8,128)S(1)} %add.10), channel_id=1, source_target_pairs={{0,1},{1,0},{2,3},{3,2},{4,5},{5,4},{6,7},{7,6},{8,9},{9,8},{10,11... | collective-permute-start | bytes 196616 | tf_op jit(solution)/shard_map/ppermute | solution.py:447
  80.9 2.8 %collective-permute-done.12 = f32[1,32,512]{2,1,0:T(8,128)S(1)} collective-permute-done((f32[1,32,512]{2,1,0:T(8,128)S(1)}, f32[1,32,512]{2,1,0:T(8,128)S(1)}, u32[]{:S(2)}, u32[]{:S(2)}) %collective-permute-start.12) | collective-permute-done | bytes 65568 | tf_op jit(solution)/shard_map/ppermute | solution.py:447
  83.7 0.6 select_bitcast_fusion
  (16 shorter events, 0.3 us)
Async XLA Ops:
  1.2 10.5 %copy-start = (s32[256,2]{0,1:T(2,128)S(1)}, s32[256,2]{0,1:T(2,128)}, u32[]{:S(2)}) copy-start(s32[256,2]{0,1:T(2,128)} %param.7) | copy-start | bytes 6148
  1.2 20.5 %collective-permute-start.2 = (bf16[768,512]{1,0:T(8,128)(2,1)S(1)}, bf16[768,512]{1,0:T(8,128)(2,1)S(1)}, u32[]{:S(2)}, u32[]{:S(2)}) collective-permute-start(bf16[768,512]{1,0:T(8,128)(2,1)S(1)} %slice.3), channel_id=1, source_target_pairs={{0,1},{1,0},{2,3},{3,2},{4,5},{5,4},{6,7},{7,6},{8,9},{9,8},{10,11... | collective-permute-start | bytes 2359304 | tf_op jit(solution)/shard_map/ppermute | solution.py:418
  4.2 0.7 copy-start.1
  9.6 3.5 %collective-permute-start = (bf16[256,512]{1,0:T(8,128)(2,1)S(1)}, bf16[256,512]{1,0:T(8,128)(2,1)S(1)}, u32[]{:S(2)}, u32[]{:S(2)}) collective-permute-start(bf16[256,512]{1,0:T(8,128)(2,1)S(1)} %get-tuple-element.44), channel_id=1, source_target_pairs={{3,5},{7,9},{11,13},{15,17},{19,21},{23,25},{27,29},{5,3},{9,7},{1... | collective-permute-start | bytes 786440 | tf_op jit(solution)/shard_map/ppermute | solution.py:404
  10.3 2.9 %collective-permute-start.1 = (bf16[256,512]{1,0:T(8,128)(2,1)S(1)}, bf16[256,512]{1,0:T(8,128)(2,1)S(1)}, u32[]{:S(2)}, u32[]{:S(2)}) collective-permute-start(bf16[256,512]{1,0:T(8,128)(2,1)S(1)} %get-tuple-element.45), channel_id=1, source_target_pairs={{1,3},{5,7},{9,11},{13,15},{17,19},{21,23},{25,27},{29,31},{3,1},{... | collective-permute-start | bytes 786440 | tf_op jit(solution)/shard_map/ppermute | solution.py:404
  21.7 38.4 %collective-permute-start.5 = (bf16[1664,512]{1,0:T(8,128)(2,1)S(1)}, bf16[1664,512]{1,0:T(8,128)(2,1)S(1)}, u32[]{:S(2)}, u32[]{:S(2)}) collective-permute-start(bf16[1664,512]{1,0:T(8,128)(2,1)S(1)} %shard_map.58.sent), channel_id=1, source_target_pairs={{0,1},{1,0},{2,3},{3,2},{4,5},{5,4},{6,7},{7,6},{8,9},{9,8},{10,11... | collective-permute-start | bytes 5111816 | tf_op jit(solution)/shard_map/ppermute | solution.py:423
  28.4 0.7 collective-permute-start.3
  29.2 0.9 %collective-permute-start.4 = (f32[4,32,512]{2,1,0:T(8,128)S(1)}, f32[4,32,512]{2,1,0:T(8,128)S(1)}, u32[]{:S(2)}, u32[]{:S(2)}) collective-permute-start(f32[4,32,512]{2,1,0:T(8,128)S(1)} %get-tuple-element.51), channel_id=1, source_target_pairs={{1,5},{3,7},{5,1},{7,3},{9,13},{11,15},{13,9},{15,11},{17,21},{19,... | collective-permute-start | bytes 786440 | tf_op jit(solution)/shard_map/ppermute | solution.py:387
  30.1 0.7 collective-permute-start.6
  61.4 2.0 %collective-permute-start.8 = (f32[8,32,512]{2,1,0:T(8,128)S(1)}, f32[8,32,512]{2,1,0:T(8,128)S(1)}, u32[]{:S(2)}, u32[]{:S(2)}) collective-permute-start(f32[8,32,512]{2,1,0:T(8,128)S(1)} %get-tuple-element.66), channel_id=1, source_target_pairs={{0,2},{2,0},{4,6},{6,4},{8,10},{10,8},{12,14},{14,12},{16,18},{18,... | collective-permute-start | bytes 1572872 | tf_op jit(solution)/shard_map/ppermute | solution.py:387
  63.5 5.6 %collective-permute-start.9 = (bf16[4,32,512]{2,1,0:T(8,128)(2,1)S(1)}, bf16[4,32,512]{2,1,0:T(8,128)(2,1)S(1)}, u32[]{:S(2)}, u32[]{:S(2)}) collective-permute-start(bf16[4,32,512]{2,1,0:T(8,128)(2,1)S(1)} %get-tuple-element.68), channel_id=1, source_target_pairs={{0,4},{2,6},{4,0},{6,2},{8,12},{10,14},{12,8},{14,10},{16,20},{18,... | collective-permute-start | bytes 393224 | tf_op jit(solution)/shard_map/ppermute | solution.py:387
  69.1 5.0 %collective-permute-start.10 = (f32[2,32,512]{2,1,0:T(8,128)S(1)}, f32[2,32,512]{2,1,0:T(8,128)S(1)}, u32[]{:S(2)}, u32[]{:S(2)}) collective-permute-start(f32[2,32,512]{2,1,0:T(8,128)S(1)} %get-tuple-element.70), channel_id=1, source_target_pairs={{0,8},{2,10},{4,12},{6,14},{8,0},{10,2},{12,4},{14,6},{16,24},{18,... | collective-permute-start | bytes 393224 | tf_op jit(solution)/shard_map/ppermute | solution.py:387
  74.2 5.2 %collective-permute-start.11 = (f32[1,32,512]{2,1,0:T(8,128)S(1)}, f32[1,32,512]{2,1,0:T(8,128)S(1)}, u32[]{:S(2)}, u32[]{:S(2)}) collective-permute-start(f32[1,32,512]{2,1,0:T(8,128)S(1)} %get-tuple-element.72), channel_id=1, source_target_pairs={{0,16},{2,18},{4,20},{6,22},{8,24},{10,26},{12,28},{14,30},{16,0},... | collective-permute-start | bytes 196616 | tf_op jit(solution)/shard_map/ppermute | solution.py:387
  76.9 4.1 %collective-permute-start.7 = (f32[1,32,512]{2,1,0:T(8,128)S(1)}, f32[1,32,512]{2,1,0:T(8,128)S(1)}, u32[]{:S(2)}, u32[]{:S(2)}) collective-permute-start(f32[1,32,512]{2,1,0:T(8,128)S(1)} %get-tuple-element.61), channel_id=1, source_target_pairs={{1,17},{3,19},{5,21},{7,23},{9,25},{11,27},{13,29},{15,31},{17,1},... | collective-permute-start | bytes 196616 | tf_op jit(solution)/shard_map/ppermute | solution.py:387
  79.4 4.3 %collective-permute-start.12 = (f32[1,32,512]{2,1,0:T(8,128)S(1)}, f32[1,32,512]{2,1,0:T(8,128)S(1)}, u32[]{:S(2)}, u32[]{:S(2)}) collective-permute-start(f32[1,32,512]{2,1,0:T(8,128)S(1)} %add.10), channel_id=1, source_target_pairs={{0,1},{1,0},{2,3},{3,2},{4,5},{5,4},{6,7},{7,6},{8,9},{9,8},{10,11... | collective-permute-start | bytes 196616 | tf_op jit(solution)/shard_map/ppermute | solution.py:447

commit v10 on v9

--- a/solution.py
+++ b/solution.py
@@ -131,7 +131,7 @@
     return first[0, nrows_blk + row0], first[0, nrows_blk + row0 + nrows]
 
 
-def gather_kernel(send_rows, tmat, blocks, first_rows, second_rows, panel, near_blocks, picked, sem):
+def gather_kernel(send_rows, tmat, blocks, first, owner_row, entries, first_rows, second_rows, panel, near_blocks, picked, sem):
     count = picked.shape[0]
     depth = 2 * count
     steps = panel.shape[0] // depth
@@ -163,13 +163,13 @@
     copy_blocks.wait()
 
 
-def gather_rows(send_rows, tmat, blocks):
+def gather_rows(send_rows, tmat, blocks, after):
     width, picked = tmat.shape[1], send_rows.size
     return pl.pallas_call(
         gather_kernel,
         out_shape=[jax.ShapeDtypeStruct((picked // 2, width), tmat.dtype)] * 2
         + [jax.ShapeDtypeStruct(a.shape, a.dtype) for a in (tmat, blocks)],
-        in_specs=[NEAR] + [FAR] * 2,
+        in_specs=[NEAR] + [FAR] * 2 + [NEAR] * 3,
         out_specs=[NEAR] * 4,
         scratch_shapes=[
             pltpu.VMEM((picked, width), jnp.float32),
@@ -177,7 +177,7 @@
         ],
         compiler_params=room_for(nbytes(tmat), nbytes(blocks), 6 * picked * width),
         cost_estimate=near_nothing(),
-    )(send_rows, *far(tmat, blocks))
+    )(send_rows, *far(tmat, blocks), *after)
 
 
 def own_kernel(row0, nrows, shift, bsize, first, owner_row, entries, blocks, panel, acc):
@@ -405,7 +405,7 @@
 
     na = (nrows_blk * 13) // 32
     nb = nrows_blk - na
-    *rows, panel, blocks = gather_rows(send_rows, tmat, stored_mass_blocks)
+    *rows, panel, blocks = gather_rows(send_rows, tmat, stored_mass_blocks, lists)
     even, odd = exchange(rows[0], 0), exchange(rows[1], 1)
 
     if n_col != 2 or n_dom < 16 or n_dom & (n_dom - 1):

time: 84.7 us -> 86.2 us (1.018)
    ppermute x1, waiting for transfers between devices: 29.3 us -> 30.3 us  [body(): got = lax.ppermute(sent, 'col', [(0, 1), (1, 0)])]
where the time goes in v10:
time: 86.2 us; the launch traced here: 85.9 us
  waiting for transfers between devices  50.6 us (59%)
  starting transfers between devices  16.3 us (19%)
  Pallas kernels  14.9 us (17%)
  local copies, waits for them, and re-layouts  2.54 us (3%)
  between operations  0.87 us (1%)
    ppermute x1, waiting for transfers between devices, body(): got = lax.ppermute(sent, 'col', [(0, 1), (1, 0)])  30.3 us
    ppermute x8, waiting for transfers between devices, step(): return [keep, lax.ppermute(send, *route(bit))]  11.5 us
    ppermute x8, starting transfers between devices, step(): return [keep, lax.ppermute(send, *route(bit))]  8.77 us
    ppermute x1, waiting for transfers between devices, body(): ahead = lax.ppermute(tmat[:early], 'col', [(0, 1), (1, 0)])  5.8 us
    pallas_call x1, Pallas kernels, panel_work(): pl.pallas_call(functools.partial(panel_kernel, panel.shape[0] // bsize, n...  4.8 us
    pallas_call x1, Pallas kernels, gather_rows(): pl.pallas_call(gather_kernel, out_shape=[jax.ShapeDtypeStruct((picked //...  4.75 us
    ppermute x1, starting transfers between devices, body(): ahead = lax.ppermute(tmat[:early], 'col', [(0, 1), (1, 0)])  3 us
    ppermute x1, waiting for transfers between devices, body(): other = x + lax.ppermute(x, 'col', [(0, 1), (1, 0)])  2.93 us
  transfers between devices with their start and end apart: 13, of which 7 were waited for; matrix products, arithmetic and copies ran while one was open for 0% of the time, Pallas kernels for 16%

profile of v10, /device:TPU:0, one launch (start us, length us, event | category | flops | bytes accessed | tf_op | source)
XLA Modules:
  0.0 85.9 jit_solution(14655011967505389401)
XLA Ops:
  0.0 1.2 %slice.3 = bf16[768,512]{1,0:T(8,128)(2,1)S(1)} slice(bf16[4096,512]{1,0:T(8,128)(2,1)} %tmat.3), slice={[0:768], [0:512]} | slice | bytes 1572864 | tf_op jit(solution)/shard_map/slice | solution.py:418
  1.2 3.0 %collective-permute-start.2 = (bf16[768,512]{1,0:T(8,128)(2,1)S(1)}, bf16[768,512]{1,0:T(8,128)(2,1)S(1)}, u32[]{:S(2)}, u32[]{:S(2)}) collective-permute-start(bf16[768,512]{1,0:T(8,128)(2,1)S(1)} %slice.3), channel_id=1, source_target_pairs={{0,1},{1,0},{2,3},{3,2},{4,5},{5,4},{6,7},{7,6},{8,9},{9,8},{10,11... | collective-permute-start | bytes 2359304 | tf_op jit(solution)/shard_map/ppermute | solution.py:418
  4.9 0.7 copy-done.1
  5.5 0.7 shard_map.55
  6.2 0.7 copy-done
  6.9 4.7 %shard_map.56 = (bf16[256,512]{1,0:T(8,128)(2,1)S(1)}, bf16[256,512]{1,0:T(8,128)(2,1)S(1)}, bf16[4096,512]{1,0:T(8,128)(2,1)S(1)}, bf16[256,128,128]{2,1,0:T(8,128)(2,1)S(1)}) custom-call(s32[2,256]{1,0:T(2,128)S(1)} %copy-done, bf16[4096,512]{1,0:T(8,128)(2,1)} %tmat.3, bf16[256,128,128]{2,1,0:T(8,128)(2,1)} %blocks.1, ...), custom_call_target="tpu_custom_call" | custom-call | flops 1 | bytes 1 | tf_op jit(solution)/shard_map/pallas_call | solution.py:168
  11.7 0.7 collective-permute-start
  12.4 0.7 collective-permute-start.1
  13.0 0.8 shard_map.57.own
  13.9 2.1 %shard_map.58.sent = bf16[1664,512]{1,0:T(8,128)(2,1)S(1)} custom-call(s32[1,128]{1,0:T(1,128)S(1)} %get-tuple-element.39.first, s32[1,128]{1,0:T(1,128)S(1)} %get-tuple-element.40.owner_row, s32[1,512]{1,0:T(1,128)S(1)} %get-tuple-element.41.entries, bf16[256,128,128]{2,1,0:T(8,128)(2,1)S(1)} %get-tuple-element.42.blocks, ...), custom_call_target="tpu_custom_call" | custom-call | flops 1 | bytes 1 | tf_op jit(solution)/shard_map/pallas_call | solution.py:229
  15.9 5.8 %collective-permute-done.2.ahead = bf16[768,512]{1,0:T(8,128)(2,1)S(1)} collective-permute-done((bf16[768,512]{1,0:T(8,128)(2,1)S(1)}, bf16[768,512]{1,0:T(8,128)(2,1)S(1)}, u32[]{:S(2)}, u32[]{:S(2)}) %collective-permute-start.2) | collective-permute-done | bytes 786464 | tf_op jit(solution)/shard_map/ppermute | solution.py:418
  21.7 1.7 %collective-permute-start.5 = (bf16[1664,512]{1,0:T(8,128)(2,1)S(1)}, bf16[1664,512]{1,0:T(8,128)(2,1)S(1)}, u32[]{:S(2)}, u32[]{:S(2)}) collective-permute-start(bf16[1664,512]{1,0:T(8,128)(2,1)S(1)} %shard_map.58.sent), channel_id=1, source_target_pairs={{0,1},{1,0},{2,3},{3,2},{4,5},{5,4},{6,7},{7,6},{8,9},{9,8},{10,11... | collective-permute-start | bytes 5111816 | tf_op jit(solution)/shard_map/ppermute | solution.py:423
  23.5 4.8 %shard_map.59 = (bf16[2432,512]{1,0:T(8,128)(2,1)S(1)}, f32[512,512]{1,0:T(8,128)S(1)}) custom-call(s32[1,128]{1,0:T(1,128)S(1)} %get-tuple-element.39.first, s32[1,128]{1,0:T(1,128)S(1)} %get-tuple-element.40.owner_row, s32[1,512]{1,0:T(1,128)S(1)} %get-tuple-element.41.entries, bf16[256,128,128]{2,1,0:T(8,128)(2,1)S(1)} %get-tuple-element.42.blocks, ...), custom_call_target="tpu_custom_call" | custom-call | flops 1 | bytes 1 | tf_op jit(solution)/shard_map/pallas_call | solution.py:275
  28.3 0.1 shard_map.60
  28.4 0.7 collective-permute-start.3
  29.2 0.7 collective-permute-start.4
  29.9 0.2 shard_map.62
  30.1 0.7 collective-permute-start.6
  30.8 30.3 %collective-permute-done.5.got = bf16[1664,512]{1,0:T(8,128)(2,1)S(1)} collective-permute-done((bf16[1664,512]{1,0:T(8,128)(2,1)S(1)}, bf16[1664,512]{1,0:T(8,128)(2,1)S(1)}, u32[]{:S(2)}, u32[]{:S(2)}) %collective-permute-start.5) | collective-permute-done | bytes 1703968 | tf_op jit(solution)/shard_map/ppermute | solution.py:423
  61.1 1.2 %shard_map.65 = f32[512,512]{1,0:T(8,128)S(1)} custom-call(bf16[1664,512]{1,0:T(8,128)(2,1)S(1)} %collective-permute-done.5.got, bf16[1664,512]{1,0:T(8,128)(2,1)S(1)} %get-tuple-element.63.partner, f32[512,512]{1,0:T(8,128)S(1)} %get-tuple-element.64.known), custom_call_target="tpu_custom_call" | custom-call | flops 1 | bytes 1 | tf_op jit(solution)/shard_map/pallas_call | solution.py:335
  62.4 0.1 shard_map.66
  62.5 1.9 %collective-permute-done.8.refs_1_ = f32[8,32,512]{2,1,0:T(8,128)S(1)} collective-permute-done((f32[8,32,512]{2,1,0:T(8,128)S(1)}, f32[8,32,512]{2,1,0:T(8,128)S(1)}, u32[]{:S(2)}, u32[]{:S(2)}) %collective-permute-start.8) | collective-permute-done | bytes 524320 | tf_op jit(solution)/shard_map/ppermute | solution.py:387
  64.5 0.5 collective-permute-start.9
  65.0 5.1 %collective-permute-done.9.refs_1_ = bf16[4,32,512]{2,1,0:T(8,128)(2,1)S(1)} collective-permute-done((bf16[4,32,512]{2,1,0:T(8,128)(2,1)S(1)}, bf16[4,32,512]{2,1,0:T(8,128)(2,1)S(1)}, u32[]{:S(2)}, u32[]{:S(2)}) %collective-permute-start.9) | collective-permute-done | bytes 131104 | tf_op jit(solution)/shard_map/ppermute | solution.py:387
  70.1 2.4 %collective-permute-start.10 = (f32[2,32,512]{2,1,0:T(8,128)S(1)}, f32[2,32,512]{2,1,0:T(8,128)S(1)}, u32[]{:S(2)}, u32[]{:S(2)}) collective-permute-start(f32[2,32,512]{2,1,0:T(8,128)S(1)} %get-tuple-element.70), channel_id=1, source_target_pairs={{0,8},{2,10},{4,12},{6,14},{8,0},{10,2},{12,4},{14,6},{16,24},{18,... | collective-permute-start | bytes 393224 | tf_op jit(solution)/shard_map/ppermute | solution.py:387
  72.5 3.0 %collective-permute-done.10.refs_1_ = f32[2,32,512]{2,1,0:T(8,128)S(1)} collective-permute-done((f32[2,32,512]{2,1,0:T(8,128)S(1)}, f32[2,32,512]{2,1,0:T(8,128)S(1)}, u32[]{:S(2)}, u32[]{:S(2)}) %collective-permute-start.10) | collective-permute-done | bytes 131104 | tf_op jit(solution)/shard_map/ppermute | solution.py:387
  75.5 3.1 %collective-permute-start.11 = (f32[1,32,512]{2,1,0:T(8,128)S(1)}, f32[1,32,512]{2,1,0:T(8,128)S(1)}, u32[]{:S(2)}, u32[]{:S(2)}) collective-permute-start(f32[1,32,512]{2,1,0:T(8,128)S(1)} %get-tuple-element.72), channel_id=1, source_target_pairs={{0,16},{2,18},{4,20},{6,22},{8,24},{10,26},{12,28},{14,30},{16,0},... | collective-permute-start | bytes 196616 | tf_op jit(solution)/shard_map/ppermute | solution.py:387
  78.6 0.7 collective-permute-start.7
  79.3 1.6 %collective-permute-done.11 = f32[1,32,512]{2,1,0:T(8,128)S(1)} collective-permute-done((f32[1,32,512]{2,1,0:T(8,128)S(1)}, f32[1,32,512]{2,1,0:T(8,128)S(1)}, u32[]{:S(2)}, u32[]{:S(2)}) %collective-permute-start.11) | collective-permute-done | bytes 65568 | tf_op jit(solution)/shard_map/ppermute | solution.py:387
  80.9 1.4 %collective-permute-start.12 = (f32[1,32,512]{2,1,0:T(8,128)S(1)}, f32[1,32,512]{2,1,0:T(8,128)S(1)}, u32[]{:S(2)}, u32[]{:S(2)}) collective-permute-start(f32[1,32,512]{2,1,0:T(8,128)S(1)} %add.10), channel_id=1, source_target_pairs={{0,1},{1,0},{2,3},{3,2},{4,5},{5,4},{6,7},{7,6},{8,9},{9,8},{10,11... | collective-permute-start | bytes 196616 | tf_op jit(solution)/shard_map/ppermute | solution.py:447
  82.3 2.9 %collective-permute-done.12 = f32[1,32,512]{2,1,0:T(8,128)S(1)} collective-permute-done((f32[1,32,512]{2,1,0:T(8,128)S(1)}, f32[1,32,512]{2,1,0:T(8,128)S(1)}, u32[]{:S(2)}, u32[]{:S(2)}) %collective-permute-start.12) | collective-permute-done | bytes 65568 | tf_op jit(solution)/shard_map/ppermute | solution.py:447
  85.2 0.6 select_bitcast_fusion
  (16 shorter events, 0.3 us)
Async XLA Ops:
  1.2 20.5 %collective-permute-start.2 = (bf16[768,512]{1,0:T(8,128)(2,1)S(1)}, bf16[768,512]{1,0:T(8,128)(2,1)S(1)}, u32[]{:S(2)}, u32[]{:S(2)}) collective-permute-start(bf16[768,512]{1,0:T(8,128)(2,1)S(1)} %slice.3), channel_id=1, source_target_pairs={{0,1},{1,0},{2,3},{3,2},{4,5},{5,4},{6,7},{7,6},{8,9},{9,8},{10,11... | collective-permute-start | bytes 2359304 | tf_op jit(solution)/shard_map/ppermute | solution.py:418
  4.8 0.7 copy-start.1
  6.2 0.7 copy-start
  11.7 2.2 %collective-permute-start = (bf16[256,512]{1,0:T(8,128)(2,1)S(1)}, bf16[256,512]{1,0:T(8,128)(2,1)S(1)}, u32[]{:S(2)}, u32[]{:S(2)}) collective-permute-start(bf16[256,512]{1,0:T(8,128)(2,1)S(1)} %get-tuple-element.44), channel_id=1, source_target_pairs={{3,5},{7,9},{11,13},{15,17},{19,21},{23,25},{27,29},{5,3},{9,7},{1... | collective-permute-start | bytes 786440 | tf_op jit(solution)/shard_map/ppermute | solution.py:404
  12.4 1.5 %collective-permute-start.1 = (bf16[256,512]{1,0:T(8,128)(2,1)S(1)}, bf16[256,512]{1,0:T(8,128)(2,1)S(1)}, u32[]{:S(2)}, u32[]{:S(2)}) collective-permute-start(bf16[256,512]{1,0:T(8,128)(2,1)S(1)} %get-tuple-element.45), channel_id=1, source_target_pairs={{1,3},{5,7},{9,11},{13,15},{17,19},{21,23},{25,27},{29,31},{3,1},{... | collective-permute-start | bytes 786440 | tf_op jit(solution)/shard_map/ppermute | solution.py:404
  21.7 39.4 %collective-permute-start.5 = (bf16[1664,512]{1,0:T(8,128)(2,1)S(1)}, bf16[1664,512]{1,0:T(8,128)(2,1)S(1)}, u32[]{:S(2)}, u32[]{:S(2)}) collective-permute-start(bf16[1664,512]{1,0:T(8,128)(2,1)S(1)} %shard_map.58.sent), channel_id=1, source_target_pairs={{0,1},{1,0},{2,3},{3,2},{4,5},{5,4},{6,7},{7,6},{8,9},{9,8},{10,11... | collective-permute-start | bytes 5111816 | tf_op jit(solution)/shard_map/ppermute | solution.py:423
  28.4 0.7 collective-permute-start.3
  29.2 0.9 %collective-permute-start.4 = (f32[4,32,512]{2,1,0:T(8,128)S(1)}, f32[4,32,512]{2,1,0:T(8,128)S(1)}, u32[]{:S(2)}, u32[]{:S(2)}) collective-permute-start(f32[4,32,512]{2,1,0:T(8,128)S(1)} %get-tuple-element.51), channel_id=1, source_target_pairs={{1,5},{3,7},{5,1},{7,3},{9,13},{11,15},{13,9},{15,11},{17,21},{19,... | collective-permute-start | bytes 786440 | tf_op jit(solution)/shard_map/ppermute | solution.py:387
  30.1 0.7 collective-permute-start.6
  62.5 2.0 %collective-permute-start.8 = (f32[8,32,512]{2,1,0:T(8,128)S(1)}, f32[8,32,512]{2,1,0:T(8,128)S(1)}, u32[]{:S(2)}, u32[]{:S(2)}) collective-permute-start(f32[8,32,512]{2,1,0:T(8,128)S(1)} %get-tuple-element.66), channel_id=1, source_target_pairs={{0,2},{2,0},{4,6},{6,4},{8,10},{10,8},{12,14},{14,12},{16,18},{18,... | collective-permute-start | bytes 1572872 | tf_op jit(solution)/shard_map/ppermute | solution.py:387
  64.5 5.6 %collective-permute-start.9 = (bf16[4,32,512]{2,1,0:T(8,128)(2,1)S(1)}, bf16[4,32,512]{2,1,0:T(8,128)(2,1)S(1)}, u32[]{:S(2)}, u32[]{:S(2)}) collective-permute-start(bf16[4,32,512]{2,1,0:T(8,128)(2,1)S(1)} %get-tuple-element.68), channel_id=1, source_target_pairs={{0,4},{2,6},{4,0},{6,2},{8,12},{10,14},{12,8},{14,10},{16,20},{18,... | collective-permute-start | bytes 393224 | tf_op jit(solution)/shard_map/ppermute | solution.py:387
  70.1 5.4 %collective-permute-start.10 = (f32[2,32,512]{2,1,0:T(8,128)S(1)}, f32[2,32,512]{2,1,0:T(8,128)S(1)}, u32[]{:S(2)}, u32[]{:S(2)}) collective-permute-start(f32[2,32,512]{2,1,0:T(8,128)S(1)} %get-tuple-element.70), channel_id=1, source_target_pairs={{0,8},{2,10},{4,12},{6,14},{8,0},{10,2},{12,4},{14,6},{16,24},{18,... | collective-permute-start | bytes 393224 | tf_op jit(solution)/shard_map/ppermute | solution.py:387
  75.5 5.3 %collective-permute-start.11 = (f32[1,32,512]{2,1,0:T(8,128)S(1)}, f32[1,32,512]{2,1,0:T(8,128)S(1)}, u32[]{:S(2)}, u32[]{:S(2)}) collective-permute-start(f32[1,32,512]{2,1,0:T(8,128)S(1)} %get-tuple-element.72), channel_id=1, source_target_pairs={{0,16},{2,18},{4,20},{6,22},{8,24},{10,26},{12,28},{14,30},{16,0},... | collective-permute-start | bytes 196616 | tf_op jit(solution)/shard_map/ppermute | solution.py:387
  78.6 3.6 %collective-permute-start.7 = (f32[1,32,512]{2,1,0:T(8,128)S(1)}, f32[1,32,512]{2,1,0:T(8,128)S(1)}, u32[]{:S(2)}, u32[]{:S(2)}) collective-permute-start(f32[1,32,512]{2,1,0:T(8,128)S(1)} %get-tuple-element.61), channel_id=1, source_target_pairs={{1,17},{3,19},{5,21},{7,23},{9,25},{11,27},{13,29},{15,31},{17,1},... | collective-permute-start | bytes 196616 | tf_op jit(solution)/shard_map/ppermute | solution.py:387
  80.9 4.3 %collective-permute-start.12 = (f32[1,32,512]{2,1,0:T(8,128)S(1)}, f32[1,32,512]{2,1,0:T(8,128)S(1)}, u32[]{:S(2)}, u32[]{:S(2)}) collective-permute-start(f32[1,32,512]{2,1,0:T(8,128)S(1)} %add.10), channel_id=1, source_target_pairs={{0,1},{1,0},{2,3},{3,2},{4,5},{5,4},{6,7},{7,6},{8,9},{9,8},{10,11... | collective-permute-start | bytes 196616 | tf_op jit(solution)/shard_map/ppermute | solution.py:447

commit v11 on v9

--- a/solution.py
+++ b/solution.py
@@ -133,7 +133,7 @@
 
 def gather_kernel(send_rows, tmat, blocks, first_rows, second_rows, panel, near_blocks, picked, sem):
     count = picked.shape[0]
-    depth = 2 * count
+    depth = 4 * count
     steps = panel.shape[0] // depth
     copy_blocks = pltpu.make_async_copy(blocks, near_blocks, sem.at[steps])
 
@@ -173,7 +173,7 @@
         out_specs=[NEAR] * 4,
         scratch_shapes=[
             pltpu.VMEM((picked, width), jnp.float32),
-            pltpu.SemaphoreType.DMA((tmat.shape[0] // (2 * picked) + 1,)),
+            pltpu.SemaphoreType.DMA((tmat.shape[0] // (4 * picked) + 1,)),
         ],
         compiler_params=room_for(nbytes(tmat), nbytes(blocks), 6 * picked * width),
         cost_estimate=near_nothing(),

time: 84.7 us -> 85.3 us (level)
  no operation moved by 1% of the time
where the time goes in v11:
time: 85.3 us; the launch traced here: 84.4 us
  waiting for transfers between devices  50.1 us (59%)
  starting transfers between devices  16.1 us (19%)
  Pallas kernels  14.8 us (17%)
  local copies, waits for them, and re-layouts  1.87 us (2%)
  between operations  0.87 us (1%)
    ppermute x1, waiting for transfers between devices, body(): got = lax.ppermute(sent, 'col', [(0, 1), (1, 0)])  29.3 us
    ppermute x8, waiting for transfers between devices, step(): return [keep, lax.ppermute(send, *route(bit))]  11.4 us
    ppermute x8, starting transfers between devices, step(): return [keep, lax.ppermute(send, *route(bit))]  8.48 us
    ppermute x1, waiting for transfers between devices, body(): ahead = lax.ppermute(tmat[:early], 'col', [(0, 1), (1, 0)])  6.55 us
    pallas_call x1, Pallas kernels, panel_work(): pl.pallas_call(functools.partial(panel_kernel, panel.shape[0] // bsize, n...  4.8 us
    pallas_call x1, Pallas kernels, gather_rows(): pl.pallas_call(gather_kernel, out_shape=[jax.ShapeDtypeStruct((picked //...  4.68 us
    ppermute x1, starting transfers between devices, body(): ahead = lax.ppermute(tmat[:early], 'col', [(0, 1), (1, 0)])  3 us
    ppermute x1, waiting for transfers between devices, body(): other = x + lax.ppermute(x, 'col', [(0, 1), (1, 0)])  2.84 us
  transfers between devices with their start and end apart: 13, of which 7 were waited for; matrix products, arithmetic and copies ran while one was open for 0% of the time, Pallas kernels for 16%

profile of v11, /device:TPU:0, one launch (start us, length us, event | category | flops | bytes accessed | tf_op | source)
XLA Modules:
  0.0 84.4 jit_solution(2423298960417332400)
XLA Ops:
  0.0 1.2 %slice.3 = bf16[768,512]{1,0:T(8,128)(2,1)S(1)} slice(bf16[4096,512]{1,0:T(8,128)(2,1)} %tmat.3), slice={[0:768], [0:512]} | slice | bytes 1572864 | tf_op jit(solution)/shard_map/slice | solution.py:418
  1.2 3.0 %collective-permute-start.2 = (bf16[768,512]{1,0:T(8,128)(2,1)S(1)}, bf16[768,512]{1,0:T(8,128)(2,1)S(1)}, u32[]{:S(2)}, u32[]{:S(2)}) collective-permute-start(bf16[768,512]{1,0:T(8,128)(2,1)S(1)} %slice.3), channel_id=1, source_target_pairs={{0,1},{1,0},{2,3},{3,2},{4,5},{5,4},{6,7},{7,6},{8,9},{9,8},{10,11... | collective-permute-start | bytes 2359304 | tf_op jit(solution)/shard_map/ppermute | solution.py:418
  4.2 0.7 copy-done.1
  4.9 4.7 %shard_map.56 = (bf16[256,512]{1,0:T(8,128)(2,1)S(1)}, bf16[256,512]{1,0:T(8,128)(2,1)S(1)}, bf16[4096,512]{1,0:T(8,128)(2,1)S(1)}, bf16[256,128,128]{2,1,0:T(8,128)(2,1)S(1)}) custom-call(s32[2,256]{1,0:T(2,128)S(1)} %copy-done.1, bf16[4096,512]{1,0:T(8,128)(2,1)} %tmat.3, bf16[256,128,128]{2,1,0:T(8,128)(2,1)} %blocks.1), custom_call_target="tpu_custom_call" | custom-call | flops 1 | bytes 1 | tf_op jit(solution)/shard_map/pallas_call | solution.py:168
  9.6 0.7 collective-permute-start
  10.3 0.7 collective-permute-start.1
  11.6 0.7 shard_map.55
  12.3 0.8 shard_map.57.own
  13.1 2.1 %shard_map.58.sent = bf16[1664,512]{1,0:T(8,128)(2,1)S(1)} custom-call(s32[1,128]{1,0:T(1,128)S(1)} %get-tuple-element.39.first, s32[1,128]{1,0:T(1,128)S(1)} %get-tuple-element.40.owner_row, s32[1,512]{1,0:T(1,128)S(1)} %get-tuple-element.41.entries, bf16[256,128,128]{2,1,0:T(8,128)(2,1)S(1)} %get-tuple-element.42.blocks, ...), custom_call_target="tpu_custom_call" | custom-call | flops 1 | bytes 1 | tf_op jit(solution)/shard_map/pallas_call | solution.py:229
  15.2 6.6 %collective-permute-done.2.ahead = bf16[768,512]{1,0:T(8,128)(2,1)S(1)} collective-permute-done((bf16[768,512]{1,0:T(8,128)(2,1)S(1)}, bf16[768,512]{1,0:T(8,128)(2,1)S(1)}, u32[]{:S(2)}, u32[]{:S(2)}) %collective-permute-start.2) | collective-permute-done | bytes 786464 | tf_op jit(solution)/shard_map/ppermute | solution.py:418
  21.7 1.7 %collective-permute-start.5 = (bf16[1664,512]{1,0:T(8,128)(2,1)S(1)}, bf16[1664,512]{1,0:T(8,128)(2,1)S(1)}, u32[]{:S(2)}, u32[]{:S(2)}) collective-permute-start(bf16[1664,512]{1,0:T(8,128)(2,1)S(1)} %shard_map.58.sent), channel_id=1, source_target_pairs={{0,1},{1,0},{2,3},{3,2},{4,5},{5,4},{6,7},{7,6},{8,9},{9,8},{10,11... | collective-permute-start | bytes 5111816 | tf_op jit(solution)/shard_map/ppermute | solution.py:423
  23.5 4.8 %shard_map.59 = (bf16[2432,512]{1,0:T(8,128)(2,1)S(1)}, f32[512,512]{1,0:T(8,128)S(1)}) custom-call(s32[1,128]{1,0:T(1,128)S(1)} %get-tuple-element.39.first, s32[1,128]{1,0:T(1,128)S(1)} %get-tuple-element.40.owner_row, s32[1,512]{1,0:T(1,128)S(1)} %get-tuple-element.41.entries, bf16[256,128,128]{2,1,0:T(8,128)(2,1)S(1)} %get-tuple-element.42.blocks, ...), custom_call_target="tpu_custom_call" | custom-call | flops 1 | bytes 1 | tf_op jit(solution)/shard_map/pallas_call | solution.py:275
  28.3 0.1 shard_map.60
  28.4 0.7 collective-permute-start.3
  29.1 0.1 shard_map.61
  29.2 0.7 collective-permute-start.4
  29.9 0.2 shard_map.62
  30.1 0.7 collective-permute-start.6
  30.8 29.3 %collective-permute-done.5.got = bf16[1664,512]{1,0:T(8,128)(2,1)S(1)} collective-permute-done((bf16[1664,512]{1,0:T(8,128)(2,1)S(1)}, bf16[1664,512]{1,0:T(8,128)(2,1)S(1)}, u32[]{:S(2)}, u32[]{:S(2)}) %collective-permute-start.5) | collective-permute-done | bytes 1703968 | tf_op jit(solution)/shard_map/ppermute | solution.py:423
  60.1 1.2 %shard_map.65 = f32[512,512]{1,0:T(8,128)S(1)} custom-call(bf16[1664,512]{1,0:T(8,128)(2,1)S(1)} %collective-permute-done.5.got, bf16[1664,512]{1,0:T(8,128)(2,1)S(1)} %get-tuple-element.63.partner, f32[512,512]{1,0:T(8,128)S(1)} %get-tuple-element.64.known), custom_call_target="tpu_custom_call" | custom-call | flops 1 | bytes 1 | tf_op jit(solution)/shard_map/pallas_call | solution.py:335
  61.4 0.1 shard_map.66
  61.5 1.9 %collective-permute-done.8.refs_1_ = f32[8,32,512]{2,1,0:T(8,128)S(1)} collective-permute-done((f32[8,32,512]{2,1,0:T(8,128)S(1)}, f32[8,32,512]{2,1,0:T(8,128)S(1)}, u32[]{:S(2)}, u32[]{:S(2)}) %collective-permute-start.8) | collective-permute-done | bytes 524320 | tf_op jit(solution)/shard_map/ppermute | solution.py:387
  63.5 1.5 %collective-permute-start.9 = (bf16[4,32,512]{2,1,0:T(8,128)(2,1)S(1)}, bf16[4,32,512]{2,1,0:T(8,128)(2,1)S(1)}, u32[]{:S(2)}, u32[]{:S(2)}) collective-permute-start(bf16[4,32,512]{2,1,0:T(8,128)(2,1)S(1)} %get-tuple-element.68), channel_id=1, source_target_pairs={{0,4},{2,6},{4,0},{6,2},{8,12},{10,14},{12,8},{14,10},{16,20},{18,... | collective-permute-start | bytes 393224 | tf_op jit(solution)/shard_map/ppermute | solution.py:387
  65.0 4.1 %collective-permute-done.9.refs_1_ = bf16[4,32,512]{2,1,0:T(8,128)(2,1)S(1)} collective-permute-done((bf16[4,32,512]{2,1,0:T(8,128)(2,1)S(1)}, bf16[4,32,512]{2,1,0:T(8,128)(2,1)S(1)}, u32[]{:S(2)}, u32[]{:S(2)}) %collective-permute-start.9) | collective-permute-done | bytes 131104 | tf_op jit(solution)/shard_map/ppermute | solution.py:387
  69.1 1.6 %collective-permute-start.10 = (f32[2,32,512]{2,1,0:T(8,128)S(1)}, f32[2,32,512]{2,1,0:T(8,128)S(1)}, u32[]{:S(2)}, u32[]{:S(2)}) collective-permute-start(f32[2,32,512]{2,1,0:T(8,128)S(1)} %get-tuple-element.70), channel_id=1, source_target_pairs={{0,8},{2,10},{4,12},{6,14},{8,0},{10,2},{12,4},{14,6},{16,24},{18,... | collective-permute-start | bytes 393224 | tf_op jit(solution)/shard_map/ppermute | solution.py:387
  70.7 3.4 %collective-permute-done.10.refs_1_ = f32[2,32,512]{2,1,0:T(8,128)S(1)} collective-permute-done((f32[2,32,512]{2,1,0:T(8,128)S(1)}, f32[2,32,512]{2,1,0:T(8,128)S(1)}, u32[]{:S(2)}, u32[]{:S(2)}) %collective-permute-start.10) | collective-permute-done | bytes 131104 | tf_op jit(solution)/shard_map/ppermute | solution.py:387
  74.2 2.6 %collective-permute-start.11 = (f32[1,32,512]{2,1,0:T(8,128)S(1)}, f32[1,32,512]{2,1,0:T(8,128)S(1)}, u32[]{:S(2)}, u32[]{:S(2)}) collective-permute-start(f32[1,32,512]{2,1,0:T(8,128)S(1)} %get-tuple-element.72), channel_id=1, source_target_pairs={{0,16},{2,18},{4,20},{6,22},{8,24},{10,26},{12,28},{14,30},{16,0},... | collective-permute-start | bytes 196616 | tf_op jit(solution)/shard_map/ppermute | solution.py:387
  76.8 0.7 collective-permute-start.7
  77.5 1.9 %collective-permute-done.11 = f32[1,32,512]{2,1,0:T(8,128)S(1)} collective-permute-done((f32[1,32,512]{2,1,0:T(8,128)S(1)}, f32[1,32,512]{2,1,0:T(8,128)S(1)}, u32[]{:S(2)}, u32[]{:S(2)}) %collective-permute-start.11) | collective-permute-done | bytes 65568 | tf_op jit(solution)/shard_map/ppermute | solution.py:387
  79.4 1.5 %collective-permute-start.12 = (f32[1,32,512]{2,1,0:T(8,128)S(1)}, f32[1,32,512]{2,1,0:T(8,128)S(1)}, u32[]{:S(2)}, u32[]{:S(2)}) collective-permute-start(f32[1,32,512]{2,1,0:T(8,128)S(1)} %add.10), channel_id=1, source_target_pairs={{0,1},{1,0},{2,3},{3,2},{4,5},{5,4},{6,7},{7,6},{8,9},{9,8},{10,11... | collective-permute-start | bytes 196616 | tf_op jit(solution)/shard_map/ppermute | solution.py:447
  80.9 2.8 %collective-permute-done.12 = f32[1,32,512]{2,1,0:T(8,128)S(1)} collective-permute-done((f32[1,32,512]{2,1,0:T(8,128)S(1)}, f32[1,32,512]{2,1,0:T(8,128)S(1)}, u32[]{:S(2)}, u32[]{:S(2)}) %collective-permute-start.12) | collective-permute-done | bytes 65568 | tf_op jit(solution)/shard_map/ppermute | solution.py:447
  83.7 0.6 select_bitcast_fusion
  (16 shorter events, 0.3 us)
Async XLA Ops:
  1.2 10.4 %copy-start = (s32[256,2]{0,1:T(2,128)S(1)}, s32[256,2]{0,1:T(2,128)}, u32[]{:S(2)}) copy-start(s32[256,2]{0,1:T(2,128)} %param.7) | copy-start | bytes 6148
  1.2 20.5 %collective-permute-start.2 = (bf16[768,512]{1,0:T(8,128)(2,1)S(1)}, bf16[768,512]{1,0:T(8,128)(2,1)S(1)}, u32[]{:S(2)}, u32[]{:S(2)}) collective-permute-start(bf16[768,512]{1,0:T(8,128)(2,1)S(1)} %slice.3), channel_id=1, source_target_pairs={{0,1},{1,0},{2,3},{3,2},{4,5},{5,4},{6,7},{7,6},{8,9},{9,8},{10,11... | collective-permute-start | bytes 2359304 | tf_op jit(solution)/shard_map/ppermute | solution.py:418
  4.2 0.7 copy-start.1
  9.6 3.5 %collective-permute-start = (bf16[256,512]{1,0:T(8,128)(2,1)S(1)}, bf16[256,512]{1,0:T(8,128)(2,1)S(1)}, u32[]{:S(2)}, u32[]{:S(2)}) collective-permute-start(bf16[256,512]{1,0:T(8,128)(2,1)S(1)} %get-tuple-element.44), channel_id=1, source_target_pairs={{3,5},{7,9},{11,13},{15,17},{19,21},{23,25},{27,29},{5,3},{9,7},{1... | collective-permute-start | bytes 786440 | tf_op jit(solution)/shard_map/ppermute | solution.py:404
  10.3 2.9 %collective-permute-start.1 = (bf16[256,512]{1,0:T(8,128)(2,1)S(1)}, bf16[256,512]{1,0:T(8,128)(2,1)S(1)}, u32[]{:S(2)}, u32[]{:S(2)}) collective-permute-start(bf16[256,512]{1,0:T(8,128)(2,1)S(1)} %get-tuple-element.45), channel_id=1, source_target_pairs={{1,3},{5,7},{9,11},{13,15},{17,19},{21,23},{25,27},{29,31},{3,1},{... | collective-permute-start | bytes 786440 | tf_op jit(solution)/shard_map/ppermute | solution.py:404
  21.7 38.4 %collective-permute-start.5 = (bf16[1664,512]{1,0:T(8,128)(2,1)S(1)}, bf16[1664,512]{1,0:T(8,128)(2,1)S(1)}, u32[]{:S(2)}, u32[]{:S(2)}) collective-permute-start(bf16[1664,512]{1,0:T(8,128)(2,1)S(1)} %shard_map.58.sent), channel_id=1, source_target_pairs={{0,1},{1,0},{2,3},{3,2},{4,5},{5,4},{6,7},{7,6},{8,9},{9,8},{10,11... | collective-permute-start | bytes 5111816 | tf_op jit(solution)/shard_map/ppermute | solution.py:423
  28.4 0.7 collective-permute-start.3
  29.2 0.9 %collective-permute-start.4 = (f32[4,32,512]{2,1,0:T(8,128)S(1)}, f32[4,32,512]{2,1,0:T(8,128)S(1)}, u32[]{:S(2)}, u32[]{:S(2)}) collective-permute-start(f32[4,32,512]{2,1,0:T(8,128)S(1)} %get-tuple-element.51), channel_id=1, source_target_pairs={{1,5},{3,7},{5,1},{7,3},{9,13},{11,15},{13,9},{15,11},{17,21},{19,... | collective-permute-start | bytes 786440 | tf_op jit(solution)/shard_map/ppermute | solution.py:387
  30.1 0.7 collective-permute-start.6
  61.4 2.0 %collective-permute-start.8 = (f32[8,32,512]{2,1,0:T(8,128)S(1)}, f32[8,32,512]{2,1,0:T(8,128)S(1)}, u32[]{:S(2)}, u32[]{:S(2)}) collective-permute-start(f32[8,32,512]{2,1,0:T(8,128)S(1)} %get-tuple-element.66), channel_id=1, source_target_pairs={{0,2},{2,0},{4,6},{6,4},{8,10},{10,8},{12,14},{14,12},{16,18},{18,... | collective-permute-start | bytes 1572872 | tf_op jit(solution)/shard_map/ppermute | solution.py:387
  63.5 5.6 %collective-permute-start.9 = (bf16[4,32,512]{2,1,0:T(8,128)(2,1)S(1)}, bf16[4,32,512]{2,1,0:T(8,128)(2,1)S(1)}, u32[]{:S(2)}, u32[]{:S(2)}) collective-permute-start(bf16[4,32,512]{2,1,0:T(8,128)(2,1)S(1)} %get-tuple-element.68), channel_id=1, source_target_pairs={{0,4},{2,6},{4,0},{6,2},{8,12},{10,14},{12,8},{14,10},{16,20},{18,... | collective-permute-start | bytes 393224 | tf_op jit(solution)/shard_map/ppermute | solution.py:387
  69.1 5.0 %collective-permute-start.10 = (f32[2,32,512]{2,1,0:T(8,128)S(1)}, f32[2,32,512]{2,1,0:T(8,128)S(1)}, u32[]{:S(2)}, u32[]{:S(2)}) collective-permute-start(f32[2,32,512]{2,1,0:T(8,128)S(1)} %get-tuple-element.70), channel_id=1, source_target_pairs={{0,8},{2,10},{4,12},{6,14},{8,0},{10,2},{12,4},{14,6},{16,24},{18,... | collective-permute-start | bytes 393224 | tf_op jit(solution)/shard_map/ppermute | solution.py:387
  74.2 5.2 %collective-permute-start.11 = (f32[1,32,512]{2,1,0:T(8,128)S(1)}, f32[1,32,512]{2,1,0:T(8,128)S(1)}, u32[]{:S(2)}, u32[]{:S(2)}) collective-permute-start(f32[1,32,512]{2,1,0:T(8,128)S(1)} %get-tuple-element.72), channel_id=1, source_target_pairs={{0,16},{2,18},{4,20},{6,22},{8,24},{10,26},{12,28},{14,30},{16,0},... | collective-permute-start | bytes 196616 | tf_op jit(solution)/shard_map/ppermute | solution.py:387
  76.8 4.1 %collective-permute-start.7 = (f32[1,32,512]{2,1,0:T(8,128)S(1)}, f32[1,32,512]{2,1,0:T(8,128)S(1)}, u32[]{:S(2)}, u32[]{:S(2)}) collective-permute-start(f32[1,32,512]{2,1,0:T(8,128)S(1)} %get-tuple-element.61), channel_id=1, source_target_pairs={{1,17},{3,19},{5,21},{7,23},{9,25},{11,27},{13,29},{15,31},{17,1},... | collective-permute-start | bytes 196616 | tf_op jit(solution)/shard_map/ppermute | solution.py:387
  79.4 4.3 %collective-permute-start.12 = (f32[1,32,512]{2,1,0:T(8,128)S(1)}, f32[1,32,512]{2,1,0:T(8,128)S(1)}, u32[]{:S(2)}, u32[]{:S(2)}) collective-permute-start(f32[1,32,512]{2,1,0:T(8,128)S(1)} %add.10), channel_id=1, source_target_pairs={{0,1},{1,0},{2,3},{3,2},{4,5},{5,4},{6,7},{7,6},{8,9},{9,8},{10,11... | collective-permute-start | bytes 196616 | tf_op jit(solution)/shard_map/ppermute | solution.py:447
